TPU v7x, 32 devices: a whole 2x2x4 slice. The times are simulated.
32 devices in a mesh: lon: 8 (over z, x), lat: 4 (over y, core).
Axes of the slice: x: 2, y: 2, z: 4, core: 2. Of those that a mesh axis runs over, the one named last changes fastest.
Arguments:
- obs_values: bfloat16 [1024, 31, 256], P(('lon', 'lat')), may hold values from -6 to 6
- obs_offset: float32 [1024, 2, 256], P(('lon', 'lat')), may hold values from -0.5 to 0.5
- obs_cell: int32 [1024, 256], P(('lon', 'lat')), may hold values from 0 to 511
- obs_slot: int32 [1024, 256], P(('lon', 'lat')), may hold values from 0 to 11
- obs_count: int32 [32, 32], P(('lon', 'lat')), may hold values from 1 to 256, as said below
- embed_weight: bfloat16 [384, 256], replicated, may hold values from -0.3125 to 0.3125
- embed_bias: float32 [256], replicated, may hold values from -3 to 3
- stride_weight: bfloat16 [9, 256, 256], replicated, may hold values from -0.125 to 0.125
- stride_bias: float32 [256], replicated, may hold values from -3 to 3
- depth_weight: float32 [9, 256], replicated, may hold values from -2 to 2
- norm_gain: float32 [256], replicated, may hold values from 0.1 to 1.9
Outputs:
- encoded: bfloat16 [32, 128, 256], P('lat', 'lon')
Inputs may be any that keep to these rules, and one draw needn't show every extreme that they name: `obs_count`: every entry is at least 1; in every draw one destination tile receives exactly 256 live slots from every source shard.
All inputs are finite; a program needn't handle non-finite values.
Results may differ from a plain program's by a relative error of at most 0.011.
Values may be sent and summed in bfloat16 or wider, within the bound.
No kernel may reach another device: no remote copies, remote signals or barrier semaphores. Data moves between devices by JAX's collectives and lax.ppermute only.
A program may use at most 128 MiB of HBM per device.

v0:
```python
import jax
import jax.numpy as jnp
from jax import lax
from jax.sharding import PartitionSpec as P

D = 256
OBS_VARS = 31
SLOTS = 12
TLAT = 16
TLON = 32
CELLS = 512


def shifted(value, axis, by):
    size = lax.axis_size(axis)
    pairs = [(i, i + by) for i in range(size) if 0 <= i + by < size]
    return lax.ppermute(value, axis, pairs)


def shifted_2(value, axis, steps):
    count = lax.axis_size(axis)
    pairs = [(source, (source + steps) % count) for source in range(count)]
    return lax.ppermute(value, axis, pairs)


def with_halo(value, sides, width, wrap):
    for axis, dim in sides:
        size, length = (lax.axis_size(axis), value.shape[dim])
        up = [(i, (i + 1) % size) for i in range(size if wrap else size - 1)]
        down = [(j, i) for i, j in up]
        last = lax.slice_in_dim(value, length - width, length, axis=dim)
        leading = lax.slice_in_dim(value, 0, width, axis=dim)
        before = lax.ppermute(last, axis, up)
        after = lax.ppermute(leading, axis, down)
        value = jnp.concatenate([before, value, after], axis=dim)
    return value


def spread_block(total, values, codes):
    slot_of = codes // CELLS
    cell_of = codes - slot_of * CELLS
    cell_hot = (cell_of[None] == lax.broadcasted_iota(jnp.int32, (CELLS,) + codes.shape, 0)).astype(
        jnp.bfloat16
    )
    slot_hot = (slot_of[None] == lax.broadcasted_iota(jnp.int32, (SLOTS,) + codes.shape, 0)).astype(
        jnp.bfloat16
    )
    spread = slot_hot[:, None] * values[None]
    return total + jnp.einsum("cgr,skgr->csk", cell_hot, spread, preferred_element_type=jnp.float32)


def layer_norm(mixed, norm_gain):
    centre = mixed - jnp.mean(mixed, axis=-1, keepdims=True)
    spread = jnp.mean(centre * centre, axis=-1, keepdims=True)
    return centre * lax.rsqrt(spread + 1e-05) * norm_gain


def on_device(
    obs_values,
    obs_offset,
    obs_cell,
    obs_slot,
    obs_count,
    embed_weight,
    embed_bias,
    stride_weight,
    stride_bias,
    depth_weight,
    norm_gain,
):
    lon_count = lax.axis_size("lon")
    lat_count = lax.axis_size("lat")
    tiles = lon_count * lat_count
    capacity = obs_values.shape[2]
    width = OBS_VARS + 1
    position = lax.broadcasted_iota(jnp.int32, obs_cell.shape, 1)
    live = position < obs_count[0][:, None]
    radius = obs_offset[:, 0, :] * obs_offset[:, 0, :] + obs_offset[:, 1, :] * obs_offset[:, 1, :]
    weight = jnp.where(live, jnp.exp(-2.0 * radius), jnp.float32(0.0))
    scaled = obs_values.astype(jnp.float32) * weight[:, None, :]
    packed = jnp.concatenate([scaled, weight[:, None, :]], axis=1).astype(jnp.bfloat16)
    codes = jnp.where(live, obs_slot * CELLS + obs_cell, -1)
    arrived, arrived_codes = (
        lax.all_to_all(packed, ("lon", "lat"), split_axis=0, concat_axis=0, tiled=True),
        lax.all_to_all(codes, ("lon", "lat"), split_axis=0, concat_axis=0, tiled=True),
    )
    rows_step = min(2048, tiles * capacity)
    empty = jnp.zeros((CELLS, SLOTS, width), jnp.float32)
    group = rows_step // capacity

    def step_padded(index, total):
        block_values = lax.dynamic_slice_in_dim(arrived, index * group, group, 0)
        block_codes = lax.dynamic_slice_in_dim(arrived_codes, index * group, group, 0)
        return spread_block(total, jnp.moveaxis(block_values, 1, 0), block_codes)

    total = lax.fori_loop(0, tiles // group, step_padded, empty)
    density = total[:, :, width - 1 :]
    ratio = total[:, :, : width - 1] / (1.0 + density)
    gridded = (
        jnp.concatenate([ratio, density], axis=2).reshape(CELLS, SLOTS * width).astype(jnp.bfloat16)
    )
    projected = jnp.dot(gridded, embed_weight, preferred_element_type=jnp.float32) + embed_bias
    embedded = jax.nn.gelu(projected).astype(jnp.bfloat16).reshape(TLAT, TLON, D)
    upper = shifted(embedded[TLAT - 1 :], "lat", 1)
    taller = jnp.concatenate([upper, embedded], axis=0)
    before = shifted_2(taller[:, TLON - 1 :], "lon", 1)
    framed = jnp.concatenate([before, taller], axis=1)
    patches = jnp.concatenate(
        [
            framed[row_at : row_at + TLAT - 1 : 2, col_at : col_at + TLON - 1 : 2]
            for row_at in range(3)
            for col_at in range(3)
        ],
        axis=2,
    )
    strided = (
        jnp.dot(
            patches.reshape(-1, 9 * D),
            stride_weight.reshape(9 * D, D),
            preferred_element_type=jnp.float32,
        )
        + stride_bias
    )
    coarse = jax.nn.gelu(strided).astype(jnp.bfloat16).reshape(TLAT // 2, TLON // 2, D)
    wide = with_halo(coarse, (("lon", 1),), 1, True)
    full = with_halo(wide, (("lat", 0),), 1, False)
    depth = jnp.zeros((TLAT // 2, TLON // 2, D), jnp.float32)
    for row_at in range(3):
        for col_at in range(3):
            depth = (
                depth
                + full[row_at : row_at + TLAT // 2, col_at : col_at + TLON // 2].astype(jnp.float32)
                * depth_weight[3 * row_at + col_at]
            )
    mixed = coarse.astype(jnp.float32) + depth
    return layer_norm(mixed, norm_gain).astype(jnp.bfloat16)


def solution(mesh):
    placed = (
        P(("lon", "lat"), None, None),
        P(("lon", "lat"), None, None),
        P(("lon", "lat"), None),
        P(("lon", "lat"), None),
        P(("lon", "lat"), None),
        P(),
        P(),
        P(),
        P(),
        P(),
        P(),
    )
    return jax.shard_map(
        on_device, mesh=mesh, in_specs=placed, out_specs=P("lat", "lon", None), check_vma=False
    )
```

profile of v0, /device:TPU:1, one launch (start us, length us, event | category | flops | bytes accessed | tf_op | source)
XLA Modules:
  0.0 69.2 jit_solution(18073862279880010354)
XLA Ops:
  0.0 0.0 copy-start
  0.0 0.9 %add_select_fusion.1 = s32[32,256]{1,0:T(8,128)S(1)} fusion(s32[32,256]{1,0:T(8,128)} %param.15, s32[32,256]{1,0:T(8,128)} %param.16, s32[32]{0:T(128)} %bitcast.77), kind=kLoop, calls=%fused_computation.65 | loop fusion | flops 32768 | bytes 98432 | tf_op jit(solution)/shard_map/jit(_where)/select_n | solution.py:82
  0.9 0.6 all_to_all.11
  1.6 7.1 %all-to-all-start = ((s32[32,1,256]{2,1,0:T(1,128)}), s32[32,1,256]{2,1,0:T(1,128)S(1)}, u32[]{:S(2)}, u32[]{:S(2)}) async-start(s32[32,1,256]{2,1,0:T(1,128)} %all_to_all.11), calls=%async_computation | async-start | bytes 65536 | tf_op jit(solution)/shard_map/all_to_all | solution.py:85
  8.7 1.0 %fusion.43 = (bf16[32,1,256]{2,1,0:T(2,128)(2,1)S(1)}, f32[32,1,256]{2,1,0:T(1,128)S(1)}) fusion(f32[32,2,256]{2,1,0:T(2,128)} %param.14, s32[32]{0:T(128)} %bitcast.78), kind=kLoop, calls=%fused_computation.86 | loop fusion | flops 57344 | bytes 114816 | tf_op jit(solution)/shard_map/convert.3
  9.7 1.4 %multiply_convert_fusion = bf16[32,31,256]{2,1,0:T(8,128)(2,1)S(1)} fusion(bf16[32,31,256]{2,0,1:T(8,128)(2,1)} %param.13, f32[32,256]{1,0:T(8,128)S(1)} %bitcast.67), kind=kLoop, calls=%fused_computation.22 | loop fusion | flops 761856 | bytes 1048576 | tf_op jit(solution)/shard_map/convert.2
  11.1 0.9 %pad_maximum_fusion = bf16[32,32,256]{2,1,0:T(8,128)(2,1)} fusion(bf16[32,1,256]{2,1,0:T(2,128)(2,1)S(1)} %get-tuple-element.142, bf16[32,31,256]{2,1,0:T(8,128)(2,1)S(1)} %multiply_convert_fusion), kind=kLoop, calls=%fused_computation.33 | loop fusion | flops 1048576 | bytes 1048576 | tf_op jit(solution)/shard_map/concatenate | solution.py:81
  12.0 3.8 %all-to-all-done = s32[32,1,256]{2,1,0:T(1,128)S(1)} async-done(((s32[32,1,256]{2,1,0:T(1,128)}), s32[32,1,256]{2,1,0:T(1,128)S(1)}, u32[]{:S(2)}, u32[]{:S(2)}) %all-to-all-start) | async-done | bytes 32800 | tf_op jit(solution)/shard_map/all_to_all | solution.py:85
  15.8 2.6 %all-to-all-start.1 = ((bf16[32,32,256]{2,1,0:T(8,128)(2,1)}), bf16[32,32,256]{2,1,0:T(8,128)(2,1)S(1)}, u32[]{:S(2)}, u32[]{:S(2)}) async-start(bf16[32,32,256]{2,1,0:T(8,128)(2,1)} %pad_maximum_fusion), calls=%async_computation.1 | async-start | bytes 1048576 | tf_op jit(solution)/shard_map/all_to_all | solution.py:84
  18.4 15.3 %all-to-all-done.1 = bf16[32,32,256]{2,1,0:T(8,128)(2,1)S(1)} async-done(((bf16[32,32,256]{2,1,0:T(8,128)(2,1)}), bf16[32,32,256]{2,1,0:T(8,128)(2,1)S(1)}, u32[]{:S(2)}, u32[]{:S(2)}) %all-to-all-start.1) | async-done | bytes 524320 | tf_op jit(solution)/shard_map/all_to_all | solution.py:84
  33.7 5.2 %while.16 = (s32[]{:T(128)}, f32[512,12,32]{0,2,1:T(8,128)S(1)}, s32[32,256]{1,0:T(8,128)S(1)}, bf16[32,32,256]{2,1,0:T(8,128)(2,1)S(1)}, s32[]{:T(128)}, /*index=5*/s32[]{:T(128)}, s32[]{:T(128)}, s32[]{:T(128)}) while((s32[]{:T(128)}, f32[512,12,32]{0,2,1:T(8,128)S(1)}, s32[32,256]{1,0:T(8,128)S(1)}, ...), condition=%wide.region_1.2_spmd.clone, body=%wide.region_0.1_spmd.clone.sunk | while | flops 809977856 | bytes 2105493 | solution.py:96
  33.8 1.2 %fusion.57 = f32[512,12,32]{0,2,1:T(8,128)S(1)} fusion(s32[8,256]{1,0:T(8,128)S(1)} %get-tuple-element.188, f32[512,12,32]{0,2,1:T(8,128)S(1)} %get-tuple-element.199, bf16[32,8,256]{2,0,1:T(8,128)(2,1)S(1)} %dynamic-slice_bitcast_fusion.2, bf16[12,8,256]{2,1,0:T(8,128)(2,1)S(1)} %fusion.56, pred[]{:T(512)S(6)} %compare.13), kind=kOutput, calls=%fused_computation.6.clone.1 | convolution fusion | flops 809893888 | bytes 1761281 | tf_op jit(solution)/shard_map/while/body/eval_jaxpr/cgr,skgr->csk/dot_general | solution.py:49
  35.1 1.2 %fusion.57 = f32[512,12,32]{0,2,1:T(8,128)S(1)} fusion(s32[8,256]{1,0:T(8,128)S(1)} %get-tuple-element.188, f32[512,12,32]{0,2,1:T(8,128)S(1)} %get-tuple-element.199, bf16[32,8,256]{2,0,1:T(8,128)(2,1)S(1)} %dynamic-slice_bitcast_fusion.2, bf16[12,8,256]{2,1,0:T(8,128)(2,1)S(1)} %fusion.56, pred[]{:T(512)S(6)} %compare.13), kind=kOutput, calls=%fused_computation.6.clone.1 | convolution fusion | flops 809893888 | bytes 1761281 | tf_op jit(solution)/shard_map/while/body/eval_jaxpr/cgr,skgr->csk/dot_general | solution.py:49
  36.4 1.2 %fusion.57 = f32[512,12,32]{0,2,1:T(8,128)S(1)} fusion(s32[8,256]{1,0:T(8,128)S(1)} %get-tuple-element.188, f32[512,12,32]{0,2,1:T(8,128)S(1)} %get-tuple-element.199, bf16[32,8,256]{2,0,1:T(8,128)(2,1)S(1)} %dynamic-slice_bitcast_fusion.2, bf16[12,8,256]{2,1,0:T(8,128)(2,1)S(1)} %fusion.56, pred[]{:T(512)S(6)} %compare.13), kind=kOutput, calls=%fused_computation.6.clone.1 | convolution fusion | flops 809893888 | bytes 1761281 | tf_op jit(solution)/shard_map/while/body/eval_jaxpr/cgr,skgr->csk/dot_general | solution.py:49
  37.7 1.2 %fusion.57 = f32[512,12,32]{0,2,1:T(8,128)S(1)} fusion(s32[8,256]{1,0:T(8,128)S(1)} %get-tuple-element.188, f32[512,12,32]{0,2,1:T(8,128)S(1)} %get-tuple-element.199, bf16[32,8,256]{2,0,1:T(8,128)(2,1)S(1)} %dynamic-slice_bitcast_fusion.2, bf16[12,8,256]{2,1,0:T(8,128)(2,1)S(1)} %fusion.56, pred[]{:T(512)S(6)} %compare.13), kind=kOutput, calls=%fused_computation.6.clone.1 | convolution fusion | flops 809893888 | bytes 1761281 | tf_op jit(solution)/shard_map/while/body/eval_jaxpr/cgr,skgr->csk/dot_general | solution.py:49
  39.0 0.0 copy-start.4
  39.0 0.0 copy-start.5
  39.1 0.1 divide_convert_fusion
  39.2 0.1 pad_maximum_fusion.1
  39.2 0.7 copy-done.4
  39.9 0.0 copy-done.5
  39.9 0.4 fusion.27
  40.3 3.1 %collective-permute-start = (bf16[1,32,256]{2,1,0:T(8,128)(2,1)S(1)}, bf16[1,32,256]{2,1,0:T(8,128)(2,1)S(1)}, u32[]{:S(2)}, u32[]{:S(2)}) collective-permute-start(bf16[1,32,256]{2,1,0:T(8,128)(2,1)S(1)} %slice_bitcast_fusion), channel_id=1, source_target_pairs={{0,1},{1,2},{2,3},{4,5},{5,6},{6,7},{8,9},{9,10},{10,11},{12,13},{... | collective-permute-start | bytes 49160 | tf_op jit(solution)/shard_map/ppermute | solution.py:17
  43.4 0.2 slice.132
  43.6 0.2 slice.133
  43.8 0.4 slice.135
  44.2 0.4 slice.136
  44.6 0.0 collective-permute-done
  44.6 1.2 %collective-permute-start.1 = (bf16[17,1,256]{2,1,0:T(2,128)(2,1)S(1)}, bf16[17,1,256]{2,1,0:T(2,128)(2,1)S(1)}, u32[]{:S(2)}, u32[]{:S(2)}) collective-permute-start(bf16[17,1,256]{2,1,0:T(2,128)(2,1)S(1)} %fusion.41), channel_id=1, source_target_pairs={{0,4},{4,8},{8,12},{12,16},{16,20},{20,24},{24,28},{28,0},{1,5},{5... | collective-permute-start | bytes 26120 | tf_op jit(solution)/shard_map/ppermute | solution.py:23
  45.9 0.2 slice.129
  46.1 0.0 copy-start.2
  46.2 0.2 slice.130
  46.4 3.7 %collective-permute-done.1 = bf16[17,1,256]{2,1,0:T(2,128)(2,1)S(1)} collective-permute-done((bf16[17,1,256]{2,1,0:T(2,128)(2,1)S(1)}, bf16[17,1,256]{2,1,0:T(2,128)(2,1)S(1)}, u32[]{:S(2)}, u32[]{:S(2)}) %collective-permute-start.1) | collective-permute-done | bytes 8736 | tf_op jit(solution)/shard_map/ppermute | solution.py:23
  50.1 0.1 maximum_maximum_fusion
  50.2 0.2 slice.128
  50.4 0.2 slice.131
  50.7 0.3 slice.134
  51.1 0.0 copy-start.1
  51.2 0.0 copy-done
  51.2 0.0 copy-done.2
  51.2 0.0 copy-start.3
  51.2 0.4 fusion.40
  51.6 0.1 collective-permute-start.2
  51.7 4.1 %collective-permute-start.3 = (bf16[8,1,256]{2,1,0:T(2,128)(2,1)S(1)}, bf16[8,1,256]{2,1,0:T(2,128)(2,1)S(1)}, u32[]{:S(2)}, u32[]{:S(2)}) collective-permute-start(bf16[8,1,256]{2,1,0:T(2,128)(2,1)S(1)} %get-tuple-element.151), channel_id=1, source_target_pairs={{4,0},{8,4},{12,8},{16,12},{20,16},{24,20},{28,24},{0,28},{5,1},{9... | collective-permute-start | bytes 12296 | tf_op jit(solution)/shard_map/ppermute | solution.py:34
  55.8 1.0 %collective-permute-done.2 = bf16[8,1,256]{2,1,0:T(2,128)(2,1)S(1)} collective-permute-done((bf16[8,1,256]{2,1,0:T(2,128)(2,1)S(1)}, bf16[8,1,256]{2,1,0:T(2,128)(2,1)S(1)}, u32[]{:S(2)}, u32[]{:S(2)}) %collective-permute-start.2) | collective-permute-done | bytes 4128 | tf_op jit(solution)/shard_map/ppermute | solution.py:33
  56.8 0.0 collective-permute-done.3
  56.9 6.0 %collective-permute-start.4 = (bf16[1,18,256]{2,1,0:T(8,128)(2,1)S(1)}, bf16[1,18,256]{2,1,0:T(8,128)(2,1)S(1)}, u32[]{:S(2)}, u32[]{:S(2)}) collective-permute-start(bf16[1,18,256]{2,1,0:T(8,128)(2,1)S(1)} %get-tuple-element.148), channel_id=1, source_target_pairs={{0,1},{1,2},{2,3},{4,5},{5,6},{6,7},{8,9},{9,10},{10,11},{12,13},{... | collective-permute-start | bytes 27656 | tf_op jit(solution)/shard_map/ppermute | solution.py:33
  62.9 1.9 %collective-permute-start.5 = (bf16[1,18,256]{2,1,0:T(8,128)(2,1)S(1)}, bf16[1,18,256]{2,1,0:T(8,128)(2,1)S(1)}, u32[]{:S(2)}, u32[]{:S(2)}) collective-permute-start(bf16[1,18,256]{2,1,0:T(8,128)(2,1)S(1)} %get-tuple-element.149), channel_id=1, source_target_pairs={{1,0},{2,1},{3,2},{5,4},{6,5},{7,6},{9,8},{10,9},{11,10},{13,12},{... | collective-permute-start | bytes 27656 | tf_op jit(solution)/shard_map/ppermute | solution.py:34
  64.8 0.0 copy-done.1
  64.9 0.0 collective-permute-done.4
  64.9 3.0 %collective-permute-done.5 = bf16[1,18,256]{2,1,0:T(8,128)(2,1)S(1)} collective-permute-done((bf16[1,18,256]{2,1,0:T(8,128)(2,1)S(1)}, bf16[1,18,256]{2,1,0:T(8,128)(2,1)S(1)}, u32[]{:S(2)}, u32[]{:S(2)}) %collective-permute-start.5) | collective-permute-done | bytes 9248 | tf_op jit(solution)/shard_map/ppermute | solution.py:34
  67.9 0.1 maximum_maximum_fusion.1
  68.0 0.2 fusion.42
  68.2 0.2 multiply_reduce_fusion
  68.4 0.0 copy-done.3
  68.5 0.7 %multiply_convert_fusion.1 = bf16[8,16,256]{2,1,0:T(8,128)(2,1)} fusion(f32[8,16,256]{2,1,0:T(8,128)S(1)} %get-tuple-element.141, f32[256]{0:T(256)S(1)} %copy-done.3, f32[8,16]{1,0:T(8,128)S(1)} %add_rsqrt_fusion, f32[8,16]{1,0:T(8,128)S(1)} %broadcast_multiply_fusion), kind=kLoop, calls=%fused_computation.55 | loop fusion | flops 131072 | bytes 198656 | tf_op jit(solution)/shard_map/convert_element_type | solution.py:136
  (35 shorter events, 0.4 us)
Async XLA Ops:
  0.0 51.2 %copy-start = (bf16[9,256,256]{2,1,0:T(8,128)(2,1)S(1)}, bf16[9,256,256]{2,1,0:T(8,128)(2,1)}, u32[]{:S(2)}) copy-start(bf16[9,256,256]{2,1,0:T(8,128)(2,1)} %param.20) | copy-start | bytes 3538948
  1.6 14.2 %all-to-all-start = ((s32[32,1,256]{2,1,0:T(1,128)}), s32[32,1,256]{2,1,0:T(1,128)S(1)}, u32[]{:S(2)}, u32[]{:S(2)}) async-start(s32[32,1,256]{2,1,0:T(1,128)} %all_to_all.11), calls=%async_computation | async-start | bytes 65536 | tf_op jit(solution)/shard_map/all_to_all | solution.py:85
  15.8 17.9 %all-to-all-start.1 = ((bf16[32,32,256]{2,1,0:T(8,128)(2,1)}), bf16[32,32,256]{2,1,0:T(8,128)(2,1)S(1)}, u32[]{:S(2)}, u32[]{:S(2)}) async-start(bf16[32,32,256]{2,1,0:T(8,128)(2,1)} %pad_maximum_fusion), calls=%async_computation.1 | async-start | bytes 1048576 | tf_op jit(solution)/shard_map/all_to_all | solution.py:84
  39.0 0.9 %copy-start.4 = (bf16[384,256]{1,0:T(8,128)(2,1)S(1)}, bf16[384,256]{1,0:T(8,128)(2,1)}, u32[]{:S(2)}) copy-start(bf16[384,256]{1,0:T(8,128)(2,1)} %param.18) | copy-start | bytes 589828
  39.0 0.9 %copy-start.5 = (f32[256]{0:T(256)S(1)}, f32[256]{0:T(256)}, u32[]{:S(2)}) copy-start(f32[256]{0:T(256)} %param.19) | copy-start | bytes 3076
  40.3 4.3 %collective-permute-start = (bf16[1,32,256]{2,1,0:T(8,128)(2,1)S(1)}, bf16[1,32,256]{2,1,0:T(8,128)(2,1)S(1)}, u32[]{:S(2)}, u32[]{:S(2)}) collective-permute-start(bf16[1,32,256]{2,1,0:T(8,128)(2,1)S(1)} %slice_bitcast_fusion), channel_id=1, source_target_pairs={{0,1},{1,2},{2,3},{4,5},{5,6},{6,7},{8,9},{9,10},{10,11},{12,13},{... | collective-permute-start | bytes 49160 | tf_op jit(solution)/shard_map/ppermute | solution.py:17
  44.6 5.4 %collective-permute-start.1 = (bf16[17,1,256]{2,1,0:T(2,128)(2,1)S(1)}, bf16[17,1,256]{2,1,0:T(2,128)(2,1)S(1)}, u32[]{:S(2)}, u32[]{:S(2)}) collective-permute-start(bf16[17,1,256]{2,1,0:T(2,128)(2,1)S(1)} %fusion.41), channel_id=1, source_target_pairs={{0,4},{4,8},{8,12},{12,16},{16,20},{20,24},{24,28},{28,0},{1,5},{5... | collective-permute-start | bytes 26120 | tf_op jit(solution)/shard_map/ppermute | solution.py:23
  46.1 5.0 %copy-start.2 = (f32[256]{0:T(256)S(1)}, f32[256]{0:T(256)}, u32[]{:S(2)}) copy-start(f32[256]{0:T(256)} %param.21) | copy-start | bytes 3076
  51.1 13.7 %copy-start.1 = (f32[9,256]{1,0:T(8,128)S(1)}, f32[9,256]{1,0:T(8,128)}, u32[]{:S(2)}) copy-start(f32[9,256]{1,0:T(8,128)} %param.22) | copy-start | bytes 27652
  51.2 17.3 %copy-start.3 = (f32[256]{0:T(256)S(1)}, f32[256]{0:T(256)}, u32[]{:S(2)}) copy-start(f32[256]{0:T(256)} %param.23) | copy-start | bytes 3076
  51.6 5.3 %collective-permute-start.2 = (bf16[8,1,256]{2,1,0:T(2,128)(2,1)S(1)}, bf16[8,1,256]{2,1,0:T(2,128)(2,1)S(1)}, u32[]{:S(2)}, u32[]{:S(2)}) collective-permute-start(bf16[8,1,256]{2,1,0:T(2,128)(2,1)S(1)} %get-tuple-element.150), channel_id=1, source_target_pairs={{0,4},{4,8},{8,12},{12,16},{16,20},{20,24},{24,28},{28,0},{1,5},{5... | collective-permute-start | bytes 12296 | tf_op jit(solution)/shard_map/ppermute | solution.py:33
  51.7 5.2 %collective-permute-start.3 = (bf16[8,1,256]{2,1,0:T(2,128)(2,1)S(1)}, bf16[8,1,256]{2,1,0:T(2,128)(2,1)S(1)}, u32[]{:S(2)}, u32[]{:S(2)}) collective-permute-start(bf16[8,1,256]{2,1,0:T(2,128)(2,1)S(1)} %get-tuple-element.151), channel_id=1, source_target_pairs={{4,0},{8,4},{12,8},{16,12},{20,16},{24,20},{28,24},{0,28},{5,1},{9... | collective-permute-start | bytes 12296 | tf_op jit(solution)/shard_map/ppermute | solution.py:34
  56.9 8.0 %collective-permute-start.4 = (bf16[1,18,256]{2,1,0:T(8,128)(2,1)S(1)}, bf16[1,18,256]{2,1,0:T(8,128)(2,1)S(1)}, u32[]{:S(2)}, u32[]{:S(2)}) collective-permute-start(bf16[1,18,256]{2,1,0:T(8,128)(2,1)S(1)} %get-tuple-element.148), channel_id=1, source_target_pairs={{0,1},{1,2},{2,3},{4,5},{5,6},{6,7},{8,9},{9,10},{10,11},{12,13},{... | collective-permute-start | bytes 27656 | tf_op jit(solution)/shard_map/ppermute | solution.py:33
  62.9 5.0 %collective-permute-start.5 = (bf16[1,18,256]{2,1,0:T(8,128)(2,1)S(1)}, bf16[1,18,256]{2,1,0:T(8,128)(2,1)S(1)}, u32[]{:S(2)}, u32[]{:S(2)}) collective-permute-start(bf16[1,18,256]{2,1,0:T(8,128)(2,1)S(1)} %get-tuple-element.149), channel_id=1, source_target_pairs={{1,0},{2,1},{3,2},{5,4},{6,5},{7,6},{9,8},{10,9},{11,10},{13,12},{... | collective-permute-start | bytes 27656 | tf_op jit(solution)/shard_map/ppermute | solution.py:34
where the time goes:
time: 69.6 us; the launch traced here: 69.2 us
  waiting for transfers between devices  26.9 us (39%)
  starting transfers between devices  26.2 us (38%)
  other arithmetic  5.94 us (9%)
  matrix products  5.62 us (8%)
  local copies, waits for them, and re-layouts  3.93 us (6%)
    all_to_all x1, waiting for transfers between devices, on_device(): lax.all_to_all(packed, ('lon', 'lat'), split_axis=0, concat_axis=0, tiled...  15.3 us
    all_to_all x1, starting transfers between devices, on_device(): lax.all_to_all(codes, ('lon', 'lat'), split_axis=0, concat_axis=0, tiled=...  7.1 us
    ppermute x2, starting transfers between devices, with_halo(): before = lax.ppermute(last, axis, up)  6.1 us
    ppermute x2, starting transfers between devices, with_halo(): after = lax.ppermute(leading, axis, down)  6.07 us
    dot_general x4, matrix products, spread_block(): jnp.einsum('cgr,skgr->csk', cell_hot, spread, preferred_element_type=jnp....  4.84 us
    all_to_all x1, waiting for transfers between devices, on_device(): lax.all_to_all(codes, ('lon', 'lat'), split_axis=0, concat_axis=0, tiled=...  3.8 us
    ppermute x1, waiting for transfers between devices, shifted_2(): return lax.ppermute(value, axis, pairs)  3.7 us
    ppermute x1, starting transfers between devices, shifted(): return lax.ppermute(value, axis, pairs)  3.07 us
  transfers between devices with their start and end apart: 8, of which 5 were waited for; matrix products, arithmetic and copies ran while one was open for 7% of the time, Pallas kernels for 0%

commit v1 on v0

v1 whole, which is shorter than its diff:
```python
import functools

import jax
import jax.numpy as jnp
from jax import lax
from jax.experimental import pallas as pl
from jax.experimental.pallas import tpu as pltpu
from jax.sharding import PartitionSpec as P

D = 256
OBS_VARS = 31
WIDTH = OBS_VARS + 1
SLOTS = 12
TLAT = 16
TLON = 32
HALF = TLON // 2
LANES = 128
VMEM_LIMIT = 48 << 20


def whole(shape):
    return pl.BlockSpec(shape, lambda *_: (0,) * len(shape))


def pack_kernel(count_ref, values_ref, offset_ref, cell_ref, slot_ref, out_ref):
    tiles, _, capacity = values_ref.shape
    halves = capacity // LANES
    position = lax.broadcasted_iota(jnp.int32, (1, capacity), 1)
    cell = cell_ref[...]
    column = cell % TLON
    row = (cell // TLON).astype(jnp.float32)
    code = ((column % 2) * HALF + column // 2).astype(jnp.float32)
    slot = slot_ref[...].astype(jnp.float32)
    for d in range(tiles):
        offset = offset_ref[d]
        radius = offset[0:1] * offset[0:1] + offset[1:2] * offset[1:2]
        weight = jnp.where(position < count_ref[0, d], jnp.exp(-2.0 * radius), 0.0)
        scaled = values_ref[d].astype(jnp.float32) * weight
        packed = jnp.concatenate([scaled, weight], axis=0).astype(jnp.bfloat16)
        codes = [
            part[d : d + 1, h * LANES : (h + 1) * LANES]
            for part in (slot, row, code)
            for h in range(halves)
        ]
        codes.append(jnp.zeros((8 - len(codes), LANES), jnp.float32))
        for h in range(halves):
            out_ref[d, h * WIDTH : (h + 1) * WIDTH, :] = packed[:, h * LANES : (h + 1) * LANES]
        out_ref[d, halves * WIDTH :, :] = jnp.concatenate(codes, axis=0).astype(jnp.bfloat16)


def pack(obs_values, obs_offset, obs_cell, obs_slot, obs_count):
    tiles, _, capacity = obs_values.shape
    rows = capacity // LANES * WIDTH + 8
    return pl.pallas_call(
        pack_kernel,
        grid=(1,),
        in_specs=[
            pl.BlockSpec(memory_space=pltpu.SMEM),
            whole(obs_values.shape),
            whole(obs_offset.shape),
            whole(obs_cell.shape),
            whole(obs_slot.shape),
        ],
        out_specs=whole((tiles, rows, LANES)),
        out_shape=jax.ShapeDtypeStruct((tiles, rows, LANES), jnp.bfloat16),
        compiler_params=pltpu.CompilerParams(vmem_limit_bytes=VMEM_LIMIT),
    )(obs_count, obs_values, obs_offset, obs_cell, obs_slot)


def scatter_kernel(
    x_ref, weight_ref, bias_ref, tile_ref, east_ref, west_ref, hot, spread, total, *, steps
):
    step = pl.program_id(0)
    sources = x_ref.shape[0]
    halves = x_ref.shape[1] // WIDTH
    bins = SLOTS * WIDTH
    iota = lax.broadcasted_iota(jnp.int32, (TLON, LANES), 0).astype(jnp.float32)
    zero = jnp.zeros((TLON, LANES), jnp.bfloat16)
    for g in range(sources):
        codes = x_ref[g, halves * WIDTH :, :].astype(jnp.float32)
        for h in range(halves):
            lanes = slice((halves * g + h) * LANES, (halves * g + h + 1) * LANES)
            value = x_ref[g, h * WIDTH : (h + 1) * WIDTH, :]
            slot = codes[h : h + 1]
            row = codes[halves + h : halves + h + 1]
            column = codes[2 * halves + h : 2 * halves + h + 1]
            lower = jnp.where(row >= TLAT // 2, 1.0, 0.0)
            within = row - lower * (TLAT // 2)
            group = slot + lower * SLOTS
            group = jnp.broadcast_to(group, (WIDTH, LANES)).astype(jnp.bfloat16)
            within = jnp.broadcast_to(within, (TLON, LANES)).astype(jnp.bfloat16)
            column = jnp.where(iota == column, 1.0, 0.0).astype(jnp.bfloat16)
            for r in range(TLAT // 2):
                hot[r * TLON : (r + 1) * TLON, lanes] = jnp.where(
                    within == jnp.bfloat16(r), column, zero
                )
            for s in range(2 * SLOTS):
                spread[s * WIDTH : (s + 1) * WIDTH, lanes] = jnp.where(
                    group == jnp.bfloat16(s), value, zero
                )
    part = lax.dot_general(
        spread[...], hot[...], (((1,), (1,)), ((), ())), preferred_element_type=jnp.float32
    )

    @pl.when(step == 0)
    def _():
        total[...] = part

    @pl.when(step > 0)
    def _():
        total[...] += part

    @pl.when(step == steps - 1)
    def _():
        for half in range(2):
            rows = []
            for s in range(SLOTS):
                first = half * bins + s * WIDTH
                block = total[first : first + WIDTH, :]
                density = block[OBS_VARS:WIDTH, :]
                inverse = 1.0 / (1.0 + density)
                channel = lax.broadcasted_iota(jnp.int32, block.shape, 0)
                rows.append(
                    jnp.where(channel == OBS_VARS, block, block * inverse).astype(jnp.bfloat16)
                )
            gridded = jnp.concatenate(rows, axis=0)
            projected = lax.dot_general(
                gridded,
                weight_ref[...],
                (((0,), (0,)), ((), ())),
                preferred_element_type=jnp.float32,
            )
            embedded = jax.nn.gelu(projected + bias_ref[...]).reshape(TLAT // 2, TLON, D)
            at = slice(half * (TLAT // 2), (half + 1) * (TLAT // 2))
            tile_ref[at] = embedded.astype(jnp.bfloat16)
            last = [embedded[:, c : c + 1] for c in (TLON - 2, HALF - 1, TLON - 1)]
            first = [embedded[:, c : c + 1] for c in (0, HALF)]
            east_ref[at] = jnp.concatenate(last, axis=1).astype(jnp.bfloat16)
            west_ref[at] = jnp.concatenate(first, axis=1).astype(jnp.bfloat16)


def scatter(arrived, embed_weight, embed_bias):
    tiles, rows, _ = arrived.shape
    sources = min(tiles, 32)
    steps = tiles // sources
    depth = sources * (rows // WIDTH) * LANES
    bins = SLOTS * WIDTH
    shapes = [(TLAT, TLON, D), (TLAT, 3, D), (TLAT, 2, D)]
    return pl.pallas_call(
        functools.partial(scatter_kernel, steps=steps),
        grid=(steps,),
        in_specs=[
            pl.BlockSpec((sources, rows, LANES), lambda i: (i, 0, 0)),
            whole(embed_weight.shape),
            whole((1, D)),
        ],
        out_specs=[whole(shape) for shape in shapes],
        out_shape=[jax.ShapeDtypeStruct(shape, jnp.bfloat16) for shape in shapes],
        scratch_shapes=[
            pltpu.VMEM((TLAT // 2 * TLON, depth), jnp.bfloat16),
            pltpu.VMEM((2 * bins, depth), jnp.bfloat16),
            pltpu.VMEM((2 * bins, TLAT // 2 * TLON), jnp.float32),
        ],
        compiler_params=pltpu.CompilerParams(vmem_limit_bytes=VMEM_LIMIT),
    )(arrived, embed_weight, embed_bias.reshape(1, D))


def finish_kernel(
    place_ref,
    tile_ref,
    west_ref,
    east_ref,
    north_ref,
    south_ref,
    weight_ref,
    bias_ref,
    depth_ref,
    gain_ref,
    out_ref,
    even,
    odd,
    coarse_ref,
):
    def place(rows, tile, west, east):
        even[rows, 0:1] = west[:, 1:2]
        even[rows, 1 : HALF + 1] = tile[:, :HALF]
        even[rows, HALF + 1 : HALF + 2] = east[:, 0:1]
        odd[rows, 0:1] = west[:, 0:1]
        odd[rows, 1:2] = west[:, 2:3]
        odd[rows, 2 : HALF + 2] = tile[:, HALF:]
        odd[rows, HALF + 2 : HALF + 3] = east[:, 1:2]

    north = north_ref[...].astype(jnp.float32)
    south = south_ref[...].astype(jnp.float32)
    place(
        slice(3, TLAT + 3),
        tile_ref[...].astype(jnp.float32),
        west_ref[...].astype(jnp.float32),
        east_ref[...].astype(jnp.float32),
    )
    place(slice(0, 3), north[:, :TLON], north[:, TLON : TLON + 3], north[:, TLON + 3 :])
    place(
        slice(TLAT + 3, TLAT + 5), south[:, :TLON], south[:, TLON : TLON + 3], south[:, TLON + 3 :]
    )
    out_rows = TLAT // 2
    span = 24
    pieces = []
    for a in range(3):
        for source, at in ((odd, 0), (even, 0), (odd, 1)):
            rows = [source[2 * p + a, at : at + span, :] for p in range(out_rows + 2)]
            pieces.append(jnp.concatenate(rows, axis=0).astype(jnp.bfloat16))
    strided = jnp.dot(
        jnp.concatenate(pieces, axis=1), weight_ref[...], preferred_element_type=jnp.float32
    )
    coarse = jax.nn.gelu(strided + bias_ref[...]).astype(jnp.bfloat16).astype(jnp.float32)
    coarse_ref[...] = coarse.reshape(out_rows + 2, span, D)

    @pl.when(place_ref[0] == 0)
    def _():
        coarse_ref[0] = jnp.zeros((span, D), jnp.float32)

    @pl.when(place_ref[0] == place_ref[1] - 1)
    def _():
        coarse_ref[out_rows + 1] = jnp.zeros((span, D), jnp.float32)

    mixed = coarse_ref[1 : out_rows + 1, 1 : HALF + 1]
    for a in range(3):
        for c in range(3):
            tap = depth_ref[3 * a + c : 3 * a + c + 1, :]
            mixed = mixed + coarse_ref[a : a + out_rows, c : c + HALF] * tap
    centre = mixed - jnp.mean(mixed, axis=-1, keepdims=True)
    variance = jnp.mean(centre * centre, axis=-1, keepdims=True)
    out_ref[...] = (centre * lax.rsqrt(variance + 1e-05) * gain_ref[...]).astype(jnp.bfloat16)


def finish(place, tile, west, east, north, south, stride_weight, stride_bias, depth_weight, gain):
    arrays = [
        tile,
        west,
        east,
        north,
        south,
        stride_weight.reshape(9 * D, D),
        stride_bias.reshape(1, D),
        depth_weight,
        gain.reshape(1, D),
    ]
    out = (TLAT // 2, HALF, D)
    return pl.pallas_call(
        finish_kernel,
        grid=(1,),
        in_specs=[pl.BlockSpec(memory_space=pltpu.SMEM)] + [whole(a.shape) for a in arrays],
        out_specs=whole(out),
        out_shape=jax.ShapeDtypeStruct(out, jnp.bfloat16),
        scratch_shapes=[
            pltpu.VMEM((TLAT + 5, 24, D), jnp.float32),
            pltpu.VMEM((TLAT + 5, 32, D), jnp.float32),
            pltpu.VMEM((TLAT // 2 + 2, 24, D), jnp.float32),
        ],
        compiler_params=pltpu.CompilerParams(vmem_limit_bytes=VMEM_LIMIT),
    )(place, *arrays)


def shifted(value, axis, by, wrap):
    size = lax.axis_size(axis)
    pairs = [(i, (i + by) % size) for i in range(size) if wrap or 0 <= i + by < size]
    return lax.ppermute(value, axis, pairs)


def on_device(
    obs_values,
    obs_offset,
    obs_cell,
    obs_slot,
    obs_count,
    embed_weight,
    embed_bias,
    stride_weight,
    stride_bias,
    depth_weight,
    norm_gain,
):
    packed = pack(obs_values, obs_offset, obs_cell, obs_slot, obs_count)
    arrived = lax.all_to_all(packed, ("lon", "lat"), split_axis=0, concat_axis=0, tiled=True)
    tile, last, first = scatter(arrived, embed_weight, embed_bias)
    west = shifted(last, "lon", 1, True)
    east = shifted(first, "lon", -1, True)
    framed = jnp.concatenate([tile, west, east], axis=1)
    north = shifted(framed[TLAT - 3 :], "lat", 1, False)
    south = shifted(framed[:2], "lat", -1, False)
    place = jnp.stack([lax.axis_index("lat"), jnp.int32(lax.axis_size("lat"))])
    return finish(
        place,
        tile,
        west,
        east,
        north,
        south,
        stride_weight,
        stride_bias,
        depth_weight,
        norm_gain,
    )


def solution(mesh):
    placed = (
        P(("lon", "lat"), None, None),
        P(("lon", "lat"), None, None),
        P(("lon", "lat"), None),
        P(("lon", "lat"), None),
        P(("lon", "lat"), None),
        P(),
        P(),
        P(),
        P(),
        P(),
        P(),
    )
    return jax.shard_map(
        on_device, mesh=mesh, in_specs=placed, out_specs=P("lat", "lon", None), check_vma=False
    )
```

time: 69.6 us -> 48.8 us (0.70)
  waiting for transfers between devices: 26.9 us -> 2.49 us
  blocking collectives: 0 us -> 23.4 us
  starting transfers between devices: 26.2 us -> 10.5 us
  Pallas kernels: 0 us -> 7.49 us
  other arithmetic: 5.94 us -> 0.1 us
  matrix products: 5.62 us -> 0 us
    all_to_all x0 -> x1, blocking collectives: none -> 23.4 us  [on_device(): lax.all_to_all(packed, ('lon', 'lat'), split_axis=0, concat_axis=0, tiled...]
    all_to_all x2 -> x0, waiting for transfers between devices: 19.1 us -> none  [the longest x1 15.3 us: on_device(): lax.all_to_all(packed, ('lon', 'lat'), split_axis=0, concat_axis=0, tiled...]
    ppermute x5 -> x0, starting transfers between devices: 13.4 us -> none  [the longest x2 6.1 us: with_halo(): before = lax.ppermute(last, axis, up)]
    all_to_all x2 -> x0, starting transfers between devices: 9.7 us -> none  [the longest x1 7.1 us: on_device(): lax.all_to_all(codes, ('lon', 'lat'), split_axis=0, concat_axis=0, tiled=...]
    ppermute x5 -> x0, waiting for transfers between devices: 7.79 us -> none  [the longest x1 3.7 us: shifted_2(): return lax.ppermute(value, axis, pairs)]
    pallas_call x0 -> x3, Pallas kernels: none -> 7.49 us  [the longest x1 4.57 us: scatter(): pl.pallas_call(functools.partial(scatter_kernel, steps=steps), grid=(step...]
    ppermute x1 -> x4, starting transfers between devices: 3.07 us -> 10.5 us  [shifted(): return lax.ppermute(value, axis, pairs)]
    dot_general x6 -> x0, matrix products: 5.62 us -> none  [the longest x4 4.84 us: spread_block(): jnp.einsum('cgr,skgr->csk', cell_hot, spread, preferred_element_type=jnp....]
  transfers between devices with their start and end apart: 8 -> 4, of which waited for: 5 -> 3; matrix products, arithmetic and copies ran while one was open for 7% -> 0% of each run, Pallas kernels for 0% -> 0%
where the time goes in v1:
time: 48.8 us; the launch traced here: 48.4 us
  blocking collectives  23.4 us (48%)
  starting transfers between devices  10.5 us (22%)
  Pallas kernels  7.49 us (15%)
  local copies, waits for them, and re-layouts  4.36 us (9%)
  waiting for transfers between devices  2.49 us (5%)
    all_to_all x1, blocking collectives, on_device(): lax.all_to_all(packed, ('lon', 'lat'), split_axis=0, concat_axis=0, tiled...  23.4 us
    ppermute x4, starting transfers between devices, shifted(): return lax.ppermute(value, axis, pairs)  10.5 us
    pallas_call x1, Pallas kernels, scatter(): pl.pallas_call(functools.partial(scatter_kernel, steps=steps), grid=(step...  4.57 us
    unnamed x21, local copies, waits for them, and re-layouts  4.36 us
    ppermute x4, waiting for transfers between devices, shifted(): return lax.ppermute(value, axis, pairs)  2.49 us
    pallas_call x1, Pallas kernels, finish(): pl.pallas_call(finish_kernel, grid=(1,), in_specs=[pl.BlockSpec(memory_sp...  2.11 us
  transfers between devices with their start and end apart: 4, of which 3 were waited for; matrix products, arithmetic and copies ran while one was open for 0% of the time, Pallas kernels for 0%

profile of v1, /device:TPU:1, one launch (start us, length us, event | category | flops | bytes accessed | tf_op | source)
XLA Modules:
  0.0 48.4 jit_solution(9167546826770328325)
XLA Ops:
  0.0 1.3 %copy.12.values_ref = bf16[32,31,256]{2,1,0:T(8,128)(2,1)S(1)} copy(bf16[32,31,256]{2,0,1:T(8,128)(2,1)} %param.11) | data formatting | bytes 1015808 | tf_op args[0]
  1.3 0.0 copy-start.2
  1.3 0.8 %copy-done.2 = f32[32,2,256]{2,1,0:T(2,128)S(1)} copy-done((f32[32,2,256]{2,1,0:T(2,128)S(1)}, f32[32,2,256]{2,1,0:T(2,128)}, u32[]{:S(2)}) %copy-start.2) | copy-done | bytes 65560
  2.2 0.0 copy-start.3
  2.2 0.8 %copy-done.3 = s32[32,256]{1,0:T(8,128)S(1)} copy-done((s32[32,256]{1,0:T(8,128)S(1)}, s32[32,256]{1,0:T(8,128)}, u32[]{:S(2)}) %copy-start.3) | copy-done | bytes 32792
  2.9 0.0 copy-start.4
  2.9 0.8 %copy-done.4 = s32[32,256]{1,0:T(8,128)S(1)} copy-done((s32[32,256]{1,0:T(8,128)S(1)}, s32[32,256]{1,0:T(8,128)}, u32[]{:S(2)}) %copy-start.4) | copy-done | bytes 32792
  3.7 0.0 copy-start.9
  3.7 0.7 %copy-done.9 = s32[1,32]{1,0:T(1,128)S(1)} copy-done((s32[1,32]{1,0:T(1,128)S(1)}, s32[1,32]{1,0:T(1,128)}, u32[]{:S(2)}) %copy-start.9) | copy-done | bytes 152
  4.3 0.0 copy-start.1
  4.3 0.0 copy-start.6
  4.3 0.8 %shard_map.109 = bf16[32,72,128]{2,1,0:T(8,128)(2,1)S(1)} custom-call(s32[1,32]{1,0:T(1,128)S(1)} %copy-done.9, bf16[32,31,256]{2,1,0:T(8,128)(2,1)S(1)} %copy.12.values_ref, f32[32,2,256]{2,1,0:T(2,128)S(1)} %copy-done.2, s32[32,256]{1,0:T(8,128)S(1)} %copy-done.3, s32[32,256]{1,0:T(8,128)S(1)} %copy-done.4), custom_call_target="tpu_custom_call" | custom-call | tf_op jit(solution)/shard_map/pallas_call | solution.py:54
  5.2 0.0 copy-start
  5.2 0.0 copy-start.5
  5.2 0.0 copy-start.7
  5.2 0.0 copy-start.8
  5.2 23.4 %all_to_all.5.x_ref = bf16[32,72,128]{2,1,0:T(8,128)(2,1)S(1)} all-to-all(bf16[32,72,128]{2,1,0:T(8,128)(2,1)S(1)} %shard_map.109), channel_id=1, replica_groups=mesh['lon'=8,'lat'=4] {'lon','lat'}, dimensions={0} | all-to-all | bytes 1179648 | tf_op jit(solution)/shard_map/all_to_all | solution.py:284
  28.6 0.0 copy-done.1
  28.6 0.0 copy-done.6
  28.6 4.6 %shard_map.110 = (bf16[16,32,256]{2,1,0:T(8,128)(2,1)S(1)}, bf16[16,3,256]{2,1,0:T(4,128)(2,1)S(1)}, bf16[16,2,256]{2,1,0:T(2,128)(2,1)S(1)}) custom-call(bf16[32,72,128]{2,1,0:T(8,128)(2,1)S(1)} %all_to_all.5.x_ref, bf16[384,256]{1,0:T(8,128)(2,1)S(1)} %copy-done.1, f32[1,256]{1,0:T(1,128)S(1)} %bitcast.6), custom_call_target="tpu_custom_call" | custom-call | tf_op jit(solution)/shard_map/pallas_call | solution.py:149
  33.2 0.9 %collective-permute-start = (bf16[16,3,256]{2,1,0:T(4,128)(2,1)S(1)}, bf16[16,3,256]{2,1,0:T(4,128)(2,1)S(1)}, u32[]{:S(2)}, u32[]{:S(2)}) collective-permute-start(bf16[16,3,256]{2,1,0:T(4,128)(2,1)S(1)} %get-tuple-element.9), channel_id=1, source_target_pairs={{0,4},{4,8},{8,12},{12,16},{16,20},{20,24},{24,28},{28,0},{1,5},{5... | collective-permute-start | bytes 73736 | tf_op jit(solution)/shard_map/ppermute | solution.py:267
  34.0 3.4 %collective-permute-start.1 = (bf16[16,2,256]{2,1,0:T(2,128)(2,1)S(1)}, bf16[16,2,256]{2,1,0:T(2,128)(2,1)S(1)}, u32[]{:S(2)}, u32[]{:S(2)}) collective-permute-start(bf16[16,2,256]{2,1,0:T(2,128)(2,1)S(1)} %get-tuple-element.10), channel_id=1, source_target_pairs={{0,28},{4,0},{8,4},{12,8},{16,12},{20,16},{24,20},{28,24},{1,29},{... | collective-permute-start | bytes 49160 | tf_op jit(solution)/shard_map/ppermute | solution.py:267
  37.4 0.9 %collective-permute-done.1.east_ref = bf16[16,2,256]{2,1,0:T(2,128)(2,1)S(1)} collective-permute-done((bf16[16,2,256]{2,1,0:T(2,128)(2,1)S(1)}, bf16[16,2,256]{2,1,0:T(2,128)(2,1)S(1)}, u32[]{:S(2)}, u32[]{:S(2)}) %collective-permute-start.1) | collective-permute-done | bytes 16416 | tf_op jit(solution)/shard_map/ppermute | solution.py:267
  38.2 0.4 collective-permute-done.west_ref
  38.7 3.6 %collective-permute-start.3 = (bf16[2,37,256]{2,1,0:T(8,128)(2,1)S(1)}, bf16[2,37,256]{2,1,0:T(8,128)(2,1)S(1)}, u32[]{:S(2)}, u32[]{:S(2)}) collective-permute-start(bf16[2,37,256]{2,1,0:T(8,128)(2,1)S(1)} %pad_maximum_fusion.1), channel_id=1, source_target_pairs={{1,0},{2,1},{3,2},{5,4},{6,5},{7,6},{9,8},{10,9},{11,10},{13,12},{... | collective-permute-start | bytes 113672 | tf_op jit(solution)/shard_map/ppermute | solution.py:267
  42.3 2.7 %collective-permute-start.2 = (bf16[3,37,256]{2,1,0:T(8,128)(2,1)S(1)}, bf16[3,37,256]{2,1,0:T(8,128)(2,1)S(1)}, u32[]{:S(2)}, u32[]{:S(2)}) collective-permute-start(bf16[3,37,256]{2,1,0:T(8,128)(2,1)S(1)} %pad_maximum_fusion), channel_id=1, source_target_pairs={{0,1},{1,2},{2,3},{4,5},{5,6},{6,7},{8,9},{9,10},{10,11},{12,13},{... | collective-permute-start | bytes 170504 | tf_op jit(solution)/shard_map/ppermute | solution.py:267
  45.0 0.1 pad_add_fusion.place_ref
  45.1 0.0 collective-permute-done.3.south_ref
  45.1 1.2 %collective-permute-done.2.north_ref = bf16[3,37,256]{2,1,0:T(8,128)(2,1)S(1)} collective-permute-done((bf16[3,37,256]{2,1,0:T(8,128)(2,1)S(1)}, bf16[3,37,256]{2,1,0:T(8,128)(2,1)S(1)}, u32[]{:S(2)}, u32[]{:S(2)}) %collective-permute-start.2) | collective-permute-done | bytes 56864 | tf_op jit(solution)/shard_map/ppermute | solution.py:267
  46.3 0.0 copy-done
  46.3 0.0 copy-done.5
  46.3 0.0 copy-done.7
  46.3 0.0 copy-done.8
  46.3 2.1 %shard_map.111 = bf16[8,16,256]{2,1,0:T(8,128)(2,1)} custom-call(s32[2]{0:T(128)S(1)} %pad_add_fusion.place_ref, bf16[16,32,256]{2,1,0:T(8,128)(2,1)S(1)} %get-tuple-element.8.tile_ref, bf16[16,3,256]{2,1,0:T(4,128)(2,1)S(1)} %collective-permute-done.west_ref, bf16[16,2,256]{2,1,0:T(2,128)(2,1)S(1)} %collective-permute-done.1.east_ref, ...), custom_call_target="tpu_custom_call" | custom-call | tf_op jit(solution)/shard_map/pallas_call | solution.py:249
  (2 shorter events, 0.0 us)
Async XLA Ops:
  1.3 0.8 %copy-start.2 = (f32[32,2,256]{2,1,0:T(2,128)S(1)}, f32[32,2,256]{2,1,0:T(2,128)}, u32[]{:S(2)}) copy-start(f32[32,2,256]{2,1,0:T(2,128)} %offset_ref.1) | copy-start | bytes 196612
  2.2 0.8 %copy-start.3 = (s32[32,256]{1,0:T(8,128)S(1)}, s32[32,256]{1,0:T(8,128)}, u32[]{:S(2)}) copy-start(s32[32,256]{1,0:T(8,128)} %cell_ref.1) | copy-start | bytes 98308
  2.9 0.8 %copy-start.4 = (s32[32,256]{1,0:T(8,128)S(1)}, s32[32,256]{1,0:T(8,128)}, u32[]{:S(2)}) copy-start(s32[32,256]{1,0:T(8,128)} %slot_ref.1) | copy-start | bytes 98308
  3.7 0.7 %copy-start.9 = (s32[1,32]{1,0:T(1,128)S(1)}, s32[1,32]{1,0:T(1,128)}, u32[]{:S(2)}) copy-start(s32[1,32]{1,0:T(1,128)} %count_ref.1) | copy-start | bytes 388
  4.3 24.2 %copy-start.1 = (bf16[384,256]{1,0:T(8,128)(2,1)S(1)}, bf16[384,256]{1,0:T(8,128)(2,1)}, u32[]{:S(2)}) copy-start(bf16[384,256]{1,0:T(8,128)(2,1)} %weight_ref.1) | copy-start | bytes 589828
  4.3 24.2 %copy-start.6 = (f32[256]{0:T(256)S(1)}, f32[256]{0:T(256)}, u32[]{:S(2)}) copy-start(f32[256]{0:T(256)} %param.17) | copy-start | bytes 3076
  5.2 41.1 %copy-start = (bf16[9,256,256]{2,1,0:T(8,128)(2,1)S(1)}, bf16[9,256,256]{2,1,0:T(8,128)(2,1)}, u32[]{:S(2)}) copy-start(bf16[9,256,256]{2,1,0:T(8,128)(2,1)} %param.18) | copy-start | bytes 3538948
  5.2 41.1 %copy-start.5 = (f32[9,256]{1,0:T(8,128)S(1)}, f32[9,256]{1,0:T(8,128)}, u32[]{:S(2)}) copy-start(f32[9,256]{1,0:T(8,128)} %depth_ref.1) | copy-start | bytes 27652
  5.2 41.1 %copy-start.7 = (f32[256]{0:T(256)S(1)}, f32[256]{0:T(256)}, u32[]{:S(2)}) copy-start(f32[256]{0:T(256)} %param.19) | copy-start | bytes 3076
  5.2 41.1 %copy-start.8 = (f32[256]{0:T(256)S(1)}, f32[256]{0:T(256)}, u32[]{:S(2)}) copy-start(f32[256]{0:T(256)} %param.21) | copy-start | bytes 3076
  33.2 5.5 %collective-permute-start = (bf16[16,3,256]{2,1,0:T(4,128)(2,1)S(1)}, bf16[16,3,256]{2,1,0:T(4,128)(2,1)S(1)}, u32[]{:S(2)}, u32[]{:S(2)}) collective-permute-start(bf16[16,3,256]{2,1,0:T(4,128)(2,1)S(1)} %get-tuple-element.9), channel_id=1, source_target_pairs={{0,4},{4,8},{8,12},{12,16},{16,20},{20,24},{24,28},{28,0},{1,5},{5... | collective-permute-start | bytes 73736 | tf_op jit(solution)/shard_map/ppermute | solution.py:267
  34.0 4.2 %collective-permute-start.1 = (bf16[16,2,256]{2,1,0:T(2,128)(2,1)S(1)}, bf16[16,2,256]{2,1,0:T(2,128)(2,1)S(1)}, u32[]{:S(2)}, u32[]{:S(2)}) collective-permute-start(bf16[16,2,256]{2,1,0:T(2,128)(2,1)S(1)} %get-tuple-element.10), channel_id=1, source_target_pairs={{0,28},{4,0},{8,4},{12,8},{16,12},{20,16},{24,20},{28,24},{1,29},{... | collective-permute-start | bytes 49160 | tf_op jit(solution)/shard_map/ppermute | solution.py:267
  38.7 6.4 %collective-permute-start.3 = (bf16[2,37,256]{2,1,0:T(8,128)(2,1)S(1)}, bf16[2,37,256]{2,1,0:T(8,128)(2,1)S(1)}, u32[]{:S(2)}, u32[]{:S(2)}) collective-permute-start(bf16[2,37,256]{2,1,0:T(8,128)(2,1)S(1)} %pad_maximum_fusion.1), channel_id=1, source_target_pairs={{1,0},{2,1},{3,2},{5,4},{6,5},{7,6},{9,8},{10,9},{11,10},{13,12},{... | collective-permute-start | bytes 113672 | tf_op jit(solution)/shard_map/ppermute | solution.py:267
  42.3 4.0 %collective-permute-start.2 = (bf16[3,37,256]{2,1,0:T(8,128)(2,1)S(1)}, bf16[3,37,256]{2,1,0:T(8,128)(2,1)S(1)}, u32[]{:S(2)}, u32[]{:S(2)}) collective-permute-start(bf16[3,37,256]{2,1,0:T(8,128)(2,1)S(1)} %pad_maximum_fusion), channel_id=1, source_target_pairs={{0,1},{1,2},{2,3},{4,5},{5,6},{6,7},{8,9},{9,10},{10,11},{12,13},{... | collective-permute-start | bytes 170504 | tf_op jit(solution)/shard_map/ppermute | solution.py:267

commit v2 on v0

v2 whole, which is shorter than its diff:
```python
import functools

import jax
import jax.numpy as jnp
from jax import lax
from jax.experimental import pallas as pl
from jax.experimental.pallas import tpu as pltpu
from jax.sharding import PartitionSpec as P

D = 256
OBS_VARS = 31
WIDTH = OBS_VARS + 1
SLOTS = 12
BINS = SLOTS * WIDTH
TLAT = 16
TLON = 32
HALF = TLON // 2
ROWS = TLAT // 2
LANES = 128
GROUP = 16
CHUNK = 8
SPAN = 24
FRAME = TLON + 5

ANY = pl.BlockSpec(memory_space=pl.ANY)
VMEM = pl.BlockSpec(memory_space=pltpu.VMEM)


def pack_kernel(
    count_hbm,
    values_hbm,
    offset_hbm,
    cell_hbm,
    slot_hbm,
    out_hbm,
    count,
    values,
    offset,
    cell,
    slot,
    rows,
    out,
    here,
    sent,
):
    tiles, capacity = cell.shape
    halves = capacity // LANES
    stride = halves * WIDTH + 8
    groups = tiles // GROUP

    def at(j):
        return pl.ds(j * GROUP, GROUP)

    pairs = ((count_hbm, count), (offset_hbm, offset), (cell_hbm, cell), (slot_hbm, slot))
    small = [
        pltpu.make_async_copy(a, b, here.at[groups + i]) for i, (a, b) in enumerate(pairs)
    ]
    large = [
        pltpu.make_async_copy(values_hbm.at[:, at(j)], values.at[:, at(j)], here.at[j])
        for j in range(groups)
    ]
    for copy in small + large:
        copy.start()
    for copy in small:
        copy.wait()
    square = (tiles, tiles)
    diagonal = lax.broadcasted_iota(jnp.int32, square, 0) == lax.broadcasted_iota(
        jnp.int32, square, 1
    )
    counts = jnp.sum(jnp.where(diagonal, count[...], 0), axis=1, keepdims=True)
    position = lax.broadcasted_iota(jnp.int32, (tiles, capacity), 1)
    dy, dx = offset[:, 0, :], offset[:, 1, :]
    weight = jnp.where(position < counts, jnp.exp(-2.0 * (dy * dy + dx * dx)), 0.0)
    column = cell[...] % TLON
    codes = (
        slot[...].astype(jnp.float32),
        (cell[...] // TLON).astype(jnp.float32),
        ((column % 2) * HALF + column // 2).astype(jnp.float32),
    )
    zero = jnp.zeros((GROUP, LANES), jnp.float32)
    base = halves * WIDTH
    sends = []
    for j in range(groups):
        own = slice(j * GROUP, (j + 1) * GROUP)

        def put(row, value, h, first=j * GROUP * stride):
            rows[pl.ds(first + row, GROUP, stride=stride), :] = value[
                :, h * LANES : (h + 1) * LANES
            ]

        for h in range(halves):
            put(h * WIDTH + OBS_VARS, weight[own], h)
            for i, code in enumerate(codes):
                put(base + i * halves + h, code[own], h)
        for r in range(len(codes) * halves, 8):
            put(base + r, zero, 0)
        large[j].wait()
        for k in range(OBS_VARS):
            scaled = values[k, own, :].astype(jnp.float32) * weight[own]
            for h in range(halves):
                put(h * WIDTH + k, scaled, h)
        for d in range(j * GROUP, (j + 1) * GROUP):
            out[d] = rows[d * stride : (d + 1) * stride, :].astype(jnp.bfloat16)
        sends.append(pltpu.make_async_copy(out.at[at(j)], out_hbm.at[at(j)], sent.at[j]))
        sends[-1].start()
    for copy in sends:
        copy.wait()


def pack(obs_values, obs_offset, obs_cell, obs_slot, obs_count):
    tiles, _, capacity = obs_values.shape
    stride = capacity // LANES * WIDTH + 8
    values = jnp.transpose(obs_values, (1, 0, 2))
    shape = (tiles, stride, LANES)
    arrays = (obs_count, values, obs_offset, obs_cell, obs_slot)
    return pl.pallas_call(
        pack_kernel,
        in_specs=[ANY] * len(arrays),
        out_specs=ANY,
        out_shape=jax.ShapeDtypeStruct(shape, jnp.bfloat16),
        scratch_shapes=[pltpu.VMEM(a.shape, a.dtype) for a in arrays]
        + [
            pltpu.VMEM((tiles * stride, LANES), jnp.float32),
            pltpu.VMEM(shape, jnp.bfloat16),
            pltpu.SemaphoreType.DMA((tiles // GROUP + 4,)),
            pltpu.SemaphoreType.DMA((tiles // GROUP,)),
        ],
        compiler_params=pltpu.CompilerParams(vmem_limit_bytes=60 << 20),
    )(*arrays)


def scatter_kernel(x_ref, weight_ref, bias_ref, tile_ref, last_ref, first_ref, hot, spread, total):
    tiles, rows, _ = x_ref.shape
    halves = rows // WIDTH
    iota = lax.broadcasted_iota(jnp.int32, (TLON, LANES), 0).astype(jnp.float32)
    zero = jnp.zeros((TLON, LANES), jnp.bfloat16)

    def part(source, first):
        for g in range(CHUNK):
            codes = x_ref[source + g, halves * WIDTH :, :].astype(jnp.float32)
            for h in range(halves):
                at = first + (halves * g + h) * LANES
                lanes = slice(at, at + LANES)
                value = x_ref[source + g, h * WIDTH : (h + 1) * WIDTH, :]
                slot = codes[h : h + 1]
                row = codes[halves + h : halves + h + 1]
                column = codes[2 * halves + h : 2 * halves + h + 1]
                lower = jnp.where(row >= ROWS, 1.0, 0.0)
                group = jnp.broadcast_to(slot + lower * SLOTS, (WIDTH, LANES))
                within = jnp.broadcast_to(row - lower * ROWS, (TLON, LANES))
                group = group.astype(jnp.bfloat16)
                within = within.astype(jnp.bfloat16)
                column = jnp.where(iota == column, 1.0, 0.0).astype(jnp.bfloat16)
                for r in range(ROWS):
                    hot[r * TLON : (r + 1) * TLON, lanes] = jnp.where(
                        within == jnp.bfloat16(r), column, zero
                    )
                for s in range(2 * SLOTS):
                    spread[s * WIDTH : (s + 1) * WIDTH, lanes] = jnp.where(
                        group == jnp.bfloat16(s), value, zero
                    )
        lanes = slice(first, first + CHUNK * halves * LANES)
        return lax.dot_general(
            spread[:, lanes],
            hot[:, lanes],
            (((1,), (1,)), ((), ())),
            preferred_element_type=jnp.float32,
        )

    def summed(start):
        chunks = range(hot.shape[1] // (CHUNK * halves * LANES))
        return functools.reduce(
            jnp.add, [part(start + c * CHUNK, c * CHUNK * halves * LANES) for c in chunks]
        )

    sources = hot.shape[1] // (halves * LANES)
    if tiles == sources:
        total[...] = summed(0)
    else:
        total[...] = jnp.zeros(total.shape, jnp.float32)

        @pl.loop(0, tiles // sources)
        def _(step):
            total[...] += summed(step * sources)

    for half in range(2):
        groups = []
        for s in range(SLOTS):
            first = half * BINS + s * WIDTH
            block = total[first : first + WIDTH, :]
            inverse = 1.0 / (1.0 + block[OBS_VARS:WIDTH, :])
            channel = lax.broadcasted_iota(jnp.int32, block.shape, 0)
            ratio = jnp.where(channel == OBS_VARS, block, block * inverse)
            groups.append(ratio.astype(jnp.bfloat16))
        projected = lax.dot_general(
            jnp.concatenate(groups, axis=0),
            weight_ref[...],
            (((0,), (0,)), ((), ())),
            preferred_element_type=jnp.float32,
        )
        embedded = jax.nn.gelu(projected + bias_ref[...]).reshape(ROWS, TLON, D)
        at = slice(half * ROWS, (half + 1) * ROWS)
        tile_ref[at] = embedded.astype(jnp.bfloat16)
        last = [embedded[:, c : c + 1] for c in (TLON - 2, HALF - 1, TLON - 1)]
        first = [embedded[:, c : c + 1] for c in (0, HALF)]
        last_ref[at] = jnp.concatenate(last, axis=1).astype(jnp.bfloat16)
        first_ref[at] = jnp.concatenate(first, axis=1).astype(jnp.bfloat16)


def scatter(arrived, embed_weight, embed_bias):
    tiles, rows, _ = arrived.shape
    depth = min(tiles, 32) * (rows // WIDTH) * LANES
    shapes = [(TLAT, TLON, D), (TLAT, 3, D), (TLAT, 2, D)]
    return pl.pallas_call(
        scatter_kernel,
        in_specs=[VMEM] * 3,
        out_specs=[VMEM] * 3,
        out_shape=[jax.ShapeDtypeStruct(shape, jnp.bfloat16) for shape in shapes],
        scratch_shapes=[
            pltpu.VMEM((ROWS * TLON, depth), jnp.bfloat16),
            pltpu.VMEM((2 * BINS, depth), jnp.bfloat16),
            pltpu.VMEM((2 * BINS, ROWS * TLON), jnp.float32),
        ],
        compiler_params=pltpu.CompilerParams(vmem_limit_bytes=32 << 20),
    )(arrived, embed_weight, embed_bias.reshape(1, D))


def put_rows(even, odd, rows, tile, west, east):
    even[rows, 0:1] = west[:, 1:2]
    even[rows, 1 : HALF + 1] = tile[:, :HALF]
    even[rows, HALF + 1 : HALF + 2] = east[:, 0:1]
    odd[rows, 0:1] = west[:, 0:1]
    odd[rows, 1:2] = west[:, 2:3]
    odd[rows, 2 : HALF + 2] = tile[:, HALF:]
    odd[rows, HALF + 2 : HALF + 3] = east[:, 1:2]


def strided_rows(even, odd, starts, weight_ref, bias_ref):
    pieces = []
    for a in range(3):
        for source, at in ((odd, 0), (even, 0), (odd, 1)):
            rows = [source[start + a, at : at + SPAN, :] for start in starts]
            pieces.append(jnp.concatenate(rows, axis=0).astype(jnp.bfloat16))
    strided = jnp.dot(
        jnp.concatenate(pieces, axis=1), weight_ref[...], preferred_element_type=jnp.float32
    )
    coarse = jax.nn.gelu(strided + bias_ref[...]).astype(jnp.bfloat16)
    return coarse.astype(jnp.float32).reshape(len(starts), SPAN, D)


def finished(coarse, first, count, depth_ref, gain_ref):
    mixed = coarse[first + 1 : first + count + 1, 1 : HALF + 1]
    for a in range(3):
        for c in range(3):
            tap = depth_ref[3 * a + c : 3 * a + c + 1, :]
            mixed = mixed + coarse[first + a : first + a + count, c : c + HALF] * tap
    centre = mixed - jnp.mean(mixed, axis=-1, keepdims=True)
    variance = jnp.mean(centre * centre, axis=-1, keepdims=True)
    return (centre * lax.rsqrt(variance + 1e-05) * gain_ref[...]).astype(jnp.bfloat16)


def inner_kernel(
    tile_ref,
    west_ref,
    east_ref,
    weight_ref,
    bias_ref,
    depth_ref,
    gain_ref,
    upper_ref,
    lower_ref,
    out_ref,
    even,
    odd,
    coarse,
):
    tile, west, east = (r[...].astype(jnp.float32) for r in (tile_ref, west_ref, east_ref))
    put_rows(even, odd, slice(0, TLAT), tile, west, east)
    coarse[...] = strided_rows(even, odd, range(1, TLAT - 2, 2), weight_ref, bias_ref)
    upper_ref[...] = coarse[0:2]
    lower_ref[...] = coarse[ROWS - 3 : ROWS - 1]
    out_ref[...] = finished(coarse, 0, ROWS - 3, depth_ref, gain_ref)


def inner(*arrays):
    pair = jax.ShapeDtypeStruct((2, SPAN, D), jnp.float32)
    return pl.pallas_call(
        inner_kernel,
        in_specs=[VMEM] * len(arrays),
        out_specs=[VMEM] * 3,
        out_shape=[pair, pair, jax.ShapeDtypeStruct((ROWS - 3, HALF, D), jnp.bfloat16)],
        scratch_shapes=[
            pltpu.VMEM((TLAT, SPAN, D), jnp.float32),
            pltpu.VMEM((TLAT, SPAN + 8, D), jnp.float32),
            pltpu.VMEM((ROWS - 1, SPAN, D), jnp.float32),
        ],
        compiler_params=pltpu.CompilerParams(vmem_limit_bytes=16 << 20),
        cost_estimate=pl.CostEstimate(
            flops=2 * 7 * SPAN * 9 * D * D, bytes_accessed=2 << 20, transcendentals=0
        ),
    )(*arrays)


def outer_kernel(
    place_ref,
    upper_ref,
    lower_ref,
    done_ref,
    tile_ref,
    west_ref,
    east_ref,
    pair_ref,
    other_ref,
    weight_ref,
    bias_ref,
    depth_ref,
    gain_ref,
    out_hbm,
    even,
    odd,
    coarse,
    top,
    bottom,
    sent,
):
    inner_copy = pltpu.make_async_copy(done_ref, out_hbm.at[2 : ROWS - 1], sent.at[0])
    inner_copy.start()
    paired, other = (r[...].astype(jnp.float32) for r in (pair_ref, other_ref))
    lower, above, below = (place_ref[i : i + 1] for i in range(3))
    upper = 1.0 - lower
    north = paired * (lower * above) + other * (upper * above)
    south = paired * upper + other * lower
    for at, source, rows in ((0, north, slice(0, 3)), (6, south, slice(0, 2))):
        part = source[rows]
        put_rows(
            even,
            odd,
            slice(at, at + rows.stop),
            part[:, :TLON],
            part[:, TLON : TLON + 3],
            part[:, TLON + 3 :],
        )
    for at, rows in ((3, slice(0, 2)), (5, slice(TLAT - 1, TLAT))):
        put_rows(
            even,
            odd,
            slice(at, at + rows.stop - rows.start),
            tile_ref[rows].astype(jnp.float32),
            west_ref[rows].astype(jnp.float32),
            east_ref[rows].astype(jnp.float32),
        )
    edge = strided_rows(even, odd, (0, 2, 5), weight_ref, bias_ref)
    coarse[0] = edge[0] * above
    coarse[1] = edge[1]
    coarse[2:4] = upper_ref[...]
    coarse[4:6] = lower_ref[...]
    coarse[6] = edge[2] * below
    top[...] = finished(coarse, 0, 2, depth_ref, gain_ref)
    bottom[...] = finished(coarse, 4, 1, depth_ref, gain_ref)
    copies = [
        inner_copy,
        pltpu.make_async_copy(top, out_hbm.at[0:2], sent.at[1]),
        pltpu.make_async_copy(bottom, out_hbm.at[ROWS - 1 : ROWS], sent.at[2]),
    ]
    for copy in copies[1:]:
        copy.start()
    for copy in copies:
        copy.wait()


def outer(*arrays):
    return pl.pallas_call(
        outer_kernel,
        in_specs=[VMEM] * len(arrays),
        out_specs=ANY,
        out_shape=jax.ShapeDtypeStruct((ROWS, HALF, D), jnp.bfloat16),
        scratch_shapes=[
            pltpu.VMEM((8, SPAN, D), jnp.float32),
            pltpu.VMEM((8, SPAN + 8, D), jnp.float32),
            pltpu.VMEM((7, SPAN, D), jnp.float32),
            pltpu.VMEM((2, HALF, D), jnp.bfloat16),
            pltpu.VMEM((1, HALF, D), jnp.bfloat16),
            pltpu.SemaphoreType.DMA((3,)),
        ],
        compiler_params=pltpu.CompilerParams(vmem_limit_bytes=16 << 20),
    )(*arrays)


def on_device(
    obs_values,
    obs_offset,
    obs_cell,
    obs_slot,
    obs_count,
    embed_weight,
    embed_bias,
    stride_weight,
    stride_bias,
    depth_weight,
    norm_gain,
):
    lon_count, lat_count = lax.axis_size("lon"), lax.axis_size("lat")
    lat = lax.axis_index("lat")
    packed = pack(obs_values, obs_offset, obs_cell, obs_slot, obs_count)
    arrived = lax.all_to_all(packed, ("lon", "lat"), split_axis=0, concat_axis=0, tiled=True)
    tile, last, first = scatter(arrived, embed_weight, embed_bias)
    ring = [(i, (i + 1) % lon_count) for i in range(lon_count)]
    west = lax.ppermute(last, "lon", ring)
    east = lax.ppermute(first, "lon", [(j, i) for i, j in ring])
    weight, bias = stride_weight.reshape(9 * D, D), stride_bias.reshape(1, D)
    framed = jnp.concatenate([tile, west, east], axis=1)
    top, bottom = framed[:3], framed[TLAT - 3 :]
    lower = lat % 2 == 1
    pairs = [(i, i + 1) for i in range(0, lat_count - 1, 2)]
    others = [(i, (i + 1) % lat_count) for i in range(1, lat_count, 2)]
    other = lax.ppermute(
        jnp.where(lower, bottom, top), "lat", others + [(j, i) for i, j in others]
    )
    paired = lax.ppermute(
        jnp.where(lower, top, bottom), "lat", pairs + [(j, i) for i, j in pairs]
    )
    gain = norm_gain.reshape(1, D)
    place = jnp.stack([lower, lat > 0, lat < lat_count - 1]).astype(jnp.float32)
    place = jnp.broadcast_to(place[:, None], (3, D))
    inside = inner(tile, west, east, weight, bias, depth_weight, gain)
    return outer(
        place, *inside, tile, west, east, paired, other, weight, bias, depth_weight, gain
    )


def solution(mesh):
    placed = (
        P(("lon", "lat"), None, None),
        P(("lon", "lat"), None, None),
        P(("lon", "lat"), None),
        P(("lon", "lat"), None),
        P(("lon", "lat"), None),
        P(),
        P(),
        P(),
        P(),
        P(),
        P(),
    )
    return jax.shard_map(
        on_device, mesh=mesh, in_specs=placed, out_specs=P("lat", "lon", None), check_vma=False
    )
```

time: 69.6 us -> 42.9 us (0.62)
  the two profiles are of different devices: /device:TPU:1 before, /device:TPU:0 now
where the time goes in v2:
time: 42.9 us; the launch traced here: 42.7 us
  blocking collectives  24 us (56%)
  Pallas kernels  8.63 us (20%)
  starting transfers between devices  6.11 us (14%)
  waiting for transfers between devices  3.57 us (8%)
    all_to_all x1, blocking collectives, on_device(): lax.all_to_all(packed, ('lon', 'lat'), split_axis=0, concat_axis=0, tiled...  24 us
    pallas_call x1, Pallas kernels, scatter(): pl.pallas_call(scatter_kernel, in_specs=[VMEM] * 3, out_specs=[VMEM] * 3,...  4.58 us
    ppermute x1, starting transfers between devices, on_device(): east = lax.ppermute(first, 'lon', [(j, i) for i, j in ring])  3.39 us
    pallas_call x1, Pallas kernels, pack(): pl.pallas_call(pack_kernel, in_specs=[ANY] * len(arrays), out_specs=ANY,...  2.09 us
    ppermute x1, waiting for transfers between devices, on_device(): lax.ppermute(jnp.where(lower, bottom, top), 'lat', others + [(j, i) for i...  1.68 us
    ppermute x1, waiting for transfers between devices, on_device(): east = lax.ppermute(first, 'lon', [(j, i) for i, j in ring])  1.44 us
    ppermute x1, starting transfers between devices, on_device(): west = lax.ppermute(last, 'lon', ring)  1.39 us
    ppermute x1, starting transfers between devices, on_device(): lax.ppermute(jnp.where(lower, bottom, top), 'lat', others + [(j, i) for i...  1.27 us
  transfers between devices with their start and end apart: 4, of which 3 were waited for; matrix products, arithmetic and copies ran while one was open for 0% of the time, Pallas kernels for 2%

profile of v2, /device:TPU:0, one launch (start us, length us, event | category | flops | bytes accessed | tf_op | source)
XLA Modules:
  0.0 42.7 jit_solution(16993263480921119867)
XLA Ops:
  0.0 0.0 copy-start.1
  0.0 0.0 copy-start.5
  0.0 2.1 %shard_map.109 = bf16[32,72,128]{2,1,0:T(8,128)(2,1)} custom-call(s32[1,32]{1,0:T(1,128)} %count_hbm.1, bf16[31,32,256]{2,1,0:T(8,128)(2,1)} %bitcast.15, f32[32,2,256]{2,1,0:T(2,128)} %offset_hbm.1, s32[32,256]{1,0:T(8,128)} %cell_hbm.1, s32[32,256]{1,0:T(8,128)} %slot_hbm.1), custom_call_target="tpu_custom_call" | custom-call | tf_op jit(solution)/shard_map/pallas_call | solution.py:116
  2.1 0.0 copy-start
  2.1 0.0 copy-start.2
  2.1 0.0 copy-start.3
  2.1 0.0 copy-start.4
  2.1 24.0 %all_to_all.5.x_ref = bf16[32,72,128]{2,1,0:T(8,128)(2,1)S(1)} all-to-all(bf16[32,72,128]{2,1,0:T(8,128)(2,1)} %shard_map.109), channel_id=1, replica_groups=mesh['lon'=8,'lat'=4] {'lon','lat'}, dimensions={0} | all-to-all | bytes 1179648 | tf_op jit(solution)/shard_map/all_to_all | solution.py:405
  26.2 0.0 copy-done.1
  26.2 0.0 copy-done.5
  26.2 4.6 %shard_map.110 = (bf16[16,32,256]{2,1,0:T(8,128)(2,1)S(1)}, bf16[16,3,256]{2,1,0:T(4,128)(2,1)S(1)}, bf16[16,2,256]{2,1,0:T(2,128)(2,1)S(1)}) custom-call(bf16[32,72,128]{2,1,0:T(8,128)(2,1)S(1)} %all_to_all.5.x_ref, bf16[384,256]{1,0:T(8,128)(2,1)S(1)} %copy-done.1, f32[1,256]{1,0:T(1,128)S(1)} %bitcast.14), custom_call_target="tpu_custom_call" | custom-call | tf_op jit(solution)/shard_map/pallas_call | solution.py:214
  30.8 1.4 %collective-permute-start = (bf16[16,3,256]{2,1,0:T(4,128)(2,1)S(1)}, bf16[16,3,256]{2,1,0:T(4,128)(2,1)S(1)}, u32[]{:S(2)}, u32[]{:S(2)}) collective-permute-start(bf16[16,3,256]{2,1,0:T(4,128)(2,1)S(1)} %get-tuple-element.12), channel_id=1, source_target_pairs={{0,4},{4,8},{8,12},{12,16},{16,20},{20,24},{24,28},{28,0},{1,5},{5... | collective-permute-start | bytes 73736 | tf_op jit(solution)/shard_map/ppermute | solution.py:408
  32.2 3.4 %collective-permute-start.1 = (bf16[16,2,256]{2,1,0:T(2,128)(2,1)S(1)}, bf16[16,2,256]{2,1,0:T(2,128)(2,1)S(1)}, u32[]{:S(2)}, u32[]{:S(2)}) collective-permute-start(bf16[16,2,256]{2,1,0:T(2,128)(2,1)S(1)} %get-tuple-element.13), channel_id=1, source_target_pairs={{4,0},{8,4},{12,8},{16,12},{20,16},{24,20},{28,24},{0,28},{5,1},{9... | collective-permute-start | bytes 49160 | tf_op jit(solution)/shard_map/ppermute | solution.py:409
  35.6 1.4 %collective-permute-done.1.east_ref = bf16[16,2,256]{2,1,0:T(2,128)(2,1)S(1)} collective-permute-done((bf16[16,2,256]{2,1,0:T(2,128)(2,1)S(1)}, bf16[16,2,256]{2,1,0:T(2,128)(2,1)S(1)}, u32[]{:S(2)}, u32[]{:S(2)}) %collective-permute-start.1) | collective-permute-done | bytes 16416 | tf_op jit(solution)/shard_map/ppermute | solution.py:409
  37.0 0.4 %collective-permute-done.west_ref = bf16[16,3,256]{2,1,0:T(4,128)(2,1)S(1)} collective-permute-done((bf16[16,3,256]{2,1,0:T(4,128)(2,1)S(1)}, bf16[16,3,256]{2,1,0:T(4,128)(2,1)S(1)}, u32[]{:S(2)}, u32[]{:S(2)}) %collective-permute-start) | collective-permute-done | bytes 24608 | tf_op jit(solution)/shard_map/ppermute | solution.py:408
  37.5 0.1 collective-permute-start.2
  37.6 1.3 %collective-permute-start.3 = (bf16[3,37,256]{2,1,0:T(8,128)(2,1)S(1)}, bf16[3,37,256]{2,1,0:T(8,128)(2,1)S(1)}, u32[]{:S(2)}, u32[]{:S(2)}) collective-permute-start(bf16[3,37,256]{2,1,0:T(8,128)(2,1)S(1)} %get-tuple-element.17), channel_id=1, source_target_pairs={{1,2},{3,0},{2,1},{0,3},{5,6},{7,4},{6,5},{4,7},{9,10},{11,8},{10,... | collective-permute-start | bytes 170504 | tf_op jit(solution)/shard_map/ppermute | solution.py:416
  38.9 0.1 add_convert_fusion
  38.9 0.0 copy-done
  38.9 0.0 copy-done.2
  38.9 0.0 copy-done.3
  38.9 0.0 copy-done.4
  39.0 0.7 %shard_map.111 = (f32[2,24,256]{2,1,0:T(8,128)S(1)}, f32[2,24,256]{2,1,0:T(8,128)S(1)}, bf16[5,16,256]{2,1,0:T(8,128)(2,1)S(1)}) custom-call(bf16[16,32,256]{2,1,0:T(8,128)(2,1)S(1)} %get-tuple-element.11.tile_ref, bf16[16,3,256]{2,1,0:T(4,128)(2,1)S(1)} %collective-permute-done.west_ref, bf16[16,2,256]{2,1,0:T(2,128)(2,1)S(1)} %collective-permute-done.1.east_ref, ...), custom_call_target="tpu_custom_call" | custom-call | flops 198180864 | bytes 2097152 | tf_op jit(solution)/shard_map/pallas_call | solution.py:287
  39.7 0.0 collective-permute-done.2.pair_ref
  39.7 1.7 %collective-permute-done.3.other_ref = bf16[3,37,256]{2,1,0:T(8,128)(2,1)S(1)} collective-permute-done((bf16[3,37,256]{2,1,0:T(8,128)(2,1)S(1)}, bf16[3,37,256]{2,1,0:T(8,128)(2,1)S(1)}, u32[]{:S(2)}, u32[]{:S(2)}) %collective-permute-start.3) | collective-permute-done | bytes 56864 | tf_op jit(solution)/shard_map/ppermute | solution.py:416
  41.4 0.1 broadcast_in_dim.2.place_ref
  41.5 1.2 %shard_map.112 = bf16[8,16,256]{2,1,0:T(8,128)(2,1)} custom-call(f32[3,256]{1,0:T(4,128)S(1)} %broadcast_in_dim.2.place_ref, f32[2,24,256]{2,1,0:T(8,128)S(1)} %get-tuple-element.14.upper_ref, f32[2,24,256]{2,1,0:T(8,128)S(1)} %get-tuple-element.15.lower_ref, bf16[5,16,256]{2,1,0:T(8,128)(2,1)S(1)} %get-tuple-element.16.done_ref, ...), custom_call_target="tpu_custom_call" | custom-call | tf_op jit(solution)/shard_map/pallas_call | solution.py:372
  (2 shorter events, 0.0 us)
Async XLA Ops:
  0.0 26.2 %copy-start.1 = (bf16[384,256]{1,0:T(8,128)(2,1)S(1)}, bf16[384,256]{1,0:T(8,128)(2,1)}, u32[]{:S(2)}) copy-start(bf16[384,256]{1,0:T(8,128)(2,1)} %weight_ref.1) | copy-start | bytes 589828
  0.0 26.2 %copy-start.5 = (f32[256]{0:T(256)S(1)}, f32[256]{0:T(256)}, u32[]{:S(2)}) copy-start(f32[256]{0:T(256)} %param.17) | copy-start | bytes 3076
  2.1 36.8 %copy-start = (bf16[9,256,256]{2,1,0:T(8,128)(2,1)S(1)}, bf16[9,256,256]{2,1,0:T(8,128)(2,1)}, u32[]{:S(2)}) copy-start(bf16[9,256,256]{2,1,0:T(8,128)(2,1)} %param.18) | copy-start | bytes 3538948
  2.1 36.8 %copy-start.2 = (f32[9,256]{1,0:T(8,128)S(1)}, f32[9,256]{1,0:T(8,128)}, u32[]{:S(2)}) copy-start(f32[9,256]{1,0:T(8,128)} %depth_ref.3) | copy-start | bytes 27652
  2.1 36.8 %copy-start.3 = (f32[256]{0:T(256)S(1)}, f32[256]{0:T(256)}, u32[]{:S(2)}) copy-start(f32[256]{0:T(256)} %param.19) | copy-start | bytes 3076
  2.1 36.8 %copy-start.4 = (f32[256]{0:T(256)S(1)}, f32[256]{0:T(256)}, u32[]{:S(2)}) copy-start(f32[256]{0:T(256)} %param.21) | copy-start | bytes 3076
  30.8 6.7 %collective-permute-start = (bf16[16,3,256]{2,1,0:T(4,128)(2,1)S(1)}, bf16[16,3,256]{2,1,0:T(4,128)(2,1)S(1)}, u32[]{:S(2)}, u32[]{:S(2)}) collective-permute-start(bf16[16,3,256]{2,1,0:T(4,128)(2,1)S(1)} %get-tuple-element.12), channel_id=1, source_target_pairs={{0,4},{4,8},{8,12},{12,16},{16,20},{20,24},{24,28},{28,0},{1,5},{5... | collective-permute-start | bytes 73736 | tf_op jit(solution)/shard_map/ppermute | solution.py:408
  32.2 4.8 %collective-permute-start.1 = (bf16[16,2,256]{2,1,0:T(2,128)(2,1)S(1)}, bf16[16,2,256]{2,1,0:T(2,128)(2,1)S(1)}, u32[]{:S(2)}, u32[]{:S(2)}) collective-permute-start(bf16[16,2,256]{2,1,0:T(2,128)(2,1)S(1)} %get-tuple-element.13), channel_id=1, source_target_pairs={{4,0},{8,4},{12,8},{16,12},{20,16},{24,20},{28,24},{0,28},{5,1},{9... | collective-permute-start | bytes 49160 | tf_op jit(solution)/shard_map/ppermute | solution.py:409
  37.5 2.2 %collective-permute-start.2 = (bf16[3,37,256]{2,1,0:T(8,128)(2,1)S(1)}, bf16[3,37,256]{2,1,0:T(8,128)(2,1)S(1)}, u32[]{:S(2)}, u32[]{:S(2)}) collective-permute-start(bf16[3,37,256]{2,1,0:T(8,128)(2,1)S(1)} %broadcast_select_fusion.1), channel_id=1, source_target_pairs={{0,1},{2,3},{1,0},{3,2},{4,5},{6,7},{5,4},{7,6},{8,9},{10,11},{9,8... | collective-permute-start | bytes 170504 | tf_op jit(solution)/shard_map/ppermute | solution.py:419
  37.6 3.8 %collective-permute-start.3 = (bf16[3,37,256]{2,1,0:T(8,128)(2,1)S(1)}, bf16[3,37,256]{2,1,0:T(8,128)(2,1)S(1)}, u32[]{:S(2)}, u32[]{:S(2)}) collective-permute-start(bf16[3,37,256]{2,1,0:T(8,128)(2,1)S(1)} %get-tuple-element.17), channel_id=1, source_target_pairs={{1,2},{3,0},{2,1},{0,3},{5,6},{7,4},{6,5},{4,7},{9,10},{11,8},{10,... | collective-permute-start | bytes 170504 | tf_op jit(solution)/shard_map/ppermute | solution.py:416

commit v3 on v2

--- a/solution.py
+++ b/solution.py
@@ -18,7 +18,8 @@
 ROWS = TLAT // 2
 LANES = 128
 GROUP = 16
-CHUNK = 8
+TILE = 4
+CHUNK = 32
 SPAN = 24
 FRAME = TLON + 5
 
@@ -45,7 +46,8 @@
 ):
     tiles, capacity = cell.shape
     halves = capacity // LANES
-    stride = halves * WIDTH + 8
+    used = out.shape[1] * TILE
+    stride = rows.shape[0] // tiles
     groups = tiles // GROUP
 
     def at(j):
@@ -72,12 +74,13 @@
     dy, dx = offset[:, 0, :], offset[:, 1, :]
     weight = jnp.where(position < counts, jnp.exp(-2.0 * (dy * dy + dx * dx)), 0.0)
     column = cell[...] % TLON
+    pair = column // 2
+    middle = (pair >= ROWS // 2) & (pair < 3 * ROWS // 2)
+    within = pair - jnp.where(pair < ROWS // 2, 0, jnp.where(middle, ROWS // 2, ROWS))
     codes = (
-        slot[...].astype(jnp.float32),
-        (cell[...] // TLON).astype(jnp.float32),
-        ((column % 2) * HALF + column // 2).astype(jnp.float32),
-    )
-    zero = jnp.zeros((GROUP, LANES), jnp.float32)
+        (slot[...] * TLAT + cell[...] // TLON).astype(jnp.float32),
+        (jnp.where(middle, HALF, 0) + (column % 2) * ROWS + within).astype(jnp.float32),
+    )
     base = halves * WIDTH
     sends = []
     for j in range(groups):
@@ -92,15 +95,15 @@
             put(h * WIDTH + OBS_VARS, weight[own], h)
             for i, code in enumerate(codes):
                 put(base + i * halves + h, code[own], h)
-        for r in range(len(codes) * halves, 8):
-            put(base + r, zero, 0)
         large[j].wait()
         for k in range(OBS_VARS):
             scaled = values[k, own, :].astype(jnp.float32) * weight[own]
             for h in range(halves):
                 put(h * WIDTH + k, scaled, h)
         for d in range(j * GROUP, (j + 1) * GROUP):
-            out[d] = rows[d * stride : (d + 1) * stride, :].astype(jnp.bfloat16)
+            for i in range(used // TILE):
+                first = d * stride + i * TILE
+                out[d, i] = rows[first : first + TILE, :].astype(jnp.bfloat16)
         sends.append(pltpu.make_async_copy(out.at[at(j)], out_hbm.at[at(j)], sent.at[j]))
         sends[-1].start()
     for copy in sends:
@@ -109,9 +112,10 @@
 
 def pack(obs_values, obs_offset, obs_cell, obs_slot, obs_count):
     tiles, _, capacity = obs_values.shape
-    stride = capacity // LANES * WIDTH + 8
+    used = capacity // LANES * (WIDTH + 2)
+    stride = -(-used // 8) * 8
     values = jnp.transpose(obs_values, (1, 0, 2))
-    shape = (tiles, stride, LANES)
+    shape = (tiles, used // TILE, TILE, LANES)
     arrays = (obs_count, values, obs_offset, obs_cell, obs_slot)
     return pl.pallas_call(
         pack_kernel,
@@ -129,100 +133,102 @@
     )(*arrays)
 
 
-def scatter_kernel(x_ref, weight_ref, bias_ref, tile_ref, last_ref, first_ref, hot, spread, total):
-    tiles, rows, _ = x_ref.shape
-    halves = rows // WIDTH
-    iota = lax.broadcasted_iota(jnp.int32, (TLON, LANES), 0).astype(jnp.float32)
-    zero = jnp.zeros((TLON, LANES), jnp.bfloat16)
-
-    def part(source, first):
-        for g in range(CHUNK):
-            codes = x_ref[source + g, halves * WIDTH :, :].astype(jnp.float32)
-            for h in range(halves):
-                at = first + (halves * g + h) * LANES
-                lanes = slice(at, at + LANES)
-                value = x_ref[source + g, h * WIDTH : (h + 1) * WIDTH, :]
-                slot = codes[h : h + 1]
-                row = codes[halves + h : halves + h + 1]
-                column = codes[2 * halves + h : 2 * halves + h + 1]
-                lower = jnp.where(row >= ROWS, 1.0, 0.0)
-                group = jnp.broadcast_to(slot + lower * SLOTS, (WIDTH, LANES))
-                within = jnp.broadcast_to(row - lower * ROWS, (TLON, LANES))
-                group = group.astype(jnp.bfloat16)
-                within = within.astype(jnp.bfloat16)
-                column = jnp.where(iota == column, 1.0, 0.0).astype(jnp.bfloat16)
-                for r in range(ROWS):
-                    hot[r * TLON : (r + 1) * TLON, lanes] = jnp.where(
-                        within == jnp.bfloat16(r), column, zero
-                    )
-                for s in range(2 * SLOTS):
-                    spread[s * WIDTH : (s + 1) * WIDTH, lanes] = jnp.where(
-                        group == jnp.bfloat16(s), value, zero
-                    )
-        lanes = slice(first, first + CHUNK * halves * LANES)
+def embedded_cells(x_ref, weight_ref, bias_ref, total, middle):
+    tiles, blocks, _, _ = x_ref.shape
+    halves = blocks * TILE // WIDTH
+    step = WIDTH // TILE
+    iota = lax.broadcasted_iota(jnp.int32, (HALF, LANES), 0).astype(jnp.float32)
+    none = jnp.zeros((HALF, LANES), jnp.bfloat16)
+    zero = jnp.zeros((WIDTH, LANES), jnp.bfloat16)
+
+    def operands(source):
+        codes = x_ref[source, halves * step].astype(jnp.float32)
+        spread, hot = [], []
+        for h in range(halves):
+            value = x_ref[source, h * step : (h + 1) * step].reshape(WIDTH, LANES)
+            code = codes[h : h + 1]
+            slot = jnp.floor(code * (1.0 / TLAT))
+            row = jnp.broadcast_to(code - slot * TLAT, (HALF, LANES)).astype(jnp.bfloat16)
+            column = codes[halves + h : halves + h + 1]
+            group = jnp.where(column >= HALF, 1.0, 0.0)
+            slot = jnp.where(group == middle, slot, SLOTS)
+            slot = jnp.broadcast_to(slot, (WIDTH, LANES)).astype(jnp.bfloat16)
+            column = jnp.where(iota == column - group * HALF, 1.0, 0.0).astype(jnp.bfloat16)
+            by_slot = [jnp.where(slot == jnp.bfloat16(s), value, zero) for s in range(SLOTS)]
+            by_row = [jnp.where(row == jnp.bfloat16(r), column, none) for r in range(TLAT)]
+            spread.append(jnp.concatenate(by_slot, axis=0))
+            hot.append(jnp.concatenate(by_row, axis=0))
+        return jnp.concatenate(spread, axis=1), jnp.concatenate(hot, axis=1)
+
+    def summed(first, count):
+        spread, hot = zip(*(operands(first + g) for g in range(count)))
         return lax.dot_general(
-            spread[:, lanes],
-            hot[:, lanes],
+            jnp.concatenate(spread, axis=1),
+            jnp.concatenate(hot, axis=1),
             (((1,), (1,)), ((), ())),
             preferred_element_type=jnp.float32,
         )
 
-    def summed(start):
-        chunks = range(hot.shape[1] // (CHUNK * halves * LANES))
-        return functools.reduce(
-            jnp.add, [part(start + c * CHUNK, c * CHUNK * halves * LANES) for c in chunks]
-        )
-
-    sources = hot.shape[1] // (halves * LANES)
-    if tiles == sources:
-        total[...] = summed(0)
-    else:
-        total[...] = jnp.zeros(total.shape, jnp.float32)
-
-        @pl.loop(0, tiles // sources)
-        def _(step):
-            total[...] += summed(step * sources)
-
-    for half in range(2):
-        groups = []
-        for s in range(SLOTS):
-            first = half * BINS + s * WIDTH
-            block = total[first : first + WIDTH, :]
-            inverse = 1.0 / (1.0 + block[OBS_VARS:WIDTH, :])
-            channel = lax.broadcasted_iota(jnp.int32, block.shape, 0)
-            ratio = jnp.where(channel == OBS_VARS, block, block * inverse)
-            groups.append(ratio.astype(jnp.bfloat16))
-        projected = lax.dot_general(
-            jnp.concatenate(groups, axis=0),
-            weight_ref[...],
-            (((0,), (0,)), ((), ())),
-            preferred_element_type=jnp.float32,
-        )
-        embedded = jax.nn.gelu(projected + bias_ref[...]).reshape(ROWS, TLON, D)
-        at = slice(half * ROWS, (half + 1) * ROWS)
-        tile_ref[at] = embedded.astype(jnp.bfloat16)
-        last = [embedded[:, c : c + 1] for c in (TLON - 2, HALF - 1, TLON - 1)]
-        first = [embedded[:, c : c + 1] for c in (0, HALF)]
-        last_ref[at] = jnp.concatenate(last, axis=1).astype(jnp.bfloat16)
-        first_ref[at] = jnp.concatenate(first, axis=1).astype(jnp.bfloat16)
-
-
-def scatter(arrived, embed_weight, embed_bias):
-    tiles, rows, _ = arrived.shape
-    depth = min(tiles, 32) * (rows // WIDTH) * LANES
-    shapes = [(TLAT, TLON, D), (TLAT, 3, D), (TLAT, 2, D)]
+    count = min(tiles, CHUNK)
+    total[...] = summed(0, count)
+
+    @pl.loop(1, tiles // count)
+    def _(step):
+        total[...] += summed(step * count, count)
+
+    groups = []
+    for s in range(SLOTS):
+        block = total[s * WIDTH : (s + 1) * WIDTH, :]
+        inverse = 1.0 / (1.0 + block[OBS_VARS:WIDTH, :])
+        channel = lax.broadcasted_iota(jnp.int32, block.shape, 0)
+        ratio = jnp.where(channel == OBS_VARS, block, block * inverse)
+        groups.append(ratio.astype(jnp.bfloat16))
+    projected = lax.dot_general(
+        jnp.concatenate(groups, axis=0),
+        weight_ref[...],
+        (((0,), (0,)), ((), ())),
+        preferred_element_type=jnp.float32,
+    )
+    return jax.nn.gelu(projected + bias_ref[...]).reshape(TLAT, HALF, D)
+
+
+def sides_kernel(x_ref, weight_ref, bias_ref, sides_ref, last_ref, first_ref, total):
+    sides = embedded_cells(x_ref, weight_ref, bias_ref, total, 0.0)
+    sides_ref[...] = sides
+    last = [sides[:, c : c + 1] for c in (HALF - 2, ROWS - 1, HALF - 1)]
+    first = [sides[:, c : c + 1] for c in (0, ROWS)]
+    last_ref[...] = jnp.concatenate(last, axis=1).astype(jnp.bfloat16)
+    first_ref[...] = jnp.concatenate(first, axis=1).astype(jnp.bfloat16)
+
+
+def middle_kernel(x_ref, weight_ref, bias_ref, sides_ref, tile_ref, total):
+    middle = embedded_cells(x_ref, weight_ref, bias_ref, total, 1.0)
+    sides = sides_ref[...]
+    quarter = ROWS // 2
+    whole = []
+    for parity in range(2):
+        at = parity * ROWS
+        whole += [
+            sides[:, at : at + quarter],
+            middle[:, at : at + ROWS],
+            sides[:, at + quarter : at + ROWS],
+        ]
+    tile_ref[...] = jnp.concatenate(whole, axis=1).astype(jnp.bfloat16)
+
+
+def scatter(kernel, arrived, embed_weight, embed_bias, *more, outs):
+    tiles = arrived.shape[0]
     return pl.pallas_call(
-        scatter_kernel,
-        in_specs=[VMEM] * 3,
-        out_specs=[VMEM] * 3,
-        out_shape=[jax.ShapeDtypeStruct(shape, jnp.bfloat16) for shape in shapes],
-        scratch_shapes=[
-            pltpu.VMEM((ROWS * TLON, depth), jnp.bfloat16),
-            pltpu.VMEM((2 * BINS, depth), jnp.bfloat16),
-            pltpu.VMEM((2 * BINS, ROWS * TLON), jnp.float32),
-        ],
+        kernel,
+        in_specs=[VMEM] * (3 + len(more)),
+        out_specs=[VMEM] * len(outs),
+        out_shape=outs,
+        scratch_shapes=[pltpu.VMEM((BINS, TLAT * HALF), jnp.float32)],
         compiler_params=pltpu.CompilerParams(vmem_limit_bytes=32 << 20),
-    )(arrived, embed_weight, embed_bias.reshape(1, D))
+        cost_estimate=pl.CostEstimate(
+            flops=2 * tiles * 256 * BINS * TLAT * HALF, bytes_accessed=4 << 20, transcendentals=0
+        ),
+    )(arrived, embed_weight, embed_bias.reshape(1, D), *more)
 
 
 def put_rows(even, odd, rows, tile, west, east):
@@ -403,10 +409,16 @@
     lat = lax.axis_index("lat")
     packed = pack(obs_values, obs_offset, obs_cell, obs_slot, obs_count)
     arrived = lax.all_to_all(packed, ("lon", "lat"), split_axis=0, concat_axis=0, tiled=True)
-    tile, last, first = scatter(arrived, embed_weight, embed_bias)
+    held = jax.ShapeDtypeStruct((TLAT, HALF, D), jnp.float32)
+    edges = [jax.ShapeDtypeStruct((TLAT, n, D), jnp.bfloat16) for n in (3, 2)]
+    sides, last, first = scatter(
+        sides_kernel, arrived, embed_weight, embed_bias, outs=[held] + edges
+    )
     ring = [(i, (i + 1) % lon_count) for i in range(lon_count)]
     west = lax.ppermute(last, "lon", ring)
     east = lax.ppermute(first, "lon", [(j, i) for i, j in ring])
+    cells = jax.ShapeDtypeStruct((TLAT, TLON, D), jnp.bfloat16)
+    (tile,) = scatter(middle_kernel, arrived, embed_weight, embed_bias, sides, outs=[cells])
     weight, bias = stride_weight.reshape(9 * D, D), stride_bias.reshape(1, D)
     framed = jnp.concatenate([tile, west, east], axis=1)
     top, bottom = framed[:3], framed[TLAT - 3 :]

time: 42.9 us -> 40.4 us (0.942)
  blocking collectives: 24 us -> 0 us
  waiting for transfers between devices: 3.57 us -> 17.9 us
  starting transfers between devices: 6.11 us -> 13.3 us
    all_to_all x1 -> x0, blocking collectives: 24 us -> none  [on_device(): lax.all_to_all(packed, ('lon', 'lat'), split_axis=0, concat_axis=0, tiled...]
    all_to_all x0 -> x1, waiting for transfers between devices: none -> 16.1 us  [on_device(): lax.all_to_all(packed, ('lon', 'lat'), split_axis=0, concat_axis=0, tiled...]
    all_to_all x0 -> x1, starting transfers between devices: none -> 7.3 us  [on_device(): lax.all_to_all(packed, ('lon', 'lat'), split_axis=0, concat_axis=0, tiled...]
    ppermute x1, waiting for transfers between devices: 1.44 us -> 0.01 us  [on_device(): east = lax.ppermute(first, 'lon', [(j, i) for i, j in ring])]
    ppermute x1, waiting for transfers between devices: 0.44 us -> 0.01 us  [on_device(): west = lax.ppermute(last, 'lon', ring)]
    pallas_call x1 -> x2, Pallas kernels: 4.58 us -> 4.48 us  [scatter(): pl.pallas_call(kernel, in_specs=[VMEM] * (3 + len(more)), out_specs=[VMEM...]
  transfers between devices with their start and end apart: 4 -> 5, of which waited for: 3 -> 2; matrix products, arithmetic and copies ran while one was open for 0% -> 0% of each run, Pallas kernels for 2% -> 7%
where the time goes in v3:
time: 40.4 us; the launch traced here: 40.2 us
  waiting for transfers between devices  17.9 us (44%)
  starting transfers between devices  13.3 us (33%)
  Pallas kernels  8.65 us (21%)
    all_to_all x1, waiting for transfers between devices, on_device(): lax.all_to_all(packed, ('lon', 'lat'), split_axis=0, concat_axis=0, tiled...  16.1 us
    all_to_all x1, starting transfers between devices, on_device(): lax.all_to_all(packed, ('lon', 'lat'), split_axis=0, concat_axis=0, tiled...  7.3 us
    pallas_call x2, Pallas kernels, scatter(): pl.pallas_call(kernel, in_specs=[VMEM] * (3 + len(more)), out_specs=[VMEM...  4.48 us
    ppermute x1, starting transfers between devices, on_device(): east = lax.ppermute(first, 'lon', [(j, i) for i, j in ring])  3.44 us
    pallas_call x1, Pallas kernels, pack(): pl.pallas_call(pack_kernel, in_specs=[ANY] * len(arrays), out_specs=ANY,...  2.22 us
    ppermute x1, waiting for transfers between devices, on_device(): lax.ppermute(jnp.where(lower, bottom, top), 'lat', others + [(j, i) for i...  1.79 us
    ppermute x1, starting transfers between devices, on_device(): west = lax.ppermute(last, 'lon', ring)  1.34 us
    pallas_call x1, Pallas kernels, outer(): pl.pallas_call(outer_kernel, in_specs=[VMEM] * len(arrays), out_specs=ANY...  1.23 us
  transfers between devices with their start and end apart: 5, of which 2 were waited for; matrix products, arithmetic and copies ran while one was open for 0% of the time, Pallas kernels for 7%

profile of v3, /device:TPU:0, one launch (start us, length us, event | category | flops | bytes accessed | tf_op | source)
XLA Modules:
  0.0 40.2 jit_solution(17495621373391331442)
XLA Ops:
  0.0 0.0 copy-start.5
  0.0 0.0 copy-start.4
  0.0 2.2 %shard_map.109 = bf16[32,17,4,128]{3,2,1,0:T(4,128)(2,1)} custom-call(s32[1,32]{1,0:T(1,128)} %count_hbm.1, bf16[31,32,256]{2,1,0:T(8,128)(2,1)} %bitcast.16, f32[32,2,256]{2,1,0:T(2,128)} %offset_hbm.1, s32[32,256]{1,0:T(8,128)} %cell_hbm.1, s32[32,256]{1,0:T(8,128)} %slot_hbm.1), custom_call_target="tpu_custom_call" | custom-call | tf_op jit(solution)/shard_map/pallas_call | solution.py:120
  2.2 7.3 %all-to-all-start = ((bf16[32,17,4,128]{3,2,1,0:T(4,128)(2,1)}), bf16[32,17,4,128]{3,2,1,0:T(4,128)(2,1)S(1)}, u32[]{:S(2)}, u32[]{:S(2)}) async-start(bf16[32,17,4,128]{3,2,1,0:T(4,128)(2,1)} %shard_map.109), calls=%async_computation | async-start | bytes 1114112 | tf_op jit(solution)/shard_map/all_to_all | solution.py:411
  9.6 16.1 %all-to-all-done.x_ref = bf16[32,17,4,128]{3,2,1,0:T(4,128)(2,1)S(1)} async-done(((bf16[32,17,4,128]{3,2,1,0:T(4,128)(2,1)}), bf16[32,17,4,128]{3,2,1,0:T(4,128)(2,1)S(1)}, u32[]{:S(2)}, u32[]{:S(2)}) %all-to-all-start) | async-done | bytes 557088 | tf_op jit(solution)/shard_map/all_to_all | solution.py:411
  25.7 0.0 copy-done.5
  25.7 0.0 copy-done.4
  25.7 2.2 %shard_map.110 = (f32[16,16,256]{2,1,0:T(8,128)S(1)}, bf16[16,3,256]{2,1,0:T(4,128)(2,1)S(1)}, bf16[16,2,256]{2,1,0:T(2,128)(2,1)S(1)}) custom-call(bf16[32,17,4,128]{3,2,1,0:T(4,128)(2,1)S(1)} %all-to-all-done.x_ref, bf16[384,256]{1,0:T(8,128)(2,1)S(1)} %copy-done.4, f32[1,256]{1,0:T(1,128)S(1)} %bitcast.14), custom_call_target="tpu_custom_call" | custom-call | flops 1610612736 | bytes 4194304 | tf_op jit(solution)/shard_map/pallas_call | solution.py:221
  27.9 1.3 %collective-permute-start = (bf16[16,3,256]{2,1,0:T(4,128)(2,1)S(1)}, bf16[16,3,256]{2,1,0:T(4,128)(2,1)S(1)}, u32[]{:S(2)}, u32[]{:S(2)}) collective-permute-start(bf16[16,3,256]{2,1,0:T(4,128)(2,1)S(1)} %get-tuple-element.12), channel_id=1, source_target_pairs={{0,4},{4,8},{8,12},{12,16},{16,20},{20,24},{24,28},{28,0},{1,5},{5... | collective-permute-start | bytes 73736 | tf_op jit(solution)/shard_map/ppermute | solution.py:418
  29.3 3.4 %collective-permute-start.1 = (bf16[16,2,256]{2,1,0:T(2,128)(2,1)S(1)}, bf16[16,2,256]{2,1,0:T(2,128)(2,1)S(1)}, u32[]{:S(2)}, u32[]{:S(2)}) collective-permute-start(bf16[16,2,256]{2,1,0:T(2,128)(2,1)S(1)} %get-tuple-element.13), channel_id=1, source_target_pairs={{4,0},{8,4},{12,8},{16,12},{20,16},{24,20},{28,24},{0,28},{5,1},{9... | collective-permute-start | bytes 49160 | tf_op jit(solution)/shard_map/ppermute | solution.py:419
  32.7 0.0 copy-start
  32.7 0.0 copy-start.1
  32.7 0.0 copy-start.2
  32.7 0.0 copy-start.3
  32.7 2.2 %shard_map.111.tile_ref = bf16[16,32,256]{2,1,0:T(8,128)(2,1)S(1)} custom-call(bf16[32,17,4,128]{3,2,1,0:T(4,128)(2,1)S(1)} %all-to-all-done.x_ref, bf16[384,256]{1,0:T(8,128)(2,1)S(1)} %copy-done.4, f32[1,256]{1,0:T(1,128)S(1)} %bitcast.15, f32[16,16,256]{2,1,0:T(8,128)S(1)} %get-tuple-element.11.sides_ref), custom_call_target="tpu_custom_call" | custom-call | flops 1610612736 | bytes 4194304 | tf_op jit(solution)/shard_map/pallas_call | solution.py:221
  35.0 0.0 collective-permute-done.1.east_ref
  35.0 0.0 collective-permute-done.west_ref
  35.0 0.1 collective-permute-start.2
  35.1 1.2 %collective-permute-start.3 = (bf16[3,37,256]{2,1,0:T(8,128)(2,1)S(1)}, bf16[3,37,256]{2,1,0:T(8,128)(2,1)S(1)}, u32[]{:S(2)}, u32[]{:S(2)}) collective-permute-start(bf16[3,37,256]{2,1,0:T(8,128)(2,1)S(1)} %get-tuple-element.17), channel_id=1, source_target_pairs={{1,2},{3,0},{2,1},{0,3},{5,6},{7,4},{6,5},{4,7},{9,10},{11,8},{10,... | collective-permute-start | bytes 170504 | tf_op jit(solution)/shard_map/ppermute | solution.py:428
  36.3 0.1 add_convert_fusion
  36.4 0.0 copy-done
  36.4 0.0 copy-done.1
  36.4 0.0 copy-done.2
  36.4 0.0 copy-done.3
  36.4 0.7 %shard_map.112 = (f32[2,24,256]{2,1,0:T(8,128)S(1)}, f32[2,24,256]{2,1,0:T(8,128)S(1)}, bf16[5,16,256]{2,1,0:T(8,128)(2,1)S(1)}) custom-call(bf16[16,32,256]{2,1,0:T(8,128)(2,1)S(1)} %shard_map.111.tile_ref, bf16[16,3,256]{2,1,0:T(4,128)(2,1)S(1)} %collective-permute-done.west_ref, bf16[16,2,256]{2,1,0:T(2,128)(2,1)S(1)} %collective-permute-done.1.east_ref, ...), custom_call_target="tpu_custom_call" | custom-call | flops 198180864 | bytes 2097152 | tf_op jit(solution)/shard_map/pallas_call | solution.py:293
  37.1 0.0 collective-permute-done.2.pair_ref
  37.1 1.8 %collective-permute-done.3.other_ref = bf16[3,37,256]{2,1,0:T(8,128)(2,1)S(1)} collective-permute-done((bf16[3,37,256]{2,1,0:T(8,128)(2,1)S(1)}, bf16[3,37,256]{2,1,0:T(8,128)(2,1)S(1)}, u32[]{:S(2)}, u32[]{:S(2)}) %collective-permute-start.3) | collective-permute-done | bytes 56864 | tf_op jit(solution)/shard_map/ppermute | solution.py:428
  38.9 0.1 broadcast_in_dim.2.place_ref
  39.0 1.2 %shard_map.113 = bf16[8,16,256]{2,1,0:T(8,128)(2,1)} custom-call(f32[3,256]{1,0:T(4,128)S(1)} %broadcast_in_dim.2.place_ref, f32[2,24,256]{2,1,0:T(8,128)S(1)} %get-tuple-element.14.upper_ref, f32[2,24,256]{2,1,0:T(8,128)S(1)} %get-tuple-element.15.lower_ref, bf16[5,16,256]{2,1,0:T(8,128)(2,1)S(1)} %get-tuple-element.16.done_ref, ...), custom_call_target="tpu_custom_call" | custom-call | tf_op jit(solution)/shard_map/pallas_call | solution.py:378
  (2 shorter events, 0.0 us)
Async XLA Ops:
  0.0 25.7 %copy-start.5 = (f32[256]{0:T(256)S(1)}, f32[256]{0:T(256)}, u32[]{:S(2)}) copy-start(f32[256]{0:T(256)} %param.17) | copy-start | bytes 3076
  0.0 25.7 %copy-start.4 = (bf16[384,256]{1,0:T(8,128)(2,1)S(1)}, bf16[384,256]{1,0:T(8,128)(2,1)}, u32[]{:S(2)}) copy-start(bf16[384,256]{1,0:T(8,128)(2,1)} %weight_ref.3) | copy-start | bytes 589828
  2.2 23.4 %all-to-all-start = ((bf16[32,17,4,128]{3,2,1,0:T(4,128)(2,1)}), bf16[32,17,4,128]{3,2,1,0:T(4,128)(2,1)S(1)}, u32[]{:S(2)}, u32[]{:S(2)}) async-start(bf16[32,17,4,128]{3,2,1,0:T(4,128)(2,1)} %shard_map.109), calls=%async_computation | async-start | bytes 1114112 | tf_op jit(solution)/shard_map/all_to_all | solution.py:411
  27.9 7.0 %collective-permute-start = (bf16[16,3,256]{2,1,0:T(4,128)(2,1)S(1)}, bf16[16,3,256]{2,1,0:T(4,128)(2,1)S(1)}, u32[]{:S(2)}, u32[]{:S(2)}) collective-permute-start(bf16[16,3,256]{2,1,0:T(4,128)(2,1)S(1)} %get-tuple-element.12), channel_id=1, source_target_pairs={{0,4},{4,8},{8,12},{12,16},{16,20},{20,24},{24,28},{28,0},{1,5},{5... | collective-permute-start | bytes 73736 | tf_op jit(solution)/shard_map/ppermute | solution.py:418
  29.3 5.7 %collective-permute-start.1 = (bf16[16,2,256]{2,1,0:T(2,128)(2,1)S(1)}, bf16[16,2,256]{2,1,0:T(2,128)(2,1)S(1)}, u32[]{:S(2)}, u32[]{:S(2)}) collective-permute-start(bf16[16,2,256]{2,1,0:T(2,128)(2,1)S(1)} %get-tuple-element.13), channel_id=1, source_target_pairs={{4,0},{8,4},{12,8},{16,12},{20,16},{24,20},{28,24},{0,28},{5,1},{9... | collective-permute-start | bytes 49160 | tf_op jit(solution)/shard_map/ppermute | solution.py:419
  32.7 3.7 %copy-start = (bf16[9,256,256]{2,1,0:T(8,128)(2,1)S(1)}, bf16[9,256,256]{2,1,0:T(8,128)(2,1)}, u32[]{:S(2)}) copy-start(bf16[9,256,256]{2,1,0:T(8,128)(2,1)} %param.18) | copy-start | bytes 3538948
  32.7 3.7 %copy-start.1 = (f32[9,256]{1,0:T(8,128)S(1)}, f32[9,256]{1,0:T(8,128)}, u32[]{:S(2)}) copy-start(f32[9,256]{1,0:T(8,128)} %depth_ref.3) | copy-start | bytes 27652
  32.7 3.7 %copy-start.2 = (f32[256]{0:T(256)S(1)}, f32[256]{0:T(256)}, u32[]{:S(2)}) copy-start(f32[256]{0:T(256)} %param.19) | copy-start | bytes 3076
  32.7 3.7 %copy-start.3 = (f32[256]{0:T(256)S(1)}, f32[256]{0:T(256)}, u32[]{:S(2)}) copy-start(f32[256]{0:T(256)} %param.21) | copy-start | bytes 3076
  35.0 2.1 %collective-permute-start.2 = (bf16[3,37,256]{2,1,0:T(8,128)(2,1)S(1)}, bf16[3,37,256]{2,1,0:T(8,128)(2,1)S(1)}, u32[]{:S(2)}, u32[]{:S(2)}) collective-permute-start(bf16[3,37,256]{2,1,0:T(8,128)(2,1)S(1)} %broadcast_select_fusion.1), channel_id=1, source_target_pairs={{0,1},{2,3},{1,0},{3,2},{4,5},{6,7},{5,4},{7,6},{8,9},{10,11},{9,8... | collective-permute-start | bytes 170504 | tf_op jit(solution)/shard_map/ppermute | solution.py:431
  35.1 3.8 %collective-permute-start.3 = (bf16[3,37,256]{2,1,0:T(8,128)(2,1)S(1)}, bf16[3,37,256]{2,1,0:T(8,128)(2,1)S(1)}, u32[]{:S(2)}, u32[]{:S(2)}) collective-permute-start(bf16[3,37,256]{2,1,0:T(8,128)(2,1)S(1)} %get-tuple-element.17), channel_id=1, source_target_pairs={{1,2},{3,0},{2,1},{0,3},{5,6},{7,4},{6,5},{4,7},{9,10},{11,8},{10,... | collective-permute-start | bytes 170504 | tf_op jit(solution)/shard_map/ppermute | solution.py:428

commit v4 on v3

--- a/solution.py
+++ b/solution.py
@@ -33,16 +33,14 @@
     offset_hbm,
     cell_hbm,
     slot_hbm,
-    out_hbm,
+    out,
     count,
     values,
     offset,
     cell,
     slot,
     rows,
-    out,
     here,
-    sent,
 ):
     tiles, capacity = cell.shape
     halves = capacity // LANES
@@ -82,7 +80,6 @@
         (jnp.where(middle, HALF, 0) + (column % 2) * ROWS + within).astype(jnp.float32),
     )
     base = halves * WIDTH
-    sends = []
     for j in range(groups):
         own = slice(j * GROUP, (j + 1) * GROUP)
 
@@ -104,10 +101,6 @@
             for i in range(used // TILE):
                 first = d * stride + i * TILE
                 out[d, i] = rows[first : first + TILE, :].astype(jnp.bfloat16)
-        sends.append(pltpu.make_async_copy(out.at[at(j)], out_hbm.at[at(j)], sent.at[j]))
-        sends[-1].start()
-    for copy in sends:
-        copy.wait()
 
 
 def pack(obs_values, obs_offset, obs_cell, obs_slot, obs_count):
@@ -120,17 +113,15 @@
     return pl.pallas_call(
         pack_kernel,
         in_specs=[ANY] * len(arrays),
-        out_specs=ANY,
-        out_shape=jax.ShapeDtypeStruct(shape, jnp.bfloat16),
+        out_specs=VMEM,
+        out_shape=pltpu.VMEM(shape, jnp.bfloat16),
         scratch_shapes=[pltpu.VMEM(a.shape, a.dtype) for a in arrays]
         + [
             pltpu.VMEM((tiles * stride, LANES), jnp.float32),
-            pltpu.VMEM(shape, jnp.bfloat16),
             pltpu.SemaphoreType.DMA((tiles // GROUP + 4,)),
-            pltpu.SemaphoreType.DMA((tiles // GROUP,)),
         ],
-        compiler_params=pltpu.CompilerParams(vmem_limit_bytes=60 << 20),
-    )(*arrays)
+        compiler_params=pltpu.CompilerParams(vmem_limit_bytes=24 << 20),
+    )(*(pltpu.with_memory_space_constraint(a, pltpu.HBM) for a in arrays))
 
 
 def embedded_cells(x_ref, weight_ref, bias_ref, total, middle):
@@ -273,6 +264,7 @@
     bias_ref,
     depth_ref,
     gain_ref,
+    _,
     upper_ref,
     lower_ref,
     out_ref,
@@ -408,6 +400,8 @@
     lon_count, lat_count = lax.axis_size("lon"), lax.axis_size("lat")
     lat = lax.axis_index("lat")
     packed = pack(obs_values, obs_offset, obs_cell, obs_slot, obs_count)
+    lower, above, below = lat % 2 == 1, lat > 0, lat < lat_count - 1
+    packed, lower, above, below = lax.optimization_barrier((packed, lower, above, below))
     arrived = lax.all_to_all(packed, ("lon", "lat"), split_axis=0, concat_axis=0, tiled=True)
     held = jax.ShapeDtypeStruct((TLAT, HALF, D), jnp.float32)
     edges = [jax.ShapeDtypeStruct((TLAT, n, D), jnp.bfloat16) for n in (3, 2)]
@@ -422,19 +416,18 @@
     weight, bias = stride_weight.reshape(9 * D, D), stride_bias.reshape(1, D)
     framed = jnp.concatenate([tile, west, east], axis=1)
     top, bottom = framed[:3], framed[TLAT - 3 :]
-    lower = lat % 2 == 1
     pairs = [(i, i + 1) for i in range(0, lat_count - 1, 2)]
     others = [(i, (i + 1) % lat_count) for i in range(1, lat_count, 2)]
+    paired = lax.ppermute(
+        jnp.where(lower, top, bottom), "lat", pairs + [(j, i) for i, j in pairs]
+    )
     other = lax.ppermute(
         jnp.where(lower, bottom, top), "lat", others + [(j, i) for i, j in others]
     )
-    paired = lax.ppermute(
-        jnp.where(lower, top, bottom), "lat", pairs + [(j, i) for i, j in pairs]
-    )
     gain = norm_gain.reshape(1, D)
-    place = jnp.stack([lower, lat > 0, lat < lat_count - 1]).astype(jnp.float32)
+    place = jnp.stack([lower, above, below]).astype(jnp.float32)
     place = jnp.broadcast_to(place[:, None], (3, D))
-    inside = inner(tile, west, east, weight, bias, depth_weight, gain)
+    inside = inner(tile, west, east, weight, bias, depth_weight, gain, place)
     return outer(
         place, *inside, tile, west, east, paired, other, weight, bias, depth_weight, gain
     )

time: 40.4 us -> 39.4 us (0.975)
  blocking collectives: 0 us -> 23.2 us
  waiting for transfers between devices: 17.9 us -> 1.7 us
  starting transfers between devices: 13.3 us -> 6.02 us
  Pallas kernels: 8.65 us -> 7.94 us
    all_to_all x0 -> x1, blocking collectives: none -> 23.2 us  [on_device(): lax.all_to_all(packed, ('lon', 'lat'), split_axis=0, concat_axis=0, tiled...]
    all_to_all x1 -> x0, waiting for transfers between devices: 16.1 us -> none  [on_device(): lax.all_to_all(packed, ('lon', 'lat'), split_axis=0, concat_axis=0, tiled...]
    all_to_all x1 -> x0, starting transfers between devices: 7.3 us -> none  [on_device(): lax.all_to_all(packed, ('lon', 'lat'), split_axis=0, concat_axis=0, tiled...]
    pallas_call x1, Pallas kernels: 2.22 us -> 1.5 us  [pack(): pl.pallas_call(pack_kernel, in_specs=[ANY] * len(arrays), out_specs=VMEM,...]
  transfers between devices with their start and end apart: 5 -> 4, of which waited for: 2 -> 1; matrix products, arithmetic and copies ran while one was open for 0% -> 0% of each run, Pallas kernels for 7% -> 8%
where the time goes in v4:
time: 39.4 us; the launch traced here: 39.2 us
  blocking collectives  23.2 us (59%)
  Pallas kernels  7.94 us (20%)
  starting transfers between devices  6.02 us (15%)
  waiting for transfers between devices  1.7 us (4%)
    all_to_all x1, blocking collectives, on_device(): lax.all_to_all(packed, ('lon', 'lat'), split_axis=0, concat_axis=0, tiled...  23.2 us
    pallas_call x2, Pallas kernels, scatter(): pl.pallas_call(kernel, in_specs=[VMEM] * (3 + len(more)), out_specs=[VMEM...  4.47 us
    ppermute x1, starting transfers between devices, on_device(): east = lax.ppermute(first, 'lon', [(j, i) for i, j in ring])  3.43 us
    ppermute x1, waiting for transfers between devices, on_device(): lax.ppermute(jnp.where(lower, bottom, top), 'lat', others + [(j, i) for i...  1.69 us
    pallas_call x1, Pallas kernels, pack(): pl.pallas_call(pack_kernel, in_specs=[ANY] * len(arrays), out_specs=VMEM,...  1.5 us
    ppermute x1, starting transfers between devices, on_device(): west = lax.ppermute(last, 'lon', ring)  1.35 us
    pallas_call x1, Pallas kernels, outer(): pl.pallas_call(outer_kernel, in_specs=[VMEM] * len(arrays), out_specs=ANY...  1.23 us
    ppermute x1, starting transfers between devices, on_device(): lax.ppermute(jnp.where(lower, bottom, top), 'lat', others + [(j, i) for i...  1.18 us
  transfers between devices with their start and end apart: 4, of which 1 were waited for; matrix products, arithmetic and copies ran while one was open for 0% of the time, Pallas kernels for 8%

profile of v4, /device:TPU:0, one launch (start us, length us, event | category | flops | bytes accessed | tf_op | source)
XLA Modules:
  0.0 39.2 jit_solution(1981867258701851551)
XLA Ops:
  0.0 0.0 copy-start.5
  0.0 0.0 copy-start.4
  0.0 1.5 %shard_map.109 = bf16[32,17,4,128]{3,2,1,0:T(4,128)(2,1)S(1)} custom-call(s32[1,32]{1,0:T(1,128)} %count_hbm.1, bf16[31,32,256]{2,1,0:T(8,128)(2,1)} %bitcast.16, f32[32,2,256]{2,1,0:T(2,128)} %offset_hbm.1, s32[32,256]{1,0:T(8,128)} %cell_hbm.1, s32[32,256]{1,0:T(8,128)} %slot_hbm.1), custom_call_target="tpu_custom_call" | custom-call | tf_op jit(solution)/shard_map/pallas_call | solution.py:113
  1.5 23.2 %all_to_all.5.x_ref = bf16[32,17,4,128]{3,2,1,0:T(4,128)(2,1)S(1)} all-to-all(bf16[32,17,4,128]{3,2,1,0:T(4,128)(2,1)S(1)} %shard_map.109), channel_id=1, replica_groups=mesh['lon'=8,'lat'=4] {'lon','lat'}, dimensions={0} | all-to-all | bytes 1114112 | tf_op jit(solution)/shard_map/all_to_all | solution.py:405
  24.8 0.0 copy-done.5
  24.8 0.0 copy-done.4
  24.8 2.2 %shard_map.110 = (f32[16,16,256]{2,1,0:T(8,128)S(1)}, bf16[16,3,256]{2,1,0:T(4,128)(2,1)S(1)}, bf16[16,2,256]{2,1,0:T(2,128)(2,1)S(1)}) custom-call(bf16[32,17,4,128]{3,2,1,0:T(4,128)(2,1)S(1)} %all_to_all.5.x_ref, bf16[384,256]{1,0:T(8,128)(2,1)S(1)} %copy-done.4, f32[1,256]{1,0:T(1,128)S(1)} %bitcast.14), custom_call_target="tpu_custom_call" | custom-call | flops 1610612736 | bytes 4194304 | tf_op jit(solution)/shard_map/pallas_call | solution.py:212
  27.0 1.3 %collective-permute-start = (bf16[16,3,256]{2,1,0:T(4,128)(2,1)S(1)}, bf16[16,3,256]{2,1,0:T(4,128)(2,1)S(1)}, u32[]{:S(2)}, u32[]{:S(2)}) collective-permute-start(bf16[16,3,256]{2,1,0:T(4,128)(2,1)S(1)} %get-tuple-element.20), channel_id=1, source_target_pairs={{0,4},{4,8},{8,12},{12,16},{16,20},{20,24},{24,28},{28,0},{1,5},{5... | collective-permute-start | bytes 73736 | tf_op jit(solution)/shard_map/ppermute | solution.py:412
  28.3 3.4 %collective-permute-start.1 = (bf16[16,2,256]{2,1,0:T(2,128)(2,1)S(1)}, bf16[16,2,256]{2,1,0:T(2,128)(2,1)S(1)}, u32[]{:S(2)}, u32[]{:S(2)}) collective-permute-start(bf16[16,2,256]{2,1,0:T(2,128)(2,1)S(1)} %get-tuple-element.21), channel_id=1, source_target_pairs={{4,0},{8,4},{12,8},{16,12},{20,16},{24,20},{28,24},{0,28},{5,1},{9... | collective-permute-start | bytes 49160 | tf_op jit(solution)/shard_map/ppermute | solution.py:413
  31.8 0.0 copy-start
  31.8 0.0 copy-start.1
  31.8 0.0 copy-start.2
  31.8 0.0 copy-start.3
  31.8 2.2 %shard_map.111.tile_ref = bf16[16,32,256]{2,1,0:T(8,128)(2,1)S(1)} custom-call(bf16[32,17,4,128]{3,2,1,0:T(4,128)(2,1)S(1)} %all_to_all.5.x_ref, bf16[384,256]{1,0:T(8,128)(2,1)S(1)} %copy-done.4, f32[1,256]{1,0:T(1,128)S(1)} %bitcast.15, f32[16,16,256]{2,1,0:T(8,128)S(1)} %get-tuple-element.19.sides_ref), custom_call_target="tpu_custom_call" | custom-call | flops 1610612736 | bytes 4194304 | tf_op jit(solution)/shard_map/pallas_call | solution.py:212
  34.0 0.0 collective-permute-done.1.east_ref
  34.0 0.0 collective-permute-done.west_ref
  34.1 0.1 collective-permute-start.2
  34.2 1.2 %collective-permute-start.3 = (bf16[3,37,256]{2,1,0:T(8,128)(2,1)S(1)}, bf16[3,37,256]{2,1,0:T(8,128)(2,1)S(1)}, u32[]{:S(2)}, u32[]{:S(2)}) collective-permute-start(bf16[3,37,256]{2,1,0:T(8,128)(2,1)S(1)} %get-tuple-element.25), channel_id=1, source_target_pairs={{1,2},{3,0},{2,1},{0,3},{5,6},{7,4},{6,5},{4,7},{9,10},{11,8},{10,... | collective-permute-start | bytes 170504 | tf_op jit(solution)/shard_map/ppermute | solution.py:424
  35.4 0.1 add_convert_fusion
  35.4 0.1 broadcast_in_dim.2._.place_ref
  35.5 0.0 copy-done
  35.5 0.0 copy-done.1
  35.5 0.0 copy-done.2
  35.5 0.0 copy-done.3
  35.5 0.7 %shard_map.112 = (f32[2,24,256]{2,1,0:T(8,128)S(1)}, f32[2,24,256]{2,1,0:T(8,128)S(1)}, bf16[5,16,256]{2,1,0:T(8,128)(2,1)S(1)}) custom-call(bf16[16,32,256]{2,1,0:T(8,128)(2,1)S(1)} %shard_map.111.tile_ref, bf16[16,3,256]{2,1,0:T(4,128)(2,1)S(1)} %collective-permute-done.west_ref, bf16[16,2,256]{2,1,0:T(2,128)(2,1)S(1)} %collective-permute-done.1.east_ref, ...), custom_call_target="tpu_custom_call" | custom-call | flops 198180864 | bytes 2097152 | tf_op jit(solution)/shard_map/pallas_call | solution.py:285
  36.3 0.0 collective-permute-done.2.pair_ref
  36.3 1.7 %collective-permute-done.3.other_ref = bf16[3,37,256]{2,1,0:T(8,128)(2,1)S(1)} collective-permute-done((bf16[3,37,256]{2,1,0:T(8,128)(2,1)S(1)}, bf16[3,37,256]{2,1,0:T(8,128)(2,1)S(1)}, u32[]{:S(2)}, u32[]{:S(2)}) %collective-permute-start.3) | collective-permute-done | bytes 56864 | tf_op jit(solution)/shard_map/ppermute | solution.py:424
  38.0 1.2 %shard_map.113 = bf16[8,16,256]{2,1,0:T(8,128)(2,1)} custom-call(f32[3,256]{1,0:T(4,128)S(1)} %broadcast_in_dim.2._.place_ref, f32[2,24,256]{2,1,0:T(8,128)S(1)} %get-tuple-element.22.upper_ref, f32[2,24,256]{2,1,0:T(8,128)S(1)} %get-tuple-element.23.lower_ref, bf16[5,16,256]{2,1,0:T(8,128)(2,1)S(1)} %get-tuple-element.24.done_ref, ...), custom_call_target="tpu_custom_call" | custom-call | tf_op jit(solution)/shard_map/pallas_call | solution.py:370
  (2 shorter events, 0.0 us)
Async XLA Ops:
  0.0 24.8 %copy-start.5 = (f32[256]{0:T(256)S(1)}, f32[256]{0:T(256)}, u32[]{:S(2)}) copy-start(f32[256]{0:T(256)} %param.17) | copy-start | bytes 3076
  0.0 24.8 %copy-start.4 = (bf16[384,256]{1,0:T(8,128)(2,1)S(1)}, bf16[384,256]{1,0:T(8,128)(2,1)}, u32[]{:S(2)}) copy-start(bf16[384,256]{1,0:T(8,128)(2,1)} %weight_ref.3) | copy-start | bytes 589828
  27.0 7.0 %collective-permute-start = (bf16[16,3,256]{2,1,0:T(4,128)(2,1)S(1)}, bf16[16,3,256]{2,1,0:T(4,128)(2,1)S(1)}, u32[]{:S(2)}, u32[]{:S(2)}) collective-permute-start(bf16[16,3,256]{2,1,0:T(4,128)(2,1)S(1)} %get-tuple-element.20), channel_id=1, source_target_pairs={{0,4},{4,8},{8,12},{12,16},{16,20},{20,24},{24,28},{28,0},{1,5},{5... | collective-permute-start | bytes 73736 | tf_op jit(solution)/shard_map/ppermute | solution.py:412
  28.3 5.7 %collective-permute-start.1 = (bf16[16,2,256]{2,1,0:T(2,128)(2,1)S(1)}, bf16[16,2,256]{2,1,0:T(2,128)(2,1)S(1)}, u32[]{:S(2)}, u32[]{:S(2)}) collective-permute-start(bf16[16,2,256]{2,1,0:T(2,128)(2,1)S(1)} %get-tuple-element.21), channel_id=1, source_target_pairs={{4,0},{8,4},{12,8},{16,12},{20,16},{24,20},{28,24},{0,28},{5,1},{9... | collective-permute-start | bytes 49160 | tf_op jit(solution)/shard_map/ppermute | solution.py:413
  31.8 3.7 %copy-start = (bf16[9,256,256]{2,1,0:T(8,128)(2,1)S(1)}, bf16[9,256,256]{2,1,0:T(8,128)(2,1)}, u32[]{:S(2)}) copy-start(bf16[9,256,256]{2,1,0:T(8,128)(2,1)} %param.18) | copy-start | bytes 3538948
  31.8 3.7 %copy-start.1 = (f32[9,256]{1,0:T(8,128)S(1)}, f32[9,256]{1,0:T(8,128)}, u32[]{:S(2)}) copy-start(f32[9,256]{1,0:T(8,128)} %depth_ref.3) | copy-start | bytes 27652
  31.8 3.7 %copy-start.2 = (f32[256]{0:T(256)S(1)}, f32[256]{0:T(256)}, u32[]{:S(2)}) copy-start(f32[256]{0:T(256)} %param.19) | copy-start | bytes 3076
  31.8 3.7 %copy-start.3 = (f32[256]{0:T(256)S(1)}, f32[256]{0:T(256)}, u32[]{:S(2)}) copy-start(f32[256]{0:T(256)} %param.21) | copy-start | bytes 3076
  34.1 2.2 %collective-permute-start.2 = (bf16[3,37,256]{2,1,0:T(8,128)(2,1)S(1)}, bf16[3,37,256]{2,1,0:T(8,128)(2,1)S(1)}, u32[]{:S(2)}, u32[]{:S(2)}) collective-permute-start(bf16[3,37,256]{2,1,0:T(8,128)(2,1)S(1)} %broadcast_select_fusion.1), channel_id=1, source_target_pairs={{0,1},{2,3},{1,0},{3,2},{4,5},{6,7},{5,4},{7,6},{8,9},{10,11},{9,8... | collective-permute-start | bytes 170504 | tf_op jit(solution)/shard_map/ppermute | solution.py:421
  34.2 3.8 %collective-permute-start.3 = (bf16[3,37,256]{2,1,0:T(8,128)(2,1)S(1)}, bf16[3,37,256]{2,1,0:T(8,128)(2,1)S(1)}, u32[]{:S(2)}, u32[]{:S(2)}) collective-permute-start(bf16[3,37,256]{2,1,0:T(8,128)(2,1)S(1)} %get-tuple-element.25), channel_id=1, source_target_pairs={{1,2},{3,0},{2,1},{0,3},{5,6},{7,4},{6,5},{4,7},{9,10},{11,8},{10,... | collective-permute-start | bytes 170504 | tf_op jit(solution)/shard_map/ppermute | solution.py:424

commit v5 on v4

--- a/solution.py
+++ b/solution.py
@@ -21,10 +21,30 @@
 TILE = 4
 CHUNK = 32
 SPAN = 24
+CELLS = TLAT * TLON
+MID = 12
+EXTRA = 4
+SIDES = TLAT * 8
 FRAME = TLON + 5
 
 ANY = pl.BlockSpec(memory_space=pl.ANY)
 VMEM = pl.BlockSpec(memory_space=pltpu.VMEM)
+
+
+def placed_cells(cell):
+    row, column = cell // TLON, cell % TLON
+    pair, parity = column // 2, column % 2
+    side = (pair < 1) | (pair > MID)
+    edge = (row < 2) | (row >= TLAT - 3)
+    corner = (row == 2) & (pair <= EXTRA)
+    at_side = row * 8 + parity * 4 + jnp.where(pair < 1, 0, pair - MID)
+    at_edge = SIDES + jnp.where(row < 2, row, row - TLAT + 5) * 2 * MID + parity * MID + pair - 1
+    at_corner = SIDES + 10 * MID + parity * EXTRA + pair - 1
+    at_row = CELLS // 2 - 2 * (MID - EXTRA) + parity * (MID - EXTRA) + pair - 1 - EXTRA
+    at_inside = (row - 3) * 2 * MID + parity * MID + pair - 1
+    rim = side | edge | corner
+    in_rim = jnp.where(side, at_side, jnp.where(edge, at_edge, at_corner))
+    return rim, jnp.where(rim, in_rim, jnp.where(row == 2, at_row, at_inside))
 
 
 def pack_kernel(
@@ -71,13 +91,10 @@
     position = lax.broadcasted_iota(jnp.int32, (tiles, capacity), 1)
     dy, dx = offset[:, 0, :], offset[:, 1, :]
     weight = jnp.where(position < counts, jnp.exp(-2.0 * (dy * dy + dx * dx)), 0.0)
-    column = cell[...] % TLON
-    pair = column // 2
-    middle = (pair >= ROWS // 2) & (pair < 3 * ROWS // 2)
-    within = pair - jnp.where(pair < ROWS // 2, 0, jnp.where(middle, ROWS // 2, ROWS))
+    rim, place = placed_cells(cell[...])
     codes = (
-        (slot[...] * TLAT + cell[...] // TLON).astype(jnp.float32),
-        (jnp.where(middle, HALF, 0) + (column % 2) * ROWS + within).astype(jnp.float32),
+        (slot[...] + jnp.where(rim, 0, SLOTS)).astype(jnp.float32),
+        place.astype(jnp.float32),
     )
     base = halves * WIDTH
     for j in range(groups):
@@ -124,31 +141,30 @@
     )(*(pltpu.with_memory_space_constraint(a, pltpu.HBM) for a in arrays))
 
 
-def embedded_cells(x_ref, weight_ref, bias_ref, total, middle):
-    tiles, blocks, _, _ = x_ref.shape
+def add_sums(x_ref, total, first_slot, begin, end, held=None):
+    blocks = x_ref.shape[1]
     halves = blocks * TILE // WIDTH
     step = WIDTH // TILE
-    iota = lax.broadcasted_iota(jnp.int32, (HALF, LANES), 0).astype(jnp.float32)
-    none = jnp.zeros((HALF, LANES), jnp.bfloat16)
+    tall = 16
+    iota = lax.broadcasted_iota(jnp.int32, (tall, LANES), 0).astype(jnp.float32)
+    one = jnp.ones((tall, LANES), jnp.bfloat16)
+    none = jnp.zeros((tall, LANES), jnp.bfloat16)
     zero = jnp.zeros((WIDTH, LANES), jnp.bfloat16)
+    cells = [(iota + r).astype(jnp.bfloat16) for r in range(0, CELLS // 2, tall)]
 
     def operands(source):
         codes = x_ref[source, halves * step].astype(jnp.float32)
         spread, hot = [], []
         for h in range(halves):
             value = x_ref[source, h * step : (h + 1) * step].reshape(WIDTH, LANES)
-            code = codes[h : h + 1]
-            slot = jnp.floor(code * (1.0 / TLAT))
-            row = jnp.broadcast_to(code - slot * TLAT, (HALF, LANES)).astype(jnp.bfloat16)
-            column = codes[halves + h : halves + h + 1]
-            group = jnp.where(column >= HALF, 1.0, 0.0)
-            slot = jnp.where(group == middle, slot, SLOTS)
-            slot = jnp.broadcast_to(slot, (WIDTH, LANES)).astype(jnp.bfloat16)
-            column = jnp.where(iota == column - group * HALF, 1.0, 0.0).astype(jnp.bfloat16)
-            by_slot = [jnp.where(slot == jnp.bfloat16(s), value, zero) for s in range(SLOTS)]
-            by_row = [jnp.where(row == jnp.bfloat16(r), column, none) for r in range(TLAT)]
+            slot = jnp.broadcast_to(codes[h : h + 1], (WIDTH, LANES)).astype(jnp.bfloat16)
+            place = codes[halves + h : halves + h + 1]
+            place = jnp.broadcast_to(place, (tall, LANES)).astype(jnp.bfloat16)
+            slots = range(first_slot, first_slot + SLOTS)
+            by_slot = [jnp.where(slot == jnp.bfloat16(s), value, zero) for s in slots]
+            by_cell = [jnp.where(place == c, one, none) for c in cells]
             spread.append(jnp.concatenate(by_slot, axis=0))
-            hot.append(jnp.concatenate(by_row, axis=0))
+            hot.append(jnp.concatenate(by_cell, axis=0))
         return jnp.concatenate(spread, axis=1), jnp.concatenate(hot, axis=1)
 
     def summed(first, count):
@@ -160,13 +176,15 @@
             preferred_element_type=jnp.float32,
         )
 
-    count = min(tiles, CHUNK)
-    total[...] = summed(0, count)
-
-    @pl.loop(1, tiles // count)
+    count = min(end - begin, CHUNK)
+    total[...] = summed(begin, count) if held is None else held + summed(begin, count)
+
+    @pl.loop(1, (end - begin) // count)
     def _(step):
-        total[...] += summed(step * count, count)
-
+        total[...] += summed(begin + step * count, count)
+
+
+def embedded_cells(total, weight_ref, bias_ref):
     groups = []
     for s in range(SLOTS):
         block = total[s * WIDTH : (s + 1) * WIDTH, :]
@@ -180,46 +198,53 @@
         (((0,), (0,)), ((), ())),
         preferred_element_type=jnp.float32,
     )
-    return jax.nn.gelu(projected + bias_ref[...]).reshape(TLAT, HALF, D)
-
-
-def sides_kernel(x_ref, weight_ref, bias_ref, sides_ref, last_ref, first_ref, total):
-    sides = embedded_cells(x_ref, weight_ref, bias_ref, total, 0.0)
-    sides_ref[...] = sides
-    last = [sides[:, c : c + 1] for c in (HALF - 2, ROWS - 1, HALF - 1)]
-    first = [sides[:, c : c + 1] for c in (0, ROWS)]
+    return jax.nn.gelu(projected + bias_ref[...])
+
+
+def rim_kernel(x_ref, weight_ref, bias_ref, rim_ref, rows_ref, last_ref, first_ref, total):
+    add_sums(x_ref, total, 0, 0, x_ref.shape[0])
+    rim = embedded_cells(total, weight_ref, bias_ref)
+    rim_ref[...] = rim
+    sides = rim[:SIDES].reshape(TLAT, 8, D)
+    middle = rim[SIDES : SIDES + 10 * MID].reshape(5, 2 * MID, D)
+    ends = jnp.concatenate([sides[:2], sides[TLAT - 3 :]], axis=0)
+    parts = []
+    for parity in range(2):
+        at = 4 * parity
+        parts += [
+            ends[:, at : at + 1],
+            middle[:, parity * MID : (parity + 1) * MID],
+            ends[:, at + 1 : at + 4],
+        ]
+    rows_ref[...] = jnp.concatenate(parts, axis=1).astype(jnp.bfloat16)
+    last = [sides[:, c : c + 1] for c in (6, 3, 7)]
+    first = [sides[:, c : c + 1] for c in (0, 4)]
     last_ref[...] = jnp.concatenate(last, axis=1).astype(jnp.bfloat16)
     first_ref[...] = jnp.concatenate(first, axis=1).astype(jnp.bfloat16)
 
 
-def middle_kernel(x_ref, weight_ref, bias_ref, sides_ref, tile_ref, total):
-    middle = embedded_cells(x_ref, weight_ref, bias_ref, total, 1.0)
-    sides = sides_ref[...]
-    quarter = ROWS // 2
-    whole = []
-    for parity in range(2):
-        at = parity * ROWS
-        whole += [
-            sides[:, at : at + quarter],
-            middle[:, at : at + ROWS],
-            sides[:, at + quarter : at + ROWS],
-        ]
-    tile_ref[...] = jnp.concatenate(whole, axis=1).astype(jnp.bfloat16)
-
-
-def scatter(kernel, arrived, embed_weight, embed_bias, *more, outs):
-    tiles = arrived.shape[0]
+def scatter_cost(tiles):
+    return pl.CostEstimate(
+        flops=2 * tiles * 256 * BINS * CELLS // 2, bytes_accessed=4 << 20, transcendentals=0
+    )
+
+
+def rim_cells(arrived, embed_weight, embed_bias):
+    outs = [
+        jax.ShapeDtypeStruct((CELLS // 2, D), jnp.float32),
+        jax.ShapeDtypeStruct((5, TLON, D), jnp.bfloat16),
+        jax.ShapeDtypeStruct((TLAT, 3, D), jnp.bfloat16),
+        jax.ShapeDtypeStruct((TLAT, 2, D), jnp.bfloat16),
+    ]
     return pl.pallas_call(
-        kernel,
-        in_specs=[VMEM] * (3 + len(more)),
+        rim_kernel,
+        in_specs=[VMEM] * 3,
         out_specs=[VMEM] * len(outs),
         out_shape=outs,
-        scratch_shapes=[pltpu.VMEM((BINS, TLAT * HALF), jnp.float32)],
+        scratch_shapes=[pltpu.VMEM((BINS, CELLS // 2), jnp.float32)],
         compiler_params=pltpu.CompilerParams(vmem_limit_bytes=32 << 20),
-        cost_estimate=pl.CostEstimate(
-            flops=2 * tiles * 256 * BINS * TLAT * HALF, bytes_accessed=4 << 20, transcendentals=0
-        ),
-    )(arrived, embed_weight, embed_bias.reshape(1, D), *more)
+        cost_estimate=scatter_cost(arrived.shape[0]),
+    )(arrived, embed_weight, embed_bias)
 
 
 def put_rows(even, odd, rows, tile, west, east):
@@ -256,8 +281,27 @@
     return (centre * lax.rsqrt(variance + 1e-05) * gain_ref[...]).astype(jnp.bfloat16)
 
 
+def half_kernel(x_ref, half_ref):
+    add_sums(x_ref, half_ref, SLOTS, 0, x_ref.shape[0] // 2)
+
+
+def half_sums(arrived):
+    return pl.pallas_call(
+        half_kernel,
+        in_specs=[VMEM],
+        out_specs=VMEM,
+        out_shape=jax.ShapeDtypeStruct((BINS, CELLS // 2), jnp.float32),
+        compiler_params=pltpu.CompilerParams(vmem_limit_bytes=32 << 20),
+        cost_estimate=scatter_cost(arrived.shape[0]),
+    )(arrived)
+
+
 def inner_kernel(
-    tile_ref,
+    x_ref,
+    half_ref,
+    embed_ref,
+    embed_bias_ref,
+    rim_ref,
     west_ref,
     east_ref,
     weight_ref,
@@ -268,35 +312,59 @@
     upper_ref,
     lower_ref,
     out_ref,
+    total,
     even,
     odd,
     coarse,
 ):
-    tile, west, east = (r[...].astype(jnp.float32) for r in (tile_ref, west_ref, east_ref))
-    put_rows(even, odd, slice(0, TLAT), tile, west, east)
+    tiles = x_ref.shape[0]
+    add_sums(x_ref, total, SLOTS, tiles // 2, tiles, half_ref[...])
+    inside = embedded_cells(total, embed_ref, embed_bias_ref)
+    west, east = (r[...].astype(jnp.float32) for r in (west_ref, east_ref))
+    sides = rim_ref[:SIDES].reshape(TLAT, 8, D)
+    edges = rim_ref[SIDES : SIDES + 10 * MID].reshape(5, 2 * MID, D)
+    corner = rim_ref[SIDES + 10 * MID :].reshape(1, 2 * EXTRA, D)
+    bulk = inside[: 20 * MID].reshape(TLAT - 6, 2 * MID, D)
+    rest = inside[20 * MID :].reshape(1, 2 * (MID - EXTRA), D)
+    even[:, 0:1] = west[:, 1:2]
+    odd[:, 0:1] = west[:, 0:1]
+    odd[:, 1:2] = west[:, 2:3]
+    for parity, held in ((0, even), (1, odd)):
+        at = 1 + parity
+        mid = slice(at + 1, at + 1 + MID)
+        cut = at + 1 + EXTRA
+        own = slice(parity * MID, (parity + 1) * MID)
+        held[:, at : at + 1] = sides[:, 4 * parity : 4 * parity + 1]
+        held[:, at + 1 + MID : at + HALF] = sides[:, 4 * parity + 1 : 4 * parity + 4]
+        held[:, at + HALF : at + HALF + 1] = east[:, parity : parity + 1]
+        held[0:2, mid] = edges[0:2, own]
+        held[TLAT - 3 :, mid] = edges[2:5, own]
+        held[3 : TLAT - 3, mid] = bulk[:, own]
+        held[2:3, at + 1 : cut] = corner[:, EXTRA * parity : EXTRA * (parity + 1)]
+        span = MID - EXTRA
+        held[2:3, cut : cut + span] = rest[:, span * parity : span * (parity + 1)]
     coarse[...] = strided_rows(even, odd, range(1, TLAT - 2, 2), weight_ref, bias_ref)
     upper_ref[...] = coarse[0:2]
     lower_ref[...] = coarse[ROWS - 3 : ROWS - 1]
     out_ref[...] = finished(coarse, 0, ROWS - 3, depth_ref, gain_ref)
 
 
-def inner(*arrays):
+def inner(arrived, *arrays):
     pair = jax.ShapeDtypeStruct((2, SPAN, D), jnp.float32)
     return pl.pallas_call(
         inner_kernel,
-        in_specs=[VMEM] * len(arrays),
+        in_specs=[VMEM] * (1 + len(arrays)),
         out_specs=[VMEM] * 3,
         out_shape=[pair, pair, jax.ShapeDtypeStruct((ROWS - 3, HALF, D), jnp.bfloat16)],
         scratch_shapes=[
+            pltpu.VMEM((BINS, CELLS // 2), jnp.float32),
             pltpu.VMEM((TLAT, SPAN, D), jnp.float32),
             pltpu.VMEM((TLAT, SPAN + 8, D), jnp.float32),
             pltpu.VMEM((ROWS - 1, SPAN, D), jnp.float32),
         ],
-        compiler_params=pltpu.CompilerParams(vmem_limit_bytes=16 << 20),
-        cost_estimate=pl.CostEstimate(
-            flops=2 * 7 * SPAN * 9 * D * D, bytes_accessed=2 << 20, transcendentals=0
-        ),
-    )(*arrays)
+        compiler_params=pltpu.CompilerParams(vmem_limit_bytes=32 << 20),
+        cost_estimate=scatter_cost(arrived.shape[0]),
+    )(arrived, *arrays)
 
 
 def outer_kernel(
@@ -304,7 +372,7 @@
     upper_ref,
     lower_ref,
     done_ref,
-    tile_ref,
+    rows_ref,
     west_ref,
     east_ref,
     pair_ref,
@@ -338,12 +406,12 @@
             part[:, TLON : TLON + 3],
             part[:, TLON + 3 :],
         )
-    for at, rows in ((3, slice(0, 2)), (5, slice(TLAT - 1, TLAT))):
+    for at, rows, own in ((3, slice(0, 2), slice(0, 2)), (5, slice(TLAT - 1, TLAT), slice(4, 5))):
         put_rows(
             even,
             odd,
             slice(at, at + rows.stop - rows.start),
-            tile_ref[rows].astype(jnp.float32),
+            rows_ref[own].astype(jnp.float32),
             west_ref[rows].astype(jnp.float32),
             east_ref[rows].astype(jnp.float32),
         )
@@ -403,19 +471,16 @@
     lower, above, below = lat % 2 == 1, lat > 0, lat < lat_count - 1
     packed, lower, above, below = lax.optimization_barrier((packed, lower, above, below))
     arrived = lax.all_to_all(packed, ("lon", "lat"), split_axis=0, concat_axis=0, tiled=True)
-    held = jax.ShapeDtypeStruct((TLAT, HALF, D), jnp.float32)
-    edges = [jax.ShapeDtypeStruct((TLAT, n, D), jnp.bfloat16) for n in (3, 2)]
-    sides, last, first = scatter(
-        sides_kernel, arrived, embed_weight, embed_bias, outs=[held] + edges
-    )
+    embed = embed_bias.reshape(1, D)
+    rim, rows, last, first = rim_cells(arrived, embed_weight, embed)
+    rows, lower, above, below = lax.optimization_barrier((rows, lower, above, below))
     ring = [(i, (i + 1) % lon_count) for i in range(lon_count)]
     west = lax.ppermute(last, "lon", ring)
     east = lax.ppermute(first, "lon", [(j, i) for i, j in ring])
-    cells = jax.ShapeDtypeStruct((TLAT, TLON, D), jnp.bfloat16)
-    (tile,) = scatter(middle_kernel, arrived, embed_weight, embed_bias, sides, outs=[cells])
+    half = half_sums(arrived)
     weight, bias = stride_weight.reshape(9 * D, D), stride_bias.reshape(1, D)
-    framed = jnp.concatenate([tile, west, east], axis=1)
-    top, bottom = framed[:3], framed[TLAT - 3 :]
+    top = jnp.concatenate([rows[:3], west[:3], east[:3]], axis=1)
+    bottom = jnp.concatenate([rows[2:], west[TLAT - 3 :], east[TLAT - 3 :]], axis=1)
     pairs = [(i, i + 1) for i in range(0, lat_count - 1, 2)]
     others = [(i, (i + 1) % lat_count) for i in range(1, lat_count, 2)]
     paired = lax.ppermute(
@@ -425,11 +490,14 @@
         jnp.where(lower, bottom, top), "lat", others + [(j, i) for i, j in others]
     )
     gain = norm_gain.reshape(1, D)
-    place = jnp.stack([lower, above, below]).astype(jnp.float32)
-    place = jnp.broadcast_to(place[:, None], (3, D))
-    inside = inner(tile, west, east, weight, bias, depth_weight, gain, place)
+    index = lax.broadcasted_iota(jnp.int32, (3, D), 0)
+    flags = jnp.where(index == 0, lower, jnp.where(index == 1, above, below))
+    place = flags.astype(jnp.float32)
+    inside = inner(
+        arrived, half, embed_weight, embed, rim, west, east, weight, bias, depth_weight, gain, place
+    )
     return outer(
-        place, *inside, tile, west, east, paired, other, weight, bias, depth_weight, gain
+        place, *inside, rows, west, east, paired, other, weight, bias, depth_weight, gain
     )
 
 

time: 39.4 us -> 39 us (0.990)
  waiting for transfers between devices: 1.7 us -> 0.89 us
  Pallas kernels: 7.94 us -> 8.44 us
    ppermute x1, waiting for transfers between devices: 1.69 us -> 0.1 us  [on_device(): lax.ppermute(jnp.where(lower, bottom, top), 'lat', others + [(j, i) for i...]
    pallas_call x3, Pallas kernels: 5.21 us -> 5.71 us  [the longest x1 2.44 us: inner(): pl.pallas_call(inner_kernel, in_specs=[VMEM] * (1 + len(arrays)), out_spe...]
    ppermute x1, waiting for transfers between devices: 0.01 us -> 0.44 us  [on_device(): west = lax.ppermute(last, 'lon', ring)]
  transfers between devices with their start and end apart: 4 -> 4, of which waited for: 1 -> 3; matrix products, arithmetic and copies ran while one was open for 0% -> 0% of each run, Pallas kernels for 8% -> 9%
where the time goes in v5:
time: 39 us; the launch traced here: 38.9 us
  blocking collectives  23.2 us (59%)
  Pallas kernels  8.44 us (22%)
  starting transfers between devices  6.01 us (15%)
  waiting for transfers between devices  0.89 us (2%)
    all_to_all x1, blocking collectives, on_device(): lax.all_to_all(packed, ('lon', 'lat'), split_axis=0, concat_axis=0, tiled...  23.2 us
    ppermute x1, starting transfers between devices, on_device(): east = lax.ppermute(first, 'lon', [(j, i) for i, j in ring])  3.44 us
    pallas_call x1, Pallas kernels, inner(): pl.pallas_call(inner_kernel, in_specs=[VMEM] * (1 + len(arrays)), out_spe...  2.44 us
    pallas_call x1, Pallas kernels, rim_cells(): pl.pallas_call(rim_kernel, in_specs=[VMEM] * 3, out_specs=[VMEM] * len(ou...  2.26 us
    pallas_call x1, Pallas kernels, pack(): pl.pallas_call(pack_kernel, in_specs=[ANY] * len(arrays), out_specs=VMEM,...  1.5 us
    ppermute x1, starting transfers between devices, on_device(): west = lax.ppermute(last, 'lon', ring)  1.33 us
    pallas_call x1, Pallas kernels, outer(): pl.pallas_call(outer_kernel, in_specs=[VMEM] * len(arrays), out_specs=ANY...  1.24 us
    ppermute x1, starting transfers between devices, on_device(): lax.ppermute(jnp.where(lower, bottom, top), 'lat', others + [(j, i) for i...  1.16 us
  transfers between devices with their start and end apart: 4, of which 3 were waited for; matrix products, arithmetic and copies ran while one was open for 0% of the time, Pallas kernels for 9%

profile of v5, /device:TPU:0, one launch (start us, length us, event | category | flops | bytes accessed | tf_op | source)
XLA Modules:
  0.0 38.9 jit_solution(13985701360787375935)
XLA Ops:
  0.0 0.0 copy-start.4
  0.0 0.0 copy-start.5
  0.0 1.5 %shard_map.109 = bf16[32,17,4,128]{3,2,1,0:T(4,128)(2,1)S(1)} custom-call(s32[1,32]{1,0:T(1,128)} %count_hbm.1, bf16[31,32,256]{2,1,0:T(8,128)(2,1)} %bitcast.13, f32[32,2,256]{2,1,0:T(2,128)} %offset_hbm.1, s32[32,256]{1,0:T(8,128)} %cell_hbm.1, s32[32,256]{1,0:T(8,128)} %slot_hbm.1), custom_call_target="tpu_custom_call" | custom-call | tf_op jit(solution)/shard_map/pallas_call | solution.py:130
  1.5 23.2 %all_to_all.5.x_ref = bf16[32,17,4,128]{3,2,1,0:T(4,128)(2,1)S(1)} all-to-all(bf16[32,17,4,128]{3,2,1,0:T(4,128)(2,1)S(1)} %shard_map.109), channel_id=1, replica_groups=mesh['lon'=8,'lat'=4] {'lon','lat'}, dimensions={0} | all-to-all | bytes 1114112 | tf_op jit(solution)/shard_map/all_to_all | solution.py:473
  24.8 0.0 copy-done.4
  24.8 0.0 copy-done.5
  24.8 2.3 %shard_map.110 = (f32[256,256]{1,0:T(8,128)S(1)}, bf16[5,32,256]{2,1,0:T(8,128)(2,1)S(1)}, bf16[16,3,256]{2,1,0:T(4,128)(2,1)S(1)}, bf16[16,2,256]{2,1,0:T(2,128)(2,1)S(1)}) custom-call(bf16[32,17,4,128]{3,2,1,0:T(4,128)(2,1)S(1)} %all_to_all.5.x_ref, bf16[384,256]{1,0:T(8,128)(2,1)S(1)} %copy-done.4, f32[1,256]{1,0:T(1,128)S(1)} %bitcast.11), custom_call_target="tpu_custom_call" | custom-call | flops 1610612736 | bytes 4194304 | tf_op jit(solution)/shard_map/pallas_call | solution.py:239
  27.0 1.3 %collective-permute-start = (bf16[16,3,256]{2,1,0:T(4,128)(2,1)S(1)}, bf16[16,3,256]{2,1,0:T(4,128)(2,1)S(1)}, u32[]{:S(2)}, u32[]{:S(2)}) collective-permute-start(bf16[16,3,256]{2,1,0:T(4,128)(2,1)S(1)} %get-tuple-element.29), channel_id=1, source_target_pairs={{0,4},{4,8},{8,12},{12,16},{16,20},{20,24},{24,28},{28,0},{1,5},{5... | collective-permute-start | bytes 73736 | tf_op jit(solution)/shard_map/ppermute | solution.py:478
  28.4 3.4 %collective-permute-start.1 = (bf16[16,2,256]{2,1,0:T(2,128)(2,1)S(1)}, bf16[16,2,256]{2,1,0:T(2,128)(2,1)S(1)}, u32[]{:S(2)}, u32[]{:S(2)}) collective-permute-start(bf16[16,2,256]{2,1,0:T(2,128)(2,1)S(1)} %get-tuple-element.30), channel_id=1, source_target_pairs={{4,0},{8,4},{12,8},{16,12},{20,16},{24,20},{28,24},{0,28},{5,1},{9... | collective-permute-start | bytes 49160 | tf_op jit(solution)/shard_map/ppermute | solution.py:479
  31.8 0.0 copy-start
  31.8 0.0 copy-start.1
  31.8 0.0 copy-start.2
  31.8 0.0 copy-start.3
  31.9 1.0 %shard_map.111.half_ref = f32[384,256]{1,0:T(8,128)S(1)} custom-call(bf16[32,17,4,128]{3,2,1,0:T(4,128)(2,1)S(1)} %all_to_all.5.x_ref), custom_call_target="tpu_custom_call" | custom-call | flops 1610612736 | bytes 4194304 | tf_op jit(solution)/shard_map/pallas_call | solution.py:289
  32.9 0.4 collective-permute-done.1.east_ref
  33.3 0.4 %collective-permute-done.west_ref = bf16[16,3,256]{2,1,0:T(4,128)(2,1)S(1)} collective-permute-done((bf16[16,3,256]{2,1,0:T(4,128)(2,1)S(1)}, bf16[16,3,256]{2,1,0:T(4,128)(2,1)S(1)}, u32[]{:S(2)}, u32[]{:S(2)}) %collective-permute-start) | collective-permute-done | bytes 24608 | tf_op jit(solution)/shard_map/ppermute | solution.py:478
  33.7 0.1 collective-permute-start.2
  33.8 1.2 %collective-permute-start.3 = (bf16[3,37,256]{2,1,0:T(8,128)(2,1)S(1)}, bf16[3,37,256]{2,1,0:T(8,128)(2,1)S(1)}, u32[]{:S(2)}, u32[]{:S(2)}) collective-permute-start(bf16[3,37,256]{2,1,0:T(8,128)(2,1)S(1)} %get-tuple-element.35), channel_id=1, source_target_pairs={{1,2},{3,0},{2,1},{0,3},{5,6},{7,4},{6,5},{4,7},{9,10},{11,8},{10,... | collective-permute-start | bytes 170504 | tf_op jit(solution)/shard_map/ppermute | solution.py:489
  35.0 0.1 iota.10._.place_ref
  35.1 0.0 copy-done
  35.1 0.0 copy-done.1
  35.1 0.0 copy-done.2
  35.1 0.0 copy-done.3
  35.1 2.4 %shard_map.112 = (f32[2,24,256]{2,1,0:T(8,128)S(1)}, f32[2,24,256]{2,1,0:T(8,128)S(1)}, bf16[5,16,256]{2,1,0:T(8,128)(2,1)S(1)}) custom-call(bf16[32,17,4,128]{3,2,1,0:T(4,128)(2,1)S(1)} %all_to_all.5.x_ref, f32[384,256]{1,0:T(8,128)S(1)} %shard_map.111.half_ref, bf16[384,256]{1,0:T(8,128)(2,1)S(1)} %copy-done.4, f32[1,256]{1,0:T(1,128)S(1)} %bitcast.12, ...), custom_call_target="tpu_custom_call" | custom-call | flops 1610612736 | bytes 4194304 | tf_op jit(solution)/shard_map/pallas_call | solution.py:354
  37.5 0.0 collective-permute-done.2.pair_ref
  37.5 0.1 collective-permute-done.3.other_ref
  37.6 1.2 %shard_map.113 = bf16[8,16,256]{2,1,0:T(8,128)(2,1)} custom-call(f32[3,256]{1,0:T(4,128)S(1)} %iota.10._.place_ref, f32[2,24,256]{2,1,0:T(8,128)S(1)} %get-tuple-element.31.upper_ref, f32[2,24,256]{2,1,0:T(8,128)S(1)} %get-tuple-element.32.lower_ref, bf16[5,16,256]{2,1,0:T(8,128)(2,1)S(1)} %get-tuple-element.33.done_ref, ...), custom_call_target="tpu_custom_call" | custom-call | tf_op jit(solution)/shard_map/pallas_call | solution.py:438
  (5 shorter events, 0.1 us)
Async XLA Ops:
  0.0 24.8 %copy-start.4 = (bf16[384,256]{1,0:T(8,128)(2,1)S(1)}, bf16[384,256]{1,0:T(8,128)(2,1)}, u32[]{:S(2)}) copy-start(bf16[384,256]{1,0:T(8,128)(2,1)} %embed_ref.1) | copy-start | bytes 589828
  0.0 24.8 %copy-start.5 = (f32[256]{0:T(256)S(1)}, f32[256]{0:T(256)}, u32[]{:S(2)}) copy-start(f32[256]{0:T(256)} %param.17) | copy-start | bytes 3076
  27.0 6.7 %collective-permute-start = (bf16[16,3,256]{2,1,0:T(4,128)(2,1)S(1)}, bf16[16,3,256]{2,1,0:T(4,128)(2,1)S(1)}, u32[]{:S(2)}, u32[]{:S(2)}) collective-permute-start(bf16[16,3,256]{2,1,0:T(4,128)(2,1)S(1)} %get-tuple-element.29), channel_id=1, source_target_pairs={{0,4},{4,8},{8,12},{12,16},{16,20},{20,24},{24,28},{28,0},{1,5},{5... | collective-permute-start | bytes 73736 | tf_op jit(solution)/shard_map/ppermute | solution.py:478
  28.4 4.9 %collective-permute-start.1 = (bf16[16,2,256]{2,1,0:T(2,128)(2,1)S(1)}, bf16[16,2,256]{2,1,0:T(2,128)(2,1)S(1)}, u32[]{:S(2)}, u32[]{:S(2)}) collective-permute-start(bf16[16,2,256]{2,1,0:T(2,128)(2,1)S(1)} %get-tuple-element.30), channel_id=1, source_target_pairs={{4,0},{8,4},{12,8},{16,12},{20,16},{24,20},{28,24},{0,28},{5,1},{9... | collective-permute-start | bytes 49160 | tf_op jit(solution)/shard_map/ppermute | solution.py:479
  31.8 3.2 %copy-start = (bf16[9,256,256]{2,1,0:T(8,128)(2,1)S(1)}, bf16[9,256,256]{2,1,0:T(8,128)(2,1)}, u32[]{:S(2)}) copy-start(bf16[9,256,256]{2,1,0:T(8,128)(2,1)} %param.18) | copy-start | bytes 3538948
  31.8 3.2 %copy-start.1 = (f32[9,256]{1,0:T(8,128)S(1)}, f32[9,256]{1,0:T(8,128)}, u32[]{:S(2)}) copy-start(f32[9,256]{1,0:T(8,128)} %depth_ref.3) | copy-start | bytes 27652
  31.8 3.2 %copy-start.2 = (f32[256]{0:T(256)S(1)}, f32[256]{0:T(256)}, u32[]{:S(2)}) copy-start(f32[256]{0:T(256)} %param.19) | copy-start | bytes 3076
  31.8 3.2 %copy-start.3 = (f32[256]{0:T(256)S(1)}, f32[256]{0:T(256)}, u32[]{:S(2)}) copy-start(f32[256]{0:T(256)} %param.21) | copy-start | bytes 3076
  33.7 3.8 %collective-permute-start.2 = (bf16[3,37,256]{2,1,0:T(8,128)(2,1)S(1)}, bf16[3,37,256]{2,1,0:T(8,128)(2,1)S(1)}, u32[]{:S(2)}, u32[]{:S(2)}) collective-permute-start(bf16[3,37,256]{2,1,0:T(8,128)(2,1)S(1)} %get-tuple-element.36), channel_id=1, source_target_pairs={{0,1},{2,3},{1,0},{3,2},{4,5},{6,7},{5,4},{7,6},{8,9},{10,11},{9,8... | collective-permute-start | bytes 170504 | tf_op jit(solution)/shard_map/ppermute | solution.py:486
  33.8 3.8 %collective-permute-start.3 = (bf16[3,37,256]{2,1,0:T(8,128)(2,1)S(1)}, bf16[3,37,256]{2,1,0:T(8,128)(2,1)S(1)}, u32[]{:S(2)}, u32[]{:S(2)}) collective-permute-start(bf16[3,37,256]{2,1,0:T(8,128)(2,1)S(1)} %get-tuple-element.35), channel_id=1, source_target_pairs={{1,2},{3,0},{2,1},{0,3},{5,6},{7,4},{6,5},{4,7},{9,10},{11,8},{10,... | collective-permute-start | bytes 170504 | tf_op jit(solution)/shard_map/ppermute | solution.py:489

commit v6 on v5

--- a/solution.py
+++ b/solution.py
@@ -20,6 +20,7 @@
 GROUP = 16
 TILE = 4
 CHUNK = 32
+EARLY = 20
 SPAN = 24
 CELLS = TLAT * TLON
 MID = 12
@@ -115,9 +116,8 @@
             for h in range(halves):
                 put(h * WIDTH + k, scaled, h)
         for d in range(j * GROUP, (j + 1) * GROUP):
-            for i in range(used // TILE):
-                first = d * stride + i * TILE
-                out[d, i] = rows[first : first + TILE, :].astype(jnp.bfloat16)
+            block = rows[d * stride : (d + 1) * stride, :].astype(jnp.bfloat16)
+            out[d] = block.reshape(stride // TILE, TILE, LANES)[: used // TILE]
 
 
 def pack(obs_values, obs_offset, obs_cell, obs_slot, obs_count):
@@ -176,7 +176,7 @@
             preferred_element_type=jnp.float32,
         )
 
-    count = min(end - begin, CHUNK)
+    count = end - begin if end - begin <= CHUNK else CHUNK // 2
     total[...] = summed(begin, count) if held is None else held + summed(begin, count)
 
     @pl.loop(1, (end - begin) // count)
@@ -201,12 +201,26 @@
     return jax.nn.gelu(projected + bias_ref[...])
 
 
-def rim_kernel(x_ref, weight_ref, bias_ref, rim_ref, rows_ref, last_ref, first_ref, total):
+def sides_kernel(x_ref, weight_ref, bias_ref, sides_ref, sums_ref, last_ref, first_ref, total):
     add_sums(x_ref, total, 0, 0, x_ref.shape[0])
-    rim = embedded_cells(total, weight_ref, bias_ref)
-    rim_ref[...] = rim
-    sides = rim[:SIDES].reshape(TLAT, 8, D)
-    middle = rim[SIDES : SIDES + 10 * MID].reshape(5, 2 * MID, D)
+    sums_ref[...] = total[:, SIDES:]
+    embedded = embedded_cells(total.at[:, :SIDES], weight_ref, bias_ref)
+    sides_ref[...] = embedded
+    sides = embedded.reshape(TLAT, 8, D)
+    last = [sides[:, c : c + 1] for c in (6, 3, 7)]
+    first = [sides[:, c : c + 1] for c in (0, 4)]
+    last_ref[...] = jnp.concatenate(last, axis=1).astype(jnp.bfloat16)
+    first_ref[...] = jnp.concatenate(first, axis=1).astype(jnp.bfloat16)
+
+
+def edges_kernel(
+    x_ref, weight_ref, bias_ref, sides_ref, sums_ref, half_ref, edges_ref, rows_ref
+):
+    add_sums(x_ref, half_ref, SLOTS, 0, x_ref.shape[0] * EARLY // 32)
+    embedded = embedded_cells(sums_ref, weight_ref, bias_ref)
+    edges_ref[...] = embedded
+    middle = embedded[: 10 * MID].reshape(5, 2 * MID, D)
+    sides = sides_ref[...].reshape(TLAT, 8, D)
     ends = jnp.concatenate([sides[:2], sides[TLAT - 3 :]], axis=0)
     parts = []
     for parity in range(2):
@@ -217,10 +231,6 @@
             ends[:, at + 1 : at + 4],
         ]
     rows_ref[...] = jnp.concatenate(parts, axis=1).astype(jnp.bfloat16)
-    last = [sides[:, c : c + 1] for c in (6, 3, 7)]
-    first = [sides[:, c : c + 1] for c in (0, 4)]
-    last_ref[...] = jnp.concatenate(last, axis=1).astype(jnp.bfloat16)
-    first_ref[...] = jnp.concatenate(first, axis=1).astype(jnp.bfloat16)
 
 
 def scatter_cost(tiles):
@@ -229,15 +239,15 @@
     )
 
 
-def rim_cells(arrived, embed_weight, embed_bias):
+def sides(arrived, embed_weight, embed_bias):
     outs = [
-        jax.ShapeDtypeStruct((CELLS // 2, D), jnp.float32),
-        jax.ShapeDtypeStruct((5, TLON, D), jnp.bfloat16),
+        jax.ShapeDtypeStruct((SIDES, D), jnp.float32),
+        jax.ShapeDtypeStruct((BINS, CELLS // 2 - SIDES), jnp.float32),
         jax.ShapeDtypeStruct((TLAT, 3, D), jnp.bfloat16),
         jax.ShapeDtypeStruct((TLAT, 2, D), jnp.bfloat16),
     ]
     return pl.pallas_call(
-        rim_kernel,
+        sides_kernel,
         in_specs=[VMEM] * 3,
         out_specs=[VMEM] * len(outs),
         out_shape=outs,
@@ -245,6 +255,22 @@
         compiler_params=pltpu.CompilerParams(vmem_limit_bytes=32 << 20),
         cost_estimate=scatter_cost(arrived.shape[0]),
     )(arrived, embed_weight, embed_bias)
+
+
+def edges(arrived, *arrays):
+    outs = [
+        jax.ShapeDtypeStruct((BINS, CELLS // 2), jnp.float32),
+        jax.ShapeDtypeStruct((CELLS // 2 - SIDES, D), jnp.float32),
+        jax.ShapeDtypeStruct((5, TLON, D), jnp.bfloat16),
+    ]
+    return pl.pallas_call(
+        edges_kernel,
+        in_specs=[VMEM] * (1 + len(arrays)),
+        out_specs=[VMEM] * len(outs),
+        out_shape=outs,
+        compiler_params=pltpu.CompilerParams(vmem_limit_bytes=32 << 20),
+        cost_estimate=scatter_cost(arrived.shape[0]),
+    )(arrived, *arrays)
 
 
 def put_rows(even, odd, rows, tile, west, east):
@@ -261,13 +287,18 @@
     pieces = []
     for a in range(3):
         for source, at in ((odd, 0), (even, 0), (odd, 1)):
-            rows = [source[start + a, at : at + SPAN, :] for start in starts]
+            rows = [source(start + a, at) for start in starts]
             pieces.append(jnp.concatenate(rows, axis=0).astype(jnp.bfloat16))
     strided = jnp.dot(
         jnp.concatenate(pieces, axis=1), weight_ref[...], preferred_element_type=jnp.float32
     )
     coarse = jax.nn.gelu(strided + bias_ref[...]).astype(jnp.bfloat16)
     return coarse.astype(jnp.float32).reshape(len(starts), SPAN, D)
+
+
+def spans(*refs):
+    rows = [(ref, i) for ref in refs for i in range(ref.shape[0])]
+    return lambda i, at: rows[i][0][rows[i][1], at : at + SPAN, :]
 
 
 def finished(coarse, first, count, depth_ref, gain_ref):
@@ -281,27 +312,13 @@
     return (centre * lax.rsqrt(variance + 1e-05) * gain_ref[...]).astype(jnp.bfloat16)
 
 
-def half_kernel(x_ref, half_ref):
-    add_sums(x_ref, half_ref, SLOTS, 0, x_ref.shape[0] // 2)
-
-
-def half_sums(arrived):
-    return pl.pallas_call(
-        half_kernel,
-        in_specs=[VMEM],
-        out_specs=VMEM,
-        out_shape=jax.ShapeDtypeStruct((BINS, CELLS // 2), jnp.float32),
-        compiler_params=pltpu.CompilerParams(vmem_limit_bytes=32 << 20),
-        cost_estimate=scatter_cost(arrived.shape[0]),
-    )(arrived)
-
-
 def inner_kernel(
     x_ref,
     half_ref,
     embed_ref,
     embed_bias_ref,
-    rim_ref,
+    sides_ref,
+    edges_ref,
     west_ref,
     east_ref,
     weight_ref,
@@ -309,6 +326,8 @@
     depth_ref,
     gain_ref,
     _,
+    own_even_ref,
+    own_odd_ref,
     upper_ref,
     lower_ref,
     out_ref,
@@ -318,12 +337,12 @@
     coarse,
 ):
     tiles = x_ref.shape[0]
-    add_sums(x_ref, total, SLOTS, tiles // 2, tiles, half_ref[...])
+    add_sums(x_ref, total, SLOTS, tiles * EARLY // 32, tiles, half_ref[...])
     inside = embedded_cells(total, embed_ref, embed_bias_ref)
     west, east = (r[...].astype(jnp.float32) for r in (west_ref, east_ref))
-    sides = rim_ref[:SIDES].reshape(TLAT, 8, D)
-    edges = rim_ref[SIDES : SIDES + 10 * MID].reshape(5, 2 * MID, D)
-    corner = rim_ref[SIDES + 10 * MID :].reshape(1, 2 * EXTRA, D)
+    sides = sides_ref[...].reshape(TLAT, 8, D)
+    edges = edges_ref[: 10 * MID].reshape(5, 2 * MID, D)
+    corner = edges_ref[10 * MID :].reshape(1, 2 * EXTRA, D)
     bulk = inside[: 20 * MID].reshape(TLAT - 6, 2 * MID, D)
     rest = inside[20 * MID :].reshape(1, 2 * (MID - EXTRA), D)
     even[:, 0:1] = west[:, 1:2]
@@ -343,7 +362,11 @@
         held[2:3, at + 1 : cut] = corner[:, EXTRA * parity : EXTRA * (parity + 1)]
         span = MID - EXTRA
         held[2:3, cut : cut + span] = rest[:, span * parity : span * (parity + 1)]
-    coarse[...] = strided_rows(even, odd, range(1, TLAT - 2, 2), weight_ref, bias_ref)
+    starts = range(1, TLAT - 2, 2)
+    coarse[...] = strided_rows(spans(even), spans(odd), starts, weight_ref, bias_ref)
+    for held, own_ref in ((even, own_even_ref), (odd, own_odd_ref)):
+        own_ref[0:2] = held[0:2]
+        own_ref[2:3] = held[TLAT - 1 :]
     upper_ref[...] = coarse[0:2]
     lower_ref[...] = coarse[ROWS - 3 : ROWS - 1]
     out_ref[...] = finished(coarse, 0, ROWS - 3, depth_ref, gain_ref)
@@ -351,11 +374,12 @@
 
 def inner(arrived, *arrays):
     pair = jax.ShapeDtypeStruct((2, SPAN, D), jnp.float32)
+    owns = [jax.ShapeDtypeStruct((3, n, D), jnp.float32) for n in (SPAN, SPAN + 8)]
     return pl.pallas_call(
         inner_kernel,
         in_specs=[VMEM] * (1 + len(arrays)),
-        out_specs=[VMEM] * 3,
-        out_shape=[pair, pair, jax.ShapeDtypeStruct((ROWS - 3, HALF, D), jnp.bfloat16)],
+        out_specs=[VMEM] * 5,
+        out_shape=owns + [pair, pair, jax.ShapeDtypeStruct((ROWS - 3, HALF, D), jnp.bfloat16)],
         scratch_shapes=[
             pltpu.VMEM((BINS, CELLS // 2), jnp.float32),
             pltpu.VMEM((TLAT, SPAN, D), jnp.float32),
@@ -369,12 +393,11 @@
 
 def outer_kernel(
     place_ref,
+    own_even_ref,
+    own_odd_ref,
     upper_ref,
     lower_ref,
     done_ref,
-    rows_ref,
-    west_ref,
-    east_ref,
     pair_ref,
     other_ref,
     weight_ref,
@@ -382,8 +405,10 @@
     depth_ref,
     gain_ref,
     out_hbm,
-    even,
-    odd,
+    north_even,
+    north_odd,
+    south_even,
+    south_odd,
     coarse,
     top,
     bottom,
@@ -395,27 +420,17 @@
     lower, above, below = (place_ref[i : i + 1] for i in range(3))
     upper = 1.0 - lower
     north = paired * (lower * above) + other * (upper * above)
-    south = paired * upper + other * lower
-    for at, source, rows in ((0, north, slice(0, 3)), (6, south, slice(0, 2))):
-        part = source[rows]
-        put_rows(
-            even,
-            odd,
-            slice(at, at + rows.stop),
-            part[:, :TLON],
-            part[:, TLON : TLON + 3],
-            part[:, TLON + 3 :],
-        )
-    for at, rows, own in ((3, slice(0, 2), slice(0, 2)), (5, slice(TLAT - 1, TLAT), slice(4, 5))):
-        put_rows(
-            even,
-            odd,
-            slice(at, at + rows.stop - rows.start),
-            rows_ref[own].astype(jnp.float32),
-            west_ref[rows].astype(jnp.float32),
-            east_ref[rows].astype(jnp.float32),
-        )
-    edge = strided_rows(even, odd, (0, 2, 5), weight_ref, bias_ref)
+    south = (paired * upper + other * lower)[:2]
+    for even, odd, part in ((north_even, north_odd, north), (south_even, south_odd, south)):
+        west, east = part[:, TLON : TLON + 3], part[:, TLON + 3 :]
+        put_rows(even, odd, slice(0, part.shape[0]), part[:, :TLON], west, east)
+    edge = strided_rows(
+        spans(north_even, own_even_ref, south_even),
+        spans(north_odd, own_odd_ref, south_odd),
+        (0, 2, 5),
+        weight_ref,
+        bias_ref,
+    )
     coarse[0] = edge[0] * above
     coarse[1] = edge[1]
     coarse[2:4] = upper_ref[...]
@@ -441,8 +456,10 @@
         out_specs=ANY,
         out_shape=jax.ShapeDtypeStruct((ROWS, HALF, D), jnp.bfloat16),
         scratch_shapes=[
-            pltpu.VMEM((8, SPAN, D), jnp.float32),
-            pltpu.VMEM((8, SPAN + 8, D), jnp.float32),
+            pltpu.VMEM((3, SPAN, D), jnp.float32),
+            pltpu.VMEM((3, SPAN + 8, D), jnp.float32),
+            pltpu.VMEM((2, SPAN, D), jnp.float32),
+            pltpu.VMEM((2, SPAN + 8, D), jnp.float32),
             pltpu.VMEM((7, SPAN, D), jnp.float32),
             pltpu.VMEM((2, HALF, D), jnp.bfloat16),
             pltpu.VMEM((1, HALF, D), jnp.bfloat16),
@@ -472,12 +489,12 @@
     packed, lower, above, below = lax.optimization_barrier((packed, lower, above, below))
     arrived = lax.all_to_all(packed, ("lon", "lat"), split_axis=0, concat_axis=0, tiled=True)
     embed = embed_bias.reshape(1, D)
-    rim, rows, last, first = rim_cells(arrived, embed_weight, embed)
-    rows, lower, above, below = lax.optimization_barrier((rows, lower, above, below))
+    side_cells, sums, last, first = sides(arrived, embed_weight, embed)
+    sums, lower, above, below = lax.optimization_barrier((sums, lower, above, below))
+    half, edge_cells, rows = edges(arrived, embed_weight, embed, side_cells, sums)
     ring = [(i, (i + 1) % lon_count) for i in range(lon_count)]
     west = lax.ppermute(last, "lon", ring)
     east = lax.ppermute(first, "lon", [(j, i) for i, j in ring])
-    half = half_sums(arrived)
     weight, bias = stride_weight.reshape(9 * D, D), stride_bias.reshape(1, D)
     top = jnp.concatenate([rows[:3], west[:3], east[:3]], axis=1)
     bottom = jnp.concatenate([rows[2:], west[TLAT - 3 :], east[TLAT - 3 :]], axis=1)
@@ -494,11 +511,21 @@
     flags = jnp.where(index == 0, lower, jnp.where(index == 1, above, below))
     place = flags.astype(jnp.float32)
     inside = inner(
-        arrived, half, embed_weight, embed, rim, west, east, weight, bias, depth_weight, gain, place
-    )
-    return outer(
-        place, *inside, rows, west, east, paired, other, weight, bias, depth_weight, gain
-    )
+        arrived,
+        half,
+        embed_weight,
+        embed,
+        side_cells,
+        edge_cells,
+        west,
+        east,
+        weight,
+        bias,
+        depth_weight,
+        gain,
+        place,
+    )
+    return outer(place, *inside, paired, other, weight, bias, depth_weight, gain)
 
 
 def solution(mesh):

time: 39 us -> 38.9 us (level)
  no operation moved by 1% of the time
where the time goes in v6:
time: 38.9 us; the launch traced here: 38.7 us
  blocking collectives  23.2 us (60%)
  Pallas kernels  8.39 us (22%)
  starting transfers between devices  6.01 us (15%)
  waiting for transfers between devices  0.84 us (2%)
    all_to_all x1, blocking collectives, on_device(): lax.all_to_all(packed, ('lon', 'lat'), split_axis=0, concat_axis=0, tiled...  23.2 us
    ppermute x1, starting transfers between devices, on_device(): east = lax.ppermute(first, 'lon', [(j, i) for i, j in ring])  3.43 us
    pallas_call x1, Pallas kernels, inner(): pl.pallas_call(inner_kernel, in_specs=[VMEM] * (1 + len(arrays)), out_spe...  2.23 us
    pallas_call x1, Pallas kernels, sides(): pl.pallas_call(sides_kernel, in_specs=[VMEM] * 3, out_specs=[VMEM] * len(...  2.15 us
    pallas_call x1, Pallas kernels, pack(): pl.pallas_call(pack_kernel, in_specs=[ANY] * len(arrays), out_specs=VMEM,...  1.48 us
    ppermute x1, starting transfers between devices, on_device(): west = lax.ppermute(last, 'lon', ring)  1.35 us
    pallas_call x1, Pallas kernels, edges(): pl.pallas_call(edges_kernel, in_specs=[VMEM] * (1 + len(arrays)), out_spe...  1.31 us
    pallas_call x1, Pallas kernels, outer(): pl.pallas_call(outer_kernel, in_specs=[VMEM] * len(arrays), out_specs=ANY...  1.23 us
  transfers between devices with their start and end apart: 4, of which 3 were waited for; matrix products, arithmetic and copies ran while one was open for 0% of the time, Pallas kernels for 9%

profile of v6, /device:TPU:0, one launch (start us, length us, event | category | flops | bytes accessed | tf_op | source)
XLA Modules:
  0.0 38.7 jit_solution(2990420162317920016)
XLA Ops:
  0.0 0.0 copy-start.4
  0.0 0.0 copy-start.5
  0.0 1.5 %shard_map.109 = bf16[32,17,4,128]{3,2,1,0:T(4,128)(2,1)S(1)} custom-call(s32[1,32]{1,0:T(1,128)} %count_hbm.1, bf16[31,32,256]{2,1,0:T(8,128)(2,1)} %bitcast.14, f32[32,2,256]{2,1,0:T(2,128)} %offset_hbm.1, s32[32,256]{1,0:T(8,128)} %cell_hbm.1, s32[32,256]{1,0:T(8,128)} %slot_hbm.1), custom_call_target="tpu_custom_call" | custom-call | tf_op jit(solution)/shard_map/pallas_call | solution.py:130
  1.5 23.2 %all_to_all.5.x_ref = bf16[32,17,4,128]{3,2,1,0:T(4,128)(2,1)S(1)} all-to-all(bf16[32,17,4,128]{3,2,1,0:T(4,128)(2,1)S(1)} %shard_map.109), channel_id=1, replica_groups=mesh['lon'=8,'lat'=4] {'lon','lat'}, dimensions={0} | all-to-all | bytes 1114112 | tf_op jit(solution)/shard_map/all_to_all | solution.py:490
  24.7 0.0 copy-done.4
  24.7 0.0 copy-done.5
  24.7 2.2 %shard_map.110 = (f32[128,256]{1,0:T(8,128)S(1)}, f32[384,128]{1,0:T(8,128)S(1)}, bf16[16,3,256]{2,1,0:T(4,128)(2,1)S(1)}, bf16[16,2,256]{2,1,0:T(2,128)(2,1)S(1)}) custom-call(bf16[32,17,4,128]{3,2,1,0:T(4,128)(2,1)S(1)} %all_to_all.5.x_ref, bf16[384,256]{1,0:T(8,128)(2,1)S(1)} %copy-done.4, f32[1,256]{1,0:T(1,128)S(1)} %bitcast.11), custom_call_target="tpu_custom_call" | custom-call | flops 1610612736 | bytes 4194304 | tf_op jit(solution)/shard_map/pallas_call | solution.py:249
  26.9 1.3 %collective-permute-start = (bf16[16,3,256]{2,1,0:T(4,128)(2,1)S(1)}, bf16[16,3,256]{2,1,0:T(4,128)(2,1)S(1)}, u32[]{:S(2)}, u32[]{:S(2)}) collective-permute-start(bf16[16,3,256]{2,1,0:T(4,128)(2,1)S(1)} %get-tuple-element.37), channel_id=1, source_target_pairs={{0,4},{4,8},{8,12},{12,16},{16,20},{20,24},{24,28},{28,0},{1,5},{5... | collective-permute-start | bytes 73736 | tf_op jit(solution)/shard_map/ppermute | solution.py:496
  28.2 3.4 %collective-permute-start.1 = (bf16[16,2,256]{2,1,0:T(2,128)(2,1)S(1)}, bf16[16,2,256]{2,1,0:T(2,128)(2,1)S(1)}, u32[]{:S(2)}, u32[]{:S(2)}) collective-permute-start(bf16[16,2,256]{2,1,0:T(2,128)(2,1)S(1)} %get-tuple-element.38), channel_id=1, source_target_pairs={{4,0},{8,4},{12,8},{16,12},{20,16},{24,20},{28,24},{0,28},{5,1},{9... | collective-permute-start | bytes 49160 | tf_op jit(solution)/shard_map/ppermute | solution.py:497
  31.7 0.0 copy-start
  31.7 0.0 copy-start.1
  31.7 0.0 copy-start.2
  31.7 0.0 copy-start.3
  31.7 1.3 %shard_map.111 = (f32[384,256]{1,0:T(8,128)S(1)}, f32[128,256]{1,0:T(8,128)S(1)}, bf16[5,32,256]{2,1,0:T(8,128)(2,1)S(1)}) custom-call(bf16[32,17,4,128]{3,2,1,0:T(4,128)(2,1)S(1)} %all_to_all.5.x_ref, bf16[384,256]{1,0:T(8,128)(2,1)S(1)} %copy-done.4, f32[1,256]{1,0:T(1,128)S(1)} %bitcast.12, f32[128,256]{1,0:T(8,128)S(1)} %get-tuple-element.33.sides_ref, ...), custom_call_target="tpu_custom_call" | custom-call | flops 1610612736 | bytes 4194304 | tf_op jit(solution)/shard_map/pallas_call | solution.py:266
  33.0 0.1 collective-permute-done.1.east_ref
  33.1 0.4 %collective-permute-done.west_ref = bf16[16,3,256]{2,1,0:T(4,128)(2,1)S(1)} collective-permute-done((bf16[16,3,256]{2,1,0:T(4,128)(2,1)S(1)}, bf16[16,3,256]{2,1,0:T(4,128)(2,1)S(1)}, u32[]{:S(2)}, u32[]{:S(2)}) %collective-permute-start) | collective-permute-done | bytes 24608 | tf_op jit(solution)/shard_map/ppermute | solution.py:496
  33.6 0.1 collective-permute-start.2
  33.7 1.2 %collective-permute-start.3 = (bf16[3,37,256]{2,1,0:T(8,128)(2,1)S(1)}, bf16[3,37,256]{2,1,0:T(8,128)(2,1)S(1)}, u32[]{:S(2)}, u32[]{:S(2)}) collective-permute-start(bf16[3,37,256]{2,1,0:T(8,128)(2,1)S(1)} %get-tuple-element.45), channel_id=1, source_target_pairs={{1,2},{3,0},{2,1},{0,3},{5,6},{7,4},{6,5},{4,7},{9,10},{11,8},{10,... | collective-permute-start | bytes 170504 | tf_op jit(solution)/shard_map/ppermute | solution.py:506
  34.9 0.1 iota.10._.place_ref
  34.9 0.0 copy-done
  34.9 0.0 copy-done.1
  34.9 0.0 copy-done.2
  34.9 0.0 copy-done.3
  34.9 2.2 %shard_map.112 = (f32[3,24,256]{2,1,0:T(8,128)S(1)}, f32[3,32,256]{2,1,0:T(8,128)S(1)}, f32[2,24,256]{2,1,0:T(8,128)S(1)}, f32[2,24,256]{2,1,0:T(8,128)S(1)}, bf16[5,16,256]{2,1,0:T(8,128)(2,1)S(1)}) custom-call(bf16[32,17,4,128]{3,2,1,0:T(4,128)(2,1)S(1)} %all_to_all.5.x_ref, f32[384,256]{1,0:T(8,128)S(1)} %get-tuple-element.35.half_ref, ...), custom_call_target="tpu_custom_call" | custom-call | flops 1610612736 | bytes 4194304 | tf_op jit(solution)/shard_map/pallas_call | solution.py:378
  37.2 0.0 collective-permute-done.2.pair_ref
  37.2 0.3 collective-permute-done.3.other_ref
  37.5 1.2 %shard_map.113 = bf16[8,16,256]{2,1,0:T(8,128)(2,1)} custom-call(f32[3,256]{1,0:T(4,128)S(1)} %iota.10._.place_ref, f32[3,24,256]{2,1,0:T(8,128)S(1)} %get-tuple-element.39.own_even_ref, f32[3,32,256]{2,1,0:T(8,128)S(1)} %get-tuple-element.40.own_odd_ref, f32[2,24,256]{2,1,0:T(8,128)S(1)} %get-tuple-element.41.upper_ref, ...), custom_call_target="tpu_custom_call" | custom-call | tf_op jit(solution)/shard_map/pallas_call | solution.py:453
  (5 shorter events, 0.1 us)
Async XLA Ops:
  0.0 24.7 %copy-start.4 = (bf16[384,256]{1,0:T(8,128)(2,1)S(1)}, bf16[384,256]{1,0:T(8,128)(2,1)}, u32[]{:S(2)}) copy-start(bf16[384,256]{1,0:T(8,128)(2,1)} %embed_ref.1) | copy-start | bytes 589828
  0.0 24.7 %copy-start.5 = (f32[256]{0:T(256)S(1)}, f32[256]{0:T(256)}, u32[]{:S(2)}) copy-start(f32[256]{0:T(256)} %param.17) | copy-start | bytes 3076
  26.9 6.7 %collective-permute-start = (bf16[16,3,256]{2,1,0:T(4,128)(2,1)S(1)}, bf16[16,3,256]{2,1,0:T(4,128)(2,1)S(1)}, u32[]{:S(2)}, u32[]{:S(2)}) collective-permute-start(bf16[16,3,256]{2,1,0:T(4,128)(2,1)S(1)} %get-tuple-element.37), channel_id=1, source_target_pairs={{0,4},{4,8},{8,12},{12,16},{16,20},{20,24},{24,28},{28,0},{1,5},{5... | collective-permute-start | bytes 73736 | tf_op jit(solution)/shard_map/ppermute | solution.py:496
  28.2 4.9 %collective-permute-start.1 = (bf16[16,2,256]{2,1,0:T(2,128)(2,1)S(1)}, bf16[16,2,256]{2,1,0:T(2,128)(2,1)S(1)}, u32[]{:S(2)}, u32[]{:S(2)}) collective-permute-start(bf16[16,2,256]{2,1,0:T(2,128)(2,1)S(1)} %get-tuple-element.38), channel_id=1, source_target_pairs={{4,0},{8,4},{12,8},{16,12},{20,16},{24,20},{28,24},{0,28},{5,1},{9... | collective-permute-start | bytes 49160 | tf_op jit(solution)/shard_map/ppermute | solution.py:497
  31.7 3.3 %copy-start = (bf16[9,256,256]{2,1,0:T(8,128)(2,1)S(1)}, bf16[9,256,256]{2,1,0:T(8,128)(2,1)}, u32[]{:S(2)}) copy-start(bf16[9,256,256]{2,1,0:T(8,128)(2,1)} %param.18) | copy-start | bytes 3538948
  31.7 3.3 %copy-start.1 = (f32[9,256]{1,0:T(8,128)S(1)}, f32[9,256]{1,0:T(8,128)}, u32[]{:S(2)}) copy-start(f32[9,256]{1,0:T(8,128)} %depth_ref.3) | copy-start | bytes 27652
  31.7 3.3 %copy-start.2 = (f32[256]{0:T(256)S(1)}, f32[256]{0:T(256)}, u32[]{:S(2)}) copy-start(f32[256]{0:T(256)} %param.19) | copy-start | bytes 3076
  31.7 3.3 %copy-start.3 = (f32[256]{0:T(256)S(1)}, f32[256]{0:T(256)}, u32[]{:S(2)}) copy-start(f32[256]{0:T(256)} %param.21) | copy-start | bytes 3076
  33.6 3.6 %collective-permute-start.2 = (bf16[3,37,256]{2,1,0:T(8,128)(2,1)S(1)}, bf16[3,37,256]{2,1,0:T(8,128)(2,1)S(1)}, u32[]{:S(2)}, u32[]{:S(2)}) collective-permute-start(bf16[3,37,256]{2,1,0:T(8,128)(2,1)S(1)} %get-tuple-element.46), channel_id=1, source_target_pairs={{0,1},{2,3},{1,0},{3,2},{4,5},{6,7},{5,4},{7,6},{8,9},{10,11},{9,8... | collective-permute-start | bytes 170504 | tf_op jit(solution)/shard_map/ppermute | solution.py:503
  33.7 3.8 %collective-permute-start.3 = (bf16[3,37,256]{2,1,0:T(8,128)(2,1)S(1)}, bf16[3,37,256]{2,1,0:T(8,128)(2,1)S(1)}, u32[]{:S(2)}, u32[]{:S(2)}) collective-permute-start(bf16[3,37,256]{2,1,0:T(8,128)(2,1)S(1)} %get-tuple-element.45), channel_id=1, source_target_pairs={{1,2},{3,0},{2,1},{0,3},{5,6},{7,4},{6,5},{4,7},{9,10},{11,8},{10,... | collective-permute-start | bytes 170504 | tf_op jit(solution)/shard_map/ppermute | solution.py:506

commit v7 on v6

--- a/solution.py
+++ b/solution.py
@@ -20,7 +20,7 @@
 GROUP = 16
 TILE = 4
 CHUNK = 32
-EARLY = 20
+EARLY = 18
 SPAN = 24
 CELLS = TLAT * TLON
 MID = 12
@@ -66,7 +66,7 @@
     tiles, capacity = cell.shape
     halves = capacity // LANES
     used = out.shape[1] * TILE
-    stride = rows.shape[0] // tiles
+    stride = rows.shape[0] // (tiles + 1)
     groups = tiles // GROUP
 
     def at(j):
@@ -134,7 +134,7 @@
         out_shape=pltpu.VMEM(shape, jnp.bfloat16),
         scratch_shapes=[pltpu.VMEM(a.shape, a.dtype) for a in arrays]
         + [
-            pltpu.VMEM((tiles * stride, LANES), jnp.float32),
+            pltpu.VMEM(((tiles + 1) * stride, LANES), jnp.float32),
             pltpu.SemaphoreType.DMA((tiles // GROUP + 4,)),
         ],
         compiler_params=pltpu.CompilerParams(vmem_limit_bytes=24 << 20),
@@ -398,8 +398,8 @@
     upper_ref,
     lower_ref,
     done_ref,
+    other_ref,
     pair_ref,
-    other_ref,
     weight_ref,
     bias_ref,
     depth_ref,
@@ -525,7 +525,7 @@
         gain,
         place,
     )
-    return outer(place, *inside, paired, other, weight, bias, depth_weight, gain)
+    return outer(place, *inside, other, paired, weight, bias, depth_weight, gain)
 
 
 def solution(mesh):

time: 38.9 us -> 39 us (level)
    ppermute x1, starting transfers between devices: 1.16 us -> 0.07 us  [on_device(): lax.ppermute(jnp.where(lower, bottom, top), 'lat', others + [(j, i) for i...]
    ppermute x1, starting transfers between devices: 0.07 us -> 1.15 us  [on_device(): lax.ppermute(jnp.where(lower, top, bottom), 'lat', pairs + [(j, i) for i,...]
where the time goes in v7:
time: 39 us; the launch traced here: 38.8 us
  blocking collectives  23.2 us (59%)
  Pallas kernels  8.35 us (21%)
  starting transfers between devices  6 us (15%)
  waiting for transfers between devices  0.97 us (2%)
    all_to_all x1, blocking collectives, on_device(): lax.all_to_all(packed, ('lon', 'lat'), split_axis=0, concat_axis=0, tiled...  23.2 us
    ppermute x1, starting transfers between devices, on_device(): east = lax.ppermute(first, 'lon', [(j, i) for i, j in ring])  3.43 us
    pallas_call x1, Pallas kernels, inner(): pl.pallas_call(inner_kernel, in_specs=[VMEM] * (1 + len(arrays)), out_spe...  2.33 us
    pallas_call x1, Pallas kernels, sides(): pl.pallas_call(sides_kernel, in_specs=[VMEM] * 3, out_specs=[VMEM] * len(...  2.14 us
    pallas_call x1, Pallas kernels, pack(): pl.pallas_call(pack_kernel, in_specs=[ANY] * len(arrays), out_specs=VMEM,...  1.46 us
    ppermute x1, starting transfers between devices, on_device(): west = lax.ppermute(last, 'lon', ring)  1.35 us
    pallas_call x1, Pallas kernels, outer(): pl.pallas_call(outer_kernel, in_specs=[VMEM] * len(arrays), out_specs=ANY...  1.22 us
    pallas_call x1, Pallas kernels, edges(): pl.pallas_call(edges_kernel, in_specs=[VMEM] * (1 + len(arrays)), out_spe...  1.19 us
  transfers between devices with their start and end apart: 4, of which 3 were waited for; matrix products, arithmetic and copies ran while one was open for 0% of the time, Pallas kernels for 9%

profile of v7, /device:TPU:0, one launch (start us, length us, event | category | flops | bytes accessed | tf_op | source)
XLA Modules:
  0.0 38.8 jit_solution(9807841372246024269)
XLA Ops:
  0.0 0.0 copy-start.4
  0.0 0.0 copy-start.5
  0.0 1.5 %shard_map.109 = bf16[32,17,4,128]{3,2,1,0:T(4,128)(2,1)S(1)} custom-call(s32[1,32]{1,0:T(1,128)} %count_hbm.1, bf16[31,32,256]{2,1,0:T(8,128)(2,1)} %bitcast.14, f32[32,2,256]{2,1,0:T(2,128)} %offset_hbm.1, s32[32,256]{1,0:T(8,128)} %cell_hbm.1, s32[32,256]{1,0:T(8,128)} %slot_hbm.1), custom_call_target="tpu_custom_call" | custom-call | tf_op jit(solution)/shard_map/pallas_call | solution.py:130
  1.5 23.2 %all_to_all.5.x_ref = bf16[32,17,4,128]{3,2,1,0:T(4,128)(2,1)S(1)} all-to-all(bf16[32,17,4,128]{3,2,1,0:T(4,128)(2,1)S(1)} %shard_map.109), channel_id=1, replica_groups=mesh['lon'=8,'lat'=4] {'lon','lat'}, dimensions={0} | all-to-all | bytes 1114112 | tf_op jit(solution)/shard_map/all_to_all | solution.py:490
  24.7 0.0 copy-done.4
  24.7 0.0 copy-done.5
  24.7 2.1 %shard_map.110 = (f32[128,256]{1,0:T(8,128)S(1)}, f32[384,128]{1,0:T(8,128)S(1)}, bf16[16,3,256]{2,1,0:T(4,128)(2,1)S(1)}, bf16[16,2,256]{2,1,0:T(2,128)(2,1)S(1)}) custom-call(bf16[32,17,4,128]{3,2,1,0:T(4,128)(2,1)S(1)} %all_to_all.5.x_ref, bf16[384,256]{1,0:T(8,128)(2,1)S(1)} %copy-done.4, f32[1,256]{1,0:T(1,128)S(1)} %bitcast.11), custom_call_target="tpu_custom_call" | custom-call | flops 1610612736 | bytes 4194304 | tf_op jit(solution)/shard_map/pallas_call | solution.py:249
  26.9 1.3 %collective-permute-start = (bf16[16,3,256]{2,1,0:T(4,128)(2,1)S(1)}, bf16[16,3,256]{2,1,0:T(4,128)(2,1)S(1)}, u32[]{:S(2)}, u32[]{:S(2)}) collective-permute-start(bf16[16,3,256]{2,1,0:T(4,128)(2,1)S(1)} %get-tuple-element.37), channel_id=1, source_target_pairs={{0,4},{4,8},{8,12},{12,16},{16,20},{20,24},{24,28},{28,0},{1,5},{5... | collective-permute-start | bytes 73736 | tf_op jit(solution)/shard_map/ppermute | solution.py:496
  28.2 3.4 %collective-permute-start.1 = (bf16[16,2,256]{2,1,0:T(2,128)(2,1)S(1)}, bf16[16,2,256]{2,1,0:T(2,128)(2,1)S(1)}, u32[]{:S(2)}, u32[]{:S(2)}) collective-permute-start(bf16[16,2,256]{2,1,0:T(2,128)(2,1)S(1)} %get-tuple-element.38), channel_id=1, source_target_pairs={{4,0},{8,4},{12,8},{16,12},{20,16},{24,20},{28,24},{0,28},{5,1},{9... | collective-permute-start | bytes 49160 | tf_op jit(solution)/shard_map/ppermute | solution.py:497
  31.6 0.0 copy-start
  31.7 0.0 copy-start.1
  31.7 0.0 copy-start.2
  31.7 0.0 copy-start.3
  31.7 1.2 %shard_map.111 = (f32[384,256]{1,0:T(8,128)S(1)}, f32[128,256]{1,0:T(8,128)S(1)}, bf16[5,32,256]{2,1,0:T(8,128)(2,1)S(1)}) custom-call(bf16[32,17,4,128]{3,2,1,0:T(4,128)(2,1)S(1)} %all_to_all.5.x_ref, bf16[384,256]{1,0:T(8,128)(2,1)S(1)} %copy-done.4, f32[1,256]{1,0:T(1,128)S(1)} %bitcast.12, f32[128,256]{1,0:T(8,128)S(1)} %get-tuple-element.33.sides_ref, ...), custom_call_target="tpu_custom_call" | custom-call | flops 1610612736 | bytes 4194304 | tf_op jit(solution)/shard_map/pallas_call | solution.py:266
  32.9 0.2 collective-permute-done.1.east_ref
  33.1 0.4 %collective-permute-done.west_ref = bf16[16,3,256]{2,1,0:T(4,128)(2,1)S(1)} collective-permute-done((bf16[16,3,256]{2,1,0:T(4,128)(2,1)S(1)}, bf16[16,3,256]{2,1,0:T(4,128)(2,1)S(1)}, u32[]{:S(2)}, u32[]{:S(2)}) %collective-permute-start) | collective-permute-done | bytes 24608 | tf_op jit(solution)/shard_map/ppermute | solution.py:496
  33.6 0.1 collective-permute-start.2
  33.7 1.2 %collective-permute-start.3 = (bf16[3,37,256]{2,1,0:T(8,128)(2,1)S(1)}, bf16[3,37,256]{2,1,0:T(8,128)(2,1)S(1)}, u32[]{:S(2)}, u32[]{:S(2)}) collective-permute-start(bf16[3,37,256]{2,1,0:T(8,128)(2,1)S(1)} %get-tuple-element.45), channel_id=1, source_target_pairs={{0,1},{2,3},{1,0},{3,2},{4,5},{6,7},{5,4},{7,6},{8,9},{10,11},{9,8... | collective-permute-start | bytes 170504 | tf_op jit(solution)/shard_map/ppermute | solution.py:503
  34.8 0.1 iota.10._.place_ref
  34.9 0.0 copy-done
  34.9 0.0 copy-done.1
  34.9 0.0 copy-done.2
  34.9 0.0 copy-done.3
  34.9 2.3 %shard_map.112 = (f32[3,24,256]{2,1,0:T(8,128)S(1)}, f32[3,32,256]{2,1,0:T(8,128)S(1)}, f32[2,24,256]{2,1,0:T(8,128)S(1)}, f32[2,24,256]{2,1,0:T(8,128)S(1)}, bf16[5,16,256]{2,1,0:T(8,128)(2,1)S(1)}) custom-call(bf16[32,17,4,128]{3,2,1,0:T(4,128)(2,1)S(1)} %all_to_all.5.x_ref, f32[384,256]{1,0:T(8,128)S(1)} %get-tuple-element.35.half_ref, ...), custom_call_target="tpu_custom_call" | custom-call | flops 1610612736 | bytes 4194304 | tf_op jit(solution)/shard_map/pallas_call | solution.py:378
  37.2 0.3 collective-permute-done.2.other_ref
  37.6 0.0 collective-permute-done.3.pair_ref
  37.6 1.2 %shard_map.113 = bf16[8,16,256]{2,1,0:T(8,128)(2,1)} custom-call(f32[3,256]{1,0:T(4,128)S(1)} %iota.10._.place_ref, f32[3,24,256]{2,1,0:T(8,128)S(1)} %get-tuple-element.39.own_even_ref, f32[3,32,256]{2,1,0:T(8,128)S(1)} %get-tuple-element.40.own_odd_ref, f32[2,24,256]{2,1,0:T(8,128)S(1)} %get-tuple-element.41.upper_ref, ...), custom_call_target="tpu_custom_call" | custom-call | tf_op jit(solution)/shard_map/pallas_call | solution.py:453
  (5 shorter events, 0.1 us)
Async XLA Ops:
  0.0 24.7 %copy-start.4 = (bf16[384,256]{1,0:T(8,128)(2,1)S(1)}, bf16[384,256]{1,0:T(8,128)(2,1)}, u32[]{:S(2)}) copy-start(bf16[384,256]{1,0:T(8,128)(2,1)} %embed_ref.1) | copy-start | bytes 589828
  0.0 24.7 %copy-start.5 = (f32[256]{0:T(256)S(1)}, f32[256]{0:T(256)}, u32[]{:S(2)}) copy-start(f32[256]{0:T(256)} %param.17) | copy-start | bytes 3076
  26.9 6.7 %collective-permute-start = (bf16[16,3,256]{2,1,0:T(4,128)(2,1)S(1)}, bf16[16,3,256]{2,1,0:T(4,128)(2,1)S(1)}, u32[]{:S(2)}, u32[]{:S(2)}) collective-permute-start(bf16[16,3,256]{2,1,0:T(4,128)(2,1)S(1)} %get-tuple-element.37), channel_id=1, source_target_pairs={{0,4},{4,8},{8,12},{12,16},{16,20},{20,24},{24,28},{28,0},{1,5},{5... | collective-permute-start | bytes 73736 | tf_op jit(solution)/shard_map/ppermute | solution.py:496
  28.2 4.9 %collective-permute-start.1 = (bf16[16,2,256]{2,1,0:T(2,128)(2,1)S(1)}, bf16[16,2,256]{2,1,0:T(2,128)(2,1)S(1)}, u32[]{:S(2)}, u32[]{:S(2)}) collective-permute-start(bf16[16,2,256]{2,1,0:T(2,128)(2,1)S(1)} %get-tuple-element.38), channel_id=1, source_target_pairs={{4,0},{8,4},{12,8},{16,12},{20,16},{24,20},{28,24},{0,28},{5,1},{9... | collective-permute-start | bytes 49160 | tf_op jit(solution)/shard_map/ppermute | solution.py:497
  31.6 3.2 %copy-start = (bf16[9,256,256]{2,1,0:T(8,128)(2,1)S(1)}, bf16[9,256,256]{2,1,0:T(8,128)(2,1)}, u32[]{:S(2)}) copy-start(bf16[9,256,256]{2,1,0:T(8,128)(2,1)} %param.18) | copy-start | bytes 3538948
  31.7 3.2 %copy-start.1 = (f32[9,256]{1,0:T(8,128)S(1)}, f32[9,256]{1,0:T(8,128)}, u32[]{:S(2)}) copy-start(f32[9,256]{1,0:T(8,128)} %depth_ref.3) | copy-start | bytes 27652
  31.7 3.2 %copy-start.2 = (f32[256]{0:T(256)S(1)}, f32[256]{0:T(256)}, u32[]{:S(2)}) copy-start(f32[256]{0:T(256)} %param.19) | copy-start | bytes 3076
  31.7 3.2 %copy-start.3 = (f32[256]{0:T(256)S(1)}, f32[256]{0:T(256)}, u32[]{:S(2)}) copy-start(f32[256]{0:T(256)} %param.21) | copy-start | bytes 3076
  33.6 4.0 %collective-permute-start.2 = (bf16[3,37,256]{2,1,0:T(8,128)(2,1)S(1)}, bf16[3,37,256]{2,1,0:T(8,128)(2,1)S(1)}, u32[]{:S(2)}, u32[]{:S(2)}) collective-permute-start(bf16[3,37,256]{2,1,0:T(8,128)(2,1)S(1)} %get-tuple-element.46), channel_id=1, source_target_pairs={{1,2},{3,0},{2,1},{0,3},{5,6},{7,4},{6,5},{4,7},{9,10},{11,8},{10,... | collective-permute-start | bytes 170504 | tf_op jit(solution)/shard_map/ppermute | solution.py:506
  33.7 3.9 %collective-permute-start.3 = (bf16[3,37,256]{2,1,0:T(8,128)(2,1)S(1)}, bf16[3,37,256]{2,1,0:T(8,128)(2,1)S(1)}, u32[]{:S(2)}, u32[]{:S(2)}) collective-permute-start(bf16[3,37,256]{2,1,0:T(8,128)(2,1)S(1)} %get-tuple-element.45), channel_id=1, source_target_pairs={{0,1},{2,3},{1,0},{3,2},{4,5},{6,7},{5,4},{7,6},{8,9},{10,11},{9,8... | collective-permute-start | bytes 170504 | tf_op jit(solution)/shard_map/ppermute | solution.py:503

commit v8 on v7

--- a/solution.py
+++ b/solution.py
@@ -207,10 +207,10 @@
     embedded = embedded_cells(total.at[:, :SIDES], weight_ref, bias_ref)
     sides_ref[...] = embedded
     sides = embedded.reshape(TLAT, 8, D)
-    last = [sides[:, c : c + 1] for c in (6, 3, 7)]
-    first = [sides[:, c : c + 1] for c in (0, 4)]
-    last_ref[...] = jnp.concatenate(last, axis=1).astype(jnp.bfloat16)
-    first_ref[...] = jnp.concatenate(first, axis=1).astype(jnp.bfloat16)
+    for i, c in enumerate((6, 3, 7)):
+        last_ref[i] = sides[:, c, :].astype(jnp.bfloat16)
+    for i, c in enumerate((0, 4)):
+        first_ref[i] = sides[:, c, :].astype(jnp.bfloat16)
 
 
 def edges_kernel(
@@ -243,8 +243,8 @@
     outs = [
         jax.ShapeDtypeStruct((SIDES, D), jnp.float32),
         jax.ShapeDtypeStruct((BINS, CELLS // 2 - SIDES), jnp.float32),
-        jax.ShapeDtypeStruct((TLAT, 3, D), jnp.bfloat16),
-        jax.ShapeDtypeStruct((TLAT, 2, D), jnp.bfloat16),
+        jax.ShapeDtypeStruct((3, TLAT, D), jnp.bfloat16),
+        jax.ShapeDtypeStruct((2, TLAT, D), jnp.bfloat16),
     ]
     return pl.pallas_call(
         sides_kernel,
@@ -345,9 +345,9 @@
     corner = edges_ref[10 * MID :].reshape(1, 2 * EXTRA, D)
     bulk = inside[: 20 * MID].reshape(TLAT - 6, 2 * MID, D)
     rest = inside[20 * MID :].reshape(1, 2 * (MID - EXTRA), D)
-    even[:, 0:1] = west[:, 1:2]
-    odd[:, 0:1] = west[:, 0:1]
-    odd[:, 1:2] = west[:, 2:3]
+    even[:, 0:1] = west[1].reshape(TLAT, 1, D)
+    odd[:, 0:1] = west[0].reshape(TLAT, 1, D)
+    odd[:, 1:2] = west[2].reshape(TLAT, 1, D)
     for parity, held in ((0, even), (1, odd)):
         at = 1 + parity
         mid = slice(at + 1, at + 1 + MID)
@@ -355,7 +355,7 @@
         own = slice(parity * MID, (parity + 1) * MID)
         held[:, at : at + 1] = sides[:, 4 * parity : 4 * parity + 1]
         held[:, at + 1 + MID : at + HALF] = sides[:, 4 * parity + 1 : 4 * parity + 4]
-        held[:, at + HALF : at + HALF + 1] = east[:, parity : parity + 1]
+        held[:, at + HALF : at + HALF + 1] = east[parity].reshape(TLAT, 1, D)
         held[0:2, mid] = edges[0:2, own]
         held[TLAT - 3 :, mid] = edges[2:5, own]
         held[3 : TLAT - 3, mid] = bulk[:, own]
@@ -420,10 +420,17 @@
     lower, above, below = (place_ref[i : i + 1] for i in range(3))
     upper = 1.0 - lower
     north = paired * (lower * above) + other * (upper * above)
-    south = (paired * upper + other * lower)[:2]
+    south = paired * upper + other * lower
     for even, odd, part in ((north_even, north_odd, north), (south_even, south_odd, south)):
-        west, east = part[:, TLON : TLON + 3], part[:, TLON + 3 :]
-        put_rows(even, odd, slice(0, part.shape[0]), part[:, :TLON], west, east)
+        count = even.shape[0]
+        tile = part[: 3 * TLON].reshape(3, TLON, D)[:count]
+        sides = [
+            part[at : at + count].reshape(count, 1, D)
+            for at in range(3 * TLON, 3 * FRAME, 3)
+        ]
+        west = jnp.concatenate(sides[:3], axis=1)
+        east = jnp.concatenate(sides[3:], axis=1)
+        put_rows(even, odd, slice(0, count), tile, west, east)
     edge = strided_rows(
         spans(north_even, own_even_ref, south_even),
         spans(north_odd, own_odd_ref, south_odd),
@@ -496,8 +503,11 @@
     west = lax.ppermute(last, "lon", ring)
     east = lax.ppermute(first, "lon", [(j, i) for i, j in ring])
     weight, bias = stride_weight.reshape(9 * D, D), stride_bias.reshape(1, D)
-    top = jnp.concatenate([rows[:3], west[:3], east[:3]], axis=1)
-    bottom = jnp.concatenate([rows[2:], west[TLAT - 3 :], east[TLAT - 3 :]], axis=1)
+    ends = [slice(0, 3), slice(TLAT - 3, TLAT)]
+    top, bottom = (
+        jnp.concatenate([part.reshape(-1, D) for part in (rows[own], west[:, end], east[:, end])])
+        for own, end in zip((slice(0, 3), slice(2, 5)), ends)
+    )
     pairs = [(i, i + 1) for i in range(0, lat_count - 1, 2)]
     others = [(i, (i + 1) % lat_count) for i in range(1, lat_count, 2)]
     paired = lax.ppermute(

time: 39 us -> 38.8 us (level)
  no operation moved by 1% of the time
where the time goes in v8:
time: 38.8 us; the launch traced here: 38.7 us
  blocking collectives  23.2 us (60%)
  Pallas kernels  8.36 us (22%)
  starting transfers between devices  6 us (15%)
  waiting for transfers between devices  0.75 us (2%)
    all_to_all x1, blocking collectives, on_device(): lax.all_to_all(packed, ('lon', 'lat'), split_axis=0, concat_axis=0, tiled...  23.2 us
    ppermute x1, starting transfers between devices, on_device(): east = lax.ppermute(first, 'lon', [(j, i) for i, j in ring])  3.43 us
    pallas_call x1, Pallas kernels, inner(): pl.pallas_call(inner_kernel, in_specs=[VMEM] * (1 + len(arrays)), out_spe...  2.34 us
    pallas_call x1, Pallas kernels, sides(): pl.pallas_call(sides_kernel, in_specs=[VMEM] * 3, out_specs=[VMEM] * len(...  2.15 us
    pallas_call x1, Pallas kernels, pack(): pl.pallas_call(pack_kernel, in_specs=[ANY] * len(arrays), out_specs=VMEM,...  1.46 us
    ppermute x1, starting transfers between devices, on_device(): west = lax.ppermute(last, 'lon', ring)  1.35 us
    pallas_call x1, Pallas kernels, outer(): pl.pallas_call(outer_kernel, in_specs=[VMEM] * len(arrays), out_specs=ANY...  1.22 us
    pallas_call x1, Pallas kernels, edges(): pl.pallas_call(edges_kernel, in_specs=[VMEM] * (1 + len(arrays)), out_spe...  1.18 us
  transfers between devices with their start and end apart: 4, of which 3 were waited for; matrix products, arithmetic and copies ran while one was open for 0% of the time, Pallas kernels for 9%

profile of v8, /device:TPU:0, one launch (start us, length us, event | category | flops | bytes accessed | tf_op | source)
XLA Modules:
  0.0 38.7 jit_solution(14392194796657182533)
XLA Ops:
  0.0 0.0 copy-start.4
  0.0 0.0 copy-start.5
  0.0 1.5 %shard_map.109 = bf16[32,17,4,128]{3,2,1,0:T(4,128)(2,1)S(1)} custom-call(s32[1,32]{1,0:T(1,128)} %count_hbm.1, bf16[31,32,256]{2,1,0:T(8,128)(2,1)} %bitcast.16, f32[32,2,256]{2,1,0:T(2,128)} %offset_hbm.1, s32[32,256]{1,0:T(8,128)} %cell_hbm.1, s32[32,256]{1,0:T(8,128)} %slot_hbm.1), custom_call_target="tpu_custom_call" | custom-call | tf_op jit(solution)/shard_map/pallas_call | solution.py:130
  1.5 23.2 %all_to_all.5.x_ref = bf16[32,17,4,128]{3,2,1,0:T(4,128)(2,1)S(1)} all-to-all(bf16[32,17,4,128]{3,2,1,0:T(4,128)(2,1)S(1)} %shard_map.109), channel_id=1, replica_groups=mesh['lon'=8,'lat'=4] {'lon','lat'}, dimensions={0} | all-to-all | bytes 1114112 | tf_op jit(solution)/shard_map/all_to_all | solution.py:497
  24.7 0.0 copy-done.4
  24.7 0.0 copy-done.5
  24.7 2.2 %shard_map.110 = (f32[128,256]{1,0:T(8,128)S(1)}, f32[384,128]{1,0:T(8,128)S(1)}, bf16[3,16,256]{2,1,0:T(8,128)(2,1)S(1)}, bf16[2,16,256]{2,1,0:T(8,128)(2,1)S(1)}) custom-call(bf16[32,17,4,128]{3,2,1,0:T(4,128)(2,1)S(1)} %all_to_all.5.x_ref, bf16[384,256]{1,0:T(8,128)(2,1)S(1)} %copy-done.4, f32[1,256]{1,0:T(1,128)S(1)} %bitcast.13), custom_call_target="tpu_custom_call" | custom-call | flops 1610612736 | bytes 4194304 | tf_op jit(solution)/shard_map/pallas_call | solution.py:249
  26.9 1.3 %collective-permute-start = (bf16[3,16,256]{2,1,0:T(8,128)(2,1)S(1)}, bf16[3,16,256]{2,1,0:T(8,128)(2,1)S(1)}, u32[]{:S(2)}, u32[]{:S(2)}) collective-permute-start(bf16[3,16,256]{2,1,0:T(8,128)(2,1)S(1)} %get-tuple-element.37), channel_id=1, source_target_pairs={{0,4},{4,8},{8,12},{12,16},{16,20},{20,24},{24,28},{28,0},{1,5},{5... | collective-permute-start | bytes 73736 | tf_op jit(solution)/shard_map/ppermute | solution.py:503
  28.2 3.4 %collective-permute-start.1 = (bf16[2,16,256]{2,1,0:T(8,128)(2,1)S(1)}, bf16[2,16,256]{2,1,0:T(8,128)(2,1)S(1)}, u32[]{:S(2)}, u32[]{:S(2)}) collective-permute-start(bf16[2,16,256]{2,1,0:T(8,128)(2,1)S(1)} %get-tuple-element.38), channel_id=1, source_target_pairs={{4,0},{8,4},{12,8},{16,12},{20,16},{24,20},{28,24},{0,28},{5,1},{9... | collective-permute-start | bytes 49160 | tf_op jit(solution)/shard_map/ppermute | solution.py:504
  31.7 0.0 copy-start
  31.7 0.0 copy-start.1
  31.7 0.0 copy-start.2
  31.7 0.0 copy-start.3
  31.7 1.2 %shard_map.111 = (f32[384,256]{1,0:T(8,128)S(1)}, f32[128,256]{1,0:T(8,128)S(1)}, bf16[5,32,256]{2,1,0:T(8,128)(2,1)S(1)}) custom-call(bf16[32,17,4,128]{3,2,1,0:T(4,128)(2,1)S(1)} %all_to_all.5.x_ref, bf16[384,256]{1,0:T(8,128)(2,1)S(1)} %copy-done.4, f32[1,256]{1,0:T(1,128)S(1)} %bitcast.14, f32[128,256]{1,0:T(8,128)S(1)} %get-tuple-element.33.sides_ref, ...), custom_call_target="tpu_custom_call" | custom-call | flops 1610612736 | bytes 4194304 | tf_op jit(solution)/shard_map/pallas_call | solution.py:266
  32.9 0.2 collective-permute-done.1.east_ref
  33.1 0.3 collective-permute-done.west_ref
  33.5 0.1 collective-permute-start.2
  33.6 1.2 %collective-permute-start.3 = (bf16[111,256]{1,0:T(8,128)(2,1)S(1)}, bf16[111,256]{1,0:T(8,128)(2,1)S(1)}, u32[]{:S(2)}, u32[]{:S(2)}) collective-permute-start(bf16[111,256]{1,0:T(8,128)(2,1)S(1)} %get-tuple-element.45), channel_id=1, source_target_pairs={{0,1},{2,3},{1,0},{3,2},{4,5},{6,7},{5,4},{7,6},{8,9},{10,11},{9,8... | collective-permute-start | bytes 170504 | tf_op jit(solution)/shard_map/ppermute | solution.py:513
  34.8 0.1 iota.10._.place_ref
  34.8 0.0 copy-done
  34.9 0.0 copy-done.1
  34.9 0.0 copy-done.2
  34.9 0.0 copy-done.3
  34.9 2.3 %shard_map.112 = (f32[3,24,256]{2,1,0:T(8,128)S(1)}, f32[3,32,256]{2,1,0:T(8,128)S(1)}, f32[2,24,256]{2,1,0:T(8,128)S(1)}, f32[2,24,256]{2,1,0:T(8,128)S(1)}, bf16[5,16,256]{2,1,0:T(8,128)(2,1)S(1)}) custom-call(bf16[32,17,4,128]{3,2,1,0:T(4,128)(2,1)S(1)} %all_to_all.5.x_ref, f32[384,256]{1,0:T(8,128)S(1)} %get-tuple-element.35.half_ref, ...), custom_call_target="tpu_custom_call" | custom-call | flops 1610612736 | bytes 4194304 | tf_op jit(solution)/shard_map/pallas_call | solution.py:378
  37.2 0.2 collective-permute-done.2.other_ref
  37.4 0.0 collective-permute-done.3.pair_ref
  37.4 1.2 %shard_map.113 = bf16[8,16,256]{2,1,0:T(8,128)(2,1)} custom-call(f32[3,256]{1,0:T(4,128)S(1)} %iota.10._.place_ref, f32[3,24,256]{2,1,0:T(8,128)S(1)} %get-tuple-element.39.own_even_ref, f32[3,32,256]{2,1,0:T(8,128)S(1)} %get-tuple-element.40.own_odd_ref, f32[2,24,256]{2,1,0:T(8,128)S(1)} %get-tuple-element.41.upper_ref, ...), custom_call_target="tpu_custom_call" | custom-call | tf_op jit(solution)/shard_map/pallas_call | solution.py:460
  (9 shorter events, 0.1 us)
Async XLA Ops:
  0.0 24.7 %copy-start.4 = (bf16[384,256]{1,0:T(8,128)(2,1)S(1)}, bf16[384,256]{1,0:T(8,128)(2,1)}, u32[]{:S(2)}) copy-start(bf16[384,256]{1,0:T(8,128)(2,1)} %embed_ref.1) | copy-start | bytes 589828
  0.0 24.7 %copy-start.5 = (f32[256]{0:T(256)S(1)}, f32[256]{0:T(256)}, u32[]{:S(2)}) copy-start(f32[256]{0:T(256)} %param.17) | copy-start | bytes 3076
  26.9 6.6 %collective-permute-start = (bf16[3,16,256]{2,1,0:T(8,128)(2,1)S(1)}, bf16[3,16,256]{2,1,0:T(8,128)(2,1)S(1)}, u32[]{:S(2)}, u32[]{:S(2)}) collective-permute-start(bf16[3,16,256]{2,1,0:T(8,128)(2,1)S(1)} %get-tuple-element.37), channel_id=1, source_target_pairs={{0,4},{4,8},{8,12},{12,16},{16,20},{20,24},{24,28},{28,0},{1,5},{5... | collective-permute-start | bytes 73736 | tf_op jit(solution)/shard_map/ppermute | solution.py:503
  28.2 4.9 %collective-permute-start.1 = (bf16[2,16,256]{2,1,0:T(8,128)(2,1)S(1)}, bf16[2,16,256]{2,1,0:T(8,128)(2,1)S(1)}, u32[]{:S(2)}, u32[]{:S(2)}) collective-permute-start(bf16[2,16,256]{2,1,0:T(8,128)(2,1)S(1)} %get-tuple-element.38), channel_id=1, source_target_pairs={{4,0},{8,4},{12,8},{16,12},{20,16},{24,20},{28,24},{0,28},{5,1},{9... | collective-permute-start | bytes 49160 | tf_op jit(solution)/shard_map/ppermute | solution.py:504
  31.7 3.2 %copy-start = (bf16[9,256,256]{2,1,0:T(8,128)(2,1)S(1)}, bf16[9,256,256]{2,1,0:T(8,128)(2,1)}, u32[]{:S(2)}) copy-start(bf16[9,256,256]{2,1,0:T(8,128)(2,1)} %param.18) | copy-start | bytes 3538948
  31.7 3.2 %copy-start.1 = (f32[9,256]{1,0:T(8,128)S(1)}, f32[9,256]{1,0:T(8,128)}, u32[]{:S(2)}) copy-start(f32[9,256]{1,0:T(8,128)} %depth_ref.3) | copy-start | bytes 27652
  31.7 3.2 %copy-start.2 = (f32[256]{0:T(256)S(1)}, f32[256]{0:T(256)}, u32[]{:S(2)}) copy-start(f32[256]{0:T(256)} %param.19) | copy-start | bytes 3076
  31.7 3.2 %copy-start.3 = (f32[256]{0:T(256)S(1)}, f32[256]{0:T(256)}, u32[]{:S(2)}) copy-start(f32[256]{0:T(256)} %param.21) | copy-start | bytes 3076
  33.5 3.9 %collective-permute-start.2 = (bf16[111,256]{1,0:T(8,128)(2,1)S(1)}, bf16[111,256]{1,0:T(8,128)(2,1)S(1)}, u32[]{:S(2)}, u32[]{:S(2)}) collective-permute-start(bf16[111,256]{1,0:T(8,128)(2,1)S(1)} %get-tuple-element.46), channel_id=1, source_target_pairs={{1,2},{3,0},{2,1},{0,3},{5,6},{7,4},{6,5},{4,7},{9,10},{11,8},{10,... | collective-permute-start | bytes 170504 | tf_op jit(solution)/shard_map/ppermute | solution.py:516
  33.6 3.8 %collective-permute-start.3 = (bf16[111,256]{1,0:T(8,128)(2,1)S(1)}, bf16[111,256]{1,0:T(8,128)(2,1)S(1)}, u32[]{:S(2)}, u32[]{:S(2)}) collective-permute-start(bf16[111,256]{1,0:T(8,128)(2,1)S(1)} %get-tuple-element.45), channel_id=1, source_target_pairs={{0,1},{2,3},{1,0},{3,2},{4,5},{6,7},{5,4},{7,6},{8,9},{10,11},{9,8... | collective-permute-start | bytes 170504 | tf_op jit(solution)/shard_map/ppermute | solution.py:513

commit v9 on v8

--- a/solution.py
+++ b/solution.py
@@ -20,7 +20,7 @@
 GROUP = 16
 TILE = 4
 CHUNK = 32
-EARLY = 18
+EARLY = 22
 SPAN = 24
 CELLS = TLAT * TLON
 MID = 12

time: 38.8 us -> 38.8 us (level)
  transfers between devices with their start and end apart: 4 -> 4, of which waited for: 3 -> 2; matrix products, arithmetic and copies ran while one was open for 0% -> 0% of each run, Pallas kernels for 9% -> 9%
where the time goes in v9:
time: 38.8 us; the launch traced here: 38.7 us
  blocking collectives  23.2 us (60%)
  Pallas kernels  8.37 us (22%)
  starting transfers between devices  6.01 us (15%)
  waiting for transfers between devices  0.74 us (2%)
    all_to_all x1, blocking collectives, on_device(): lax.all_to_all(packed, ('lon', 'lat'), split_axis=0, concat_axis=0, tiled...  23.2 us
    ppermute x1, starting transfers between devices, on_device(): east = lax.ppermute(first, 'lon', [(j, i) for i, j in ring])  3.43 us
    pallas_call x1, Pallas kernels, sides(): pl.pallas_call(sides_kernel, in_specs=[VMEM] * 3, out_specs=[VMEM] * len(...  2.15 us
    pallas_call x1, Pallas kernels, inner(): pl.pallas_call(inner_kernel, in_specs=[VMEM] * (1 + len(arrays)), out_spe...  2.14 us
    pallas_call x1, Pallas kernels, pack(): pl.pallas_call(pack_kernel, in_specs=[ANY] * len(arrays), out_specs=VMEM,...  1.46 us
    pallas_call x1, Pallas kernels, edges(): pl.pallas_call(edges_kernel, in_specs=[VMEM] * (1 + len(arrays)), out_spe...  1.39 us
    ppermute x1, starting transfers between devices, on_device(): west = lax.ppermute(last, 'lon', ring)  1.35 us
    pallas_call x1, Pallas kernels, outer(): pl.pallas_call(outer_kernel, in_specs=[VMEM] * len(arrays), out_specs=ANY...  1.22 us
  transfers between devices with their start and end apart: 4, of which 2 were waited for; matrix products, arithmetic and copies ran while one was open for 0% of the time, Pallas kernels for 9%

profile of v9, /device:TPU:0, one launch (start us, length us, event | category | flops | bytes accessed | tf_op | source)
XLA Modules:
  0.0 38.7 jit_solution(12461824801057641346)
XLA Ops:
  0.0 0.0 copy-start.4
  0.0 0.0 copy-start.5
  0.0 1.5 %shard_map.109 = bf16[32,17,4,128]{3,2,1,0:T(4,128)(2,1)S(1)} custom-call(s32[1,32]{1,0:T(1,128)} %count_hbm.1, bf16[31,32,256]{2,1,0:T(8,128)(2,1)} %bitcast.16, f32[32,2,256]{2,1,0:T(2,128)} %offset_hbm.1, s32[32,256]{1,0:T(8,128)} %cell_hbm.1, s32[32,256]{1,0:T(8,128)} %slot_hbm.1), custom_call_target="tpu_custom_call" | custom-call | tf_op jit(solution)/shard_map/pallas_call | solution.py:130
  1.5 23.2 %all_to_all.5.x_ref = bf16[32,17,4,128]{3,2,1,0:T(4,128)(2,1)S(1)} all-to-all(bf16[32,17,4,128]{3,2,1,0:T(4,128)(2,1)S(1)} %shard_map.109), channel_id=1, replica_groups=mesh['lon'=8,'lat'=4] {'lon','lat'}, dimensions={0} | all-to-all | bytes 1114112 | tf_op jit(solution)/shard_map/all_to_all | solution.py:497
  24.7 0.0 copy-done.4
  24.7 0.0 copy-done.5
  24.7 2.2 %shard_map.110 = (f32[128,256]{1,0:T(8,128)S(1)}, f32[384,128]{1,0:T(8,128)S(1)}, bf16[3,16,256]{2,1,0:T(8,128)(2,1)S(1)}, bf16[2,16,256]{2,1,0:T(8,128)(2,1)S(1)}) custom-call(bf16[32,17,4,128]{3,2,1,0:T(4,128)(2,1)S(1)} %all_to_all.5.x_ref, bf16[384,256]{1,0:T(8,128)(2,1)S(1)} %copy-done.4, f32[1,256]{1,0:T(1,128)S(1)} %bitcast.13), custom_call_target="tpu_custom_call" | custom-call | flops 1610612736 | bytes 4194304 | tf_op jit(solution)/shard_map/pallas_call | solution.py:249
  26.9 1.3 %collective-permute-start = (bf16[3,16,256]{2,1,0:T(8,128)(2,1)S(1)}, bf16[3,16,256]{2,1,0:T(8,128)(2,1)S(1)}, u32[]{:S(2)}, u32[]{:S(2)}) collective-permute-start(bf16[3,16,256]{2,1,0:T(8,128)(2,1)S(1)} %get-tuple-element.37), channel_id=1, source_target_pairs={{0,4},{4,8},{8,12},{12,16},{16,20},{20,24},{24,28},{28,0},{1,5},{5... | collective-permute-start | bytes 73736 | tf_op jit(solution)/shard_map/ppermute | solution.py:503
  28.2 3.4 %collective-permute-start.1 = (bf16[2,16,256]{2,1,0:T(8,128)(2,1)S(1)}, bf16[2,16,256]{2,1,0:T(8,128)(2,1)S(1)}, u32[]{:S(2)}, u32[]{:S(2)}) collective-permute-start(bf16[2,16,256]{2,1,0:T(8,128)(2,1)S(1)} %get-tuple-element.38), channel_id=1, source_target_pairs={{4,0},{8,4},{12,8},{16,12},{20,16},{24,20},{28,24},{0,28},{5,1},{9... | collective-permute-start | bytes 49160 | tf_op jit(solution)/shard_map/ppermute | solution.py:504
  31.7 0.0 copy-start
  31.7 0.0 copy-start.1
  31.7 0.0 copy-start.2
  31.7 0.0 copy-start.3
  31.7 1.4 %shard_map.111 = (f32[384,256]{1,0:T(8,128)S(1)}, f32[128,256]{1,0:T(8,128)S(1)}, bf16[5,32,256]{2,1,0:T(8,128)(2,1)S(1)}) custom-call(bf16[32,17,4,128]{3,2,1,0:T(4,128)(2,1)S(1)} %all_to_all.5.x_ref, bf16[384,256]{1,0:T(8,128)(2,1)S(1)} %copy-done.4, f32[1,256]{1,0:T(1,128)S(1)} %bitcast.14, f32[128,256]{1,0:T(8,128)S(1)} %get-tuple-element.33.sides_ref, ...), custom_call_target="tpu_custom_call" | custom-call | flops 1610612736 | bytes 4194304 | tf_op jit(solution)/shard_map/pallas_call | solution.py:266
  33.1 0.0 collective-permute-done.1.east_ref
  33.2 0.3 collective-permute-done.west_ref
  33.5 0.2 collective-permute-start.2
  33.8 1.0 %collective-permute-start.3 = (bf16[111,256]{1,0:T(8,128)(2,1)S(1)}, bf16[111,256]{1,0:T(8,128)(2,1)S(1)}, u32[]{:S(2)}, u32[]{:S(2)}) collective-permute-start(bf16[111,256]{1,0:T(8,128)(2,1)S(1)} %get-tuple-element.45), channel_id=1, source_target_pairs={{0,1},{2,3},{1,0},{3,2},{4,5},{6,7},{5,4},{7,6},{8,9},{10,11},{9,8... | collective-permute-start | bytes 170504 | tf_op jit(solution)/shard_map/ppermute | solution.py:513
  34.8 0.1 iota.10._.place_ref
  34.8 0.0 copy-done
  34.9 0.0 copy-done.1
  34.9 0.0 copy-done.2
  34.9 0.0 copy-done.3
  34.9 2.1 %shard_map.112 = (f32[3,24,256]{2,1,0:T(8,128)S(1)}, f32[3,32,256]{2,1,0:T(8,128)S(1)}, f32[2,24,256]{2,1,0:T(8,128)S(1)}, f32[2,24,256]{2,1,0:T(8,128)S(1)}, bf16[5,16,256]{2,1,0:T(8,128)(2,1)S(1)}) custom-call(bf16[32,17,4,128]{3,2,1,0:T(4,128)(2,1)S(1)} %all_to_all.5.x_ref, f32[384,256]{1,0:T(8,128)S(1)} %get-tuple-element.35.half_ref, ...), custom_call_target="tpu_custom_call" | custom-call | flops 1610612736 | bytes 4194304 | tf_op jit(solution)/shard_map/pallas_call | solution.py:378
  37.0 0.4 %collective-permute-done.2.other_ref = bf16[111,256]{1,0:T(8,128)(2,1)S(1)} collective-permute-done((bf16[111,256]{1,0:T(8,128)(2,1)S(1)}, bf16[111,256]{1,0:T(8,128)(2,1)S(1)}, u32[]{:S(2)}, u32[]{:S(2)}) %collective-permute-start.2) | collective-permute-done | bytes 56864 | tf_op jit(solution)/shard_map/ppermute | solution.py:516
  37.4 0.0 collective-permute-done.3.pair_ref
  37.4 1.2 %shard_map.113 = bf16[8,16,256]{2,1,0:T(8,128)(2,1)} custom-call(f32[3,256]{1,0:T(4,128)S(1)} %iota.10._.place_ref, f32[3,24,256]{2,1,0:T(8,128)S(1)} %get-tuple-element.39.own_even_ref, f32[3,32,256]{2,1,0:T(8,128)S(1)} %get-tuple-element.40.own_odd_ref, f32[2,24,256]{2,1,0:T(8,128)S(1)} %get-tuple-element.41.upper_ref, ...), custom_call_target="tpu_custom_call" | custom-call | tf_op jit(solution)/shard_map/pallas_call | solution.py:460
  (9 shorter events, 0.1 us)
Async XLA Ops:
  0.0 24.7 %copy-start.4 = (bf16[384,256]{1,0:T(8,128)(2,1)S(1)}, bf16[384,256]{1,0:T(8,128)(2,1)}, u32[]{:S(2)}) copy-start(bf16[384,256]{1,0:T(8,128)(2,1)} %embed_ref.1) | copy-start | bytes 589828
  0.0 24.7 %copy-start.5 = (f32[256]{0:T(256)S(1)}, f32[256]{0:T(256)}, u32[]{:S(2)}) copy-start(f32[256]{0:T(256)} %param.17) | copy-start | bytes 3076
  26.9 6.6 %collective-permute-start = (bf16[3,16,256]{2,1,0:T(8,128)(2,1)S(1)}, bf16[3,16,256]{2,1,0:T(8,128)(2,1)S(1)}, u32[]{:S(2)}, u32[]{:S(2)}) collective-permute-start(bf16[3,16,256]{2,1,0:T(8,128)(2,1)S(1)} %get-tuple-element.37), channel_id=1, source_target_pairs={{0,4},{4,8},{8,12},{12,16},{16,20},{20,24},{24,28},{28,0},{1,5},{5... | collective-permute-start | bytes 73736 | tf_op jit(solution)/shard_map/ppermute | solution.py:503
  28.2 4.9 %collective-permute-start.1 = (bf16[2,16,256]{2,1,0:T(8,128)(2,1)S(1)}, bf16[2,16,256]{2,1,0:T(8,128)(2,1)S(1)}, u32[]{:S(2)}, u32[]{:S(2)}) collective-permute-start(bf16[2,16,256]{2,1,0:T(8,128)(2,1)S(1)} %get-tuple-element.38), channel_id=1, source_target_pairs={{4,0},{8,4},{12,8},{16,12},{20,16},{24,20},{28,24},{0,28},{5,1},{9... | collective-permute-start | bytes 49160 | tf_op jit(solution)/shard_map/ppermute | solution.py:504
  31.7 3.2 %copy-start = (bf16[9,256,256]{2,1,0:T(8,128)(2,1)S(1)}, bf16[9,256,256]{2,1,0:T(8,128)(2,1)}, u32[]{:S(2)}) copy-start(bf16[9,256,256]{2,1,0:T(8,128)(2,1)} %param.18) | copy-start | bytes 3538948
  31.7 3.2 %copy-start.1 = (f32[9,256]{1,0:T(8,128)S(1)}, f32[9,256]{1,0:T(8,128)}, u32[]{:S(2)}) copy-start(f32[9,256]{1,0:T(8,128)} %depth_ref.3) | copy-start | bytes 27652
  31.7 3.2 %copy-start.2 = (f32[256]{0:T(256)S(1)}, f32[256]{0:T(256)}, u32[]{:S(2)}) copy-start(f32[256]{0:T(256)} %param.19) | copy-start | bytes 3076
  31.7 3.2 %copy-start.3 = (f32[256]{0:T(256)S(1)}, f32[256]{0:T(256)}, u32[]{:S(2)}) copy-start(f32[256]{0:T(256)} %param.21) | copy-start | bytes 3076
  33.5 3.9 %collective-permute-start.2 = (bf16[111,256]{1,0:T(8,128)(2,1)S(1)}, bf16[111,256]{1,0:T(8,128)(2,1)S(1)}, u32[]{:S(2)}, u32[]{:S(2)}) collective-permute-start(bf16[111,256]{1,0:T(8,128)(2,1)S(1)} %get-tuple-element.46), channel_id=1, source_target_pairs={{1,2},{3,0},{2,1},{0,3},{5,6},{7,4},{6,5},{4,7},{9,10},{11,8},{10,... | collective-permute-start | bytes 170504 | tf_op jit(solution)/shard_map/ppermute | solution.py:516
  33.8 3.7 %collective-permute-start.3 = (bf16[111,256]{1,0:T(8,128)(2,1)S(1)}, bf16[111,256]{1,0:T(8,128)(2,1)S(1)}, u32[]{:S(2)}, u32[]{:S(2)}) collective-permute-start(bf16[111,256]{1,0:T(8,128)(2,1)S(1)} %get-tuple-element.45), channel_id=1, source_target_pairs={{0,1},{2,3},{1,0},{3,2},{4,5},{6,7},{5,4},{7,6},{8,9},{10,11},{9,8... | collective-permute-start | bytes 170504 | tf_op jit(solution)/shard_map/ppermute | solution.py:513

commit v10 on v9

--- a/solution.py
+++ b/solution.py
@@ -176,10 +176,13 @@
             preferred_element_type=jnp.float32,
         )
 
-    count = end - begin if end - begin <= CHUNK else CHUNK // 2
+    parts = -(-(end - begin) // CHUNK)
+    while (end - begin) % parts:
+        parts += 1
+    count = (end - begin) // parts
     total[...] = summed(begin, count) if held is None else held + summed(begin, count)
 
-    @pl.loop(1, (end - begin) // count)
+    @pl.loop(1, parts)
     def _(step):
         total[...] += summed(begin + step * count, count)
 

time: 38.8 us -> 38.8 us (level)
  no operation moved by 1% of the time
where the time goes in v10:
time: 38.8 us; the launch traced here: 38.7 us
  blocking collectives  23.2 us (60%)
  Pallas kernels  8.37 us (22%)
  starting transfers between devices  6.01 us (15%)
  waiting for transfers between devices  0.74 us (2%)
    all_to_all x1, blocking collectives, on_device(): lax.all_to_all(packed, ('lon', 'lat'), split_axis=0, concat_axis=0, tiled...  23.2 us
    ppermute x1, starting transfers between devices, on_device(): east = lax.ppermute(first, 'lon', [(j, i) for i, j in ring])  3.43 us
    pallas_call x1, Pallas kernels, sides(): pl.pallas_call(sides_kernel, in_specs=[VMEM] * 3, out_specs=[VMEM] * len(...  2.15 us
    pallas_call x1, Pallas kernels, inner(): pl.pallas_call(inner_kernel, in_specs=[VMEM] * (1 + len(arrays)), out_spe...  2.14 us
    pallas_call x1, Pallas kernels, pack(): pl.pallas_call(pack_kernel, in_specs=[ANY] * len(arrays), out_specs=VMEM,...  1.46 us
    pallas_call x1, Pallas kernels, edges(): pl.pallas_call(edges_kernel, in_specs=[VMEM] * (1 + len(arrays)), out_spe...  1.39 us
    ppermute x1, starting transfers between devices, on_device(): west = lax.ppermute(last, 'lon', ring)  1.35 us
    pallas_call x1, Pallas kernels, outer(): pl.pallas_call(outer_kernel, in_specs=[VMEM] * len(arrays), out_specs=ANY...  1.22 us
  transfers between devices with their start and end apart: 4, of which 2 were waited for; matrix products, arithmetic and copies ran while one was open for 0% of the time, Pallas kernels for 9%

profile of v10, /device:TPU:0, one launch (start us, length us, event | category | flops | bytes accessed | tf_op | source)
XLA Modules:
  0.0 38.7 jit_solution(12461824801057641346)
XLA Ops:
  0.0 0.0 copy-start.4
  0.0 0.0 copy-start.5
  0.0 1.5 %shard_map.109 = bf16[32,17,4,128]{3,2,1,0:T(4,128)(2,1)S(1)} custom-call(s32[1,32]{1,0:T(1,128)} %count_hbm.1, bf16[31,32,256]{2,1,0:T(8,128)(2,1)} %bitcast.16, f32[32,2,256]{2,1,0:T(2,128)} %offset_hbm.1, s32[32,256]{1,0:T(8,128)} %cell_hbm.1, s32[32,256]{1,0:T(8,128)} %slot_hbm.1), custom_call_target="tpu_custom_call" | custom-call | tf_op jit(solution)/shard_map/pallas_call | solution.py:130
  1.5 23.2 %all_to_all.5.x_ref = bf16[32,17,4,128]{3,2,1,0:T(4,128)(2,1)S(1)} all-to-all(bf16[32,17,4,128]{3,2,1,0:T(4,128)(2,1)S(1)} %shard_map.109), channel_id=1, replica_groups=mesh['lon'=8,'lat'=4] {'lon','lat'}, dimensions={0} | all-to-all | bytes 1114112 | tf_op jit(solution)/shard_map/all_to_all | solution.py:500
  24.7 0.0 copy-done.4
  24.7 0.0 copy-done.5
  24.7 2.2 %shard_map.110 = (f32[128,256]{1,0:T(8,128)S(1)}, f32[384,128]{1,0:T(8,128)S(1)}, bf16[3,16,256]{2,1,0:T(8,128)(2,1)S(1)}, bf16[2,16,256]{2,1,0:T(8,128)(2,1)S(1)}) custom-call(bf16[32,17,4,128]{3,2,1,0:T(4,128)(2,1)S(1)} %all_to_all.5.x_ref, bf16[384,256]{1,0:T(8,128)(2,1)S(1)} %copy-done.4, f32[1,256]{1,0:T(1,128)S(1)} %bitcast.13), custom_call_target="tpu_custom_call" | custom-call | flops 1610612736 | bytes 4194304 | tf_op jit(solution)/shard_map/pallas_call | solution.py:252
  26.9 1.3 %collective-permute-start = (bf16[3,16,256]{2,1,0:T(8,128)(2,1)S(1)}, bf16[3,16,256]{2,1,0:T(8,128)(2,1)S(1)}, u32[]{:S(2)}, u32[]{:S(2)}) collective-permute-start(bf16[3,16,256]{2,1,0:T(8,128)(2,1)S(1)} %get-tuple-element.37), channel_id=1, source_target_pairs={{0,4},{4,8},{8,12},{12,16},{16,20},{20,24},{24,28},{28,0},{1,5},{5... | collective-permute-start | bytes 73736 | tf_op jit(solution)/shard_map/ppermute | solution.py:506
  28.2 3.4 %collective-permute-start.1 = (bf16[2,16,256]{2,1,0:T(8,128)(2,1)S(1)}, bf16[2,16,256]{2,1,0:T(8,128)(2,1)S(1)}, u32[]{:S(2)}, u32[]{:S(2)}) collective-permute-start(bf16[2,16,256]{2,1,0:T(8,128)(2,1)S(1)} %get-tuple-element.38), channel_id=1, source_target_pairs={{4,0},{8,4},{12,8},{16,12},{20,16},{24,20},{28,24},{0,28},{5,1},{9... | collective-permute-start | bytes 49160 | tf_op jit(solution)/shard_map/ppermute | solution.py:507
  31.7 0.0 copy-start
  31.7 0.0 copy-start.1
  31.7 0.0 copy-start.2
  31.7 0.0 copy-start.3
  31.7 1.4 %shard_map.111 = (f32[384,256]{1,0:T(8,128)S(1)}, f32[128,256]{1,0:T(8,128)S(1)}, bf16[5,32,256]{2,1,0:T(8,128)(2,1)S(1)}) custom-call(bf16[32,17,4,128]{3,2,1,0:T(4,128)(2,1)S(1)} %all_to_all.5.x_ref, bf16[384,256]{1,0:T(8,128)(2,1)S(1)} %copy-done.4, f32[1,256]{1,0:T(1,128)S(1)} %bitcast.14, f32[128,256]{1,0:T(8,128)S(1)} %get-tuple-element.33.sides_ref, ...), custom_call_target="tpu_custom_call" | custom-call | flops 1610612736 | bytes 4194304 | tf_op jit(solution)/shard_map/pallas_call | solution.py:269
  33.1 0.0 collective-permute-done.1.east_ref
  33.2 0.3 collective-permute-done.west_ref
  33.5 0.2 collective-permute-start.2
  33.8 1.0 %collective-permute-start.3 = (bf16[111,256]{1,0:T(8,128)(2,1)S(1)}, bf16[111,256]{1,0:T(8,128)(2,1)S(1)}, u32[]{:S(2)}, u32[]{:S(2)}) collective-permute-start(bf16[111,256]{1,0:T(8,128)(2,1)S(1)} %get-tuple-element.45), channel_id=1, source_target_pairs={{0,1},{2,3},{1,0},{3,2},{4,5},{6,7},{5,4},{7,6},{8,9},{10,11},{9,8... | collective-permute-start | bytes 170504 | tf_op jit(solution)/shard_map/ppermute | solution.py:516
  34.8 0.1 iota.10._.place_ref
  34.8 0.0 copy-done
  34.9 0.0 copy-done.1
  34.9 0.0 copy-done.2
  34.9 0.0 copy-done.3
  34.9 2.1 %shard_map.112 = (f32[3,24,256]{2,1,0:T(8,128)S(1)}, f32[3,32,256]{2,1,0:T(8,128)S(1)}, f32[2,24,256]{2,1,0:T(8,128)S(1)}, f32[2,24,256]{2,1,0:T(8,128)S(1)}, bf16[5,16,256]{2,1,0:T(8,128)(2,1)S(1)}) custom-call(bf16[32,17,4,128]{3,2,1,0:T(4,128)(2,1)S(1)} %all_to_all.5.x_ref, f32[384,256]{1,0:T(8,128)S(1)} %get-tuple-element.35.half_ref, ...), custom_call_target="tpu_custom_call" | custom-call | flops 1610612736 | bytes 4194304 | tf_op jit(solution)/shard_map/pallas_call | solution.py:381
  37.0 0.4 %collective-permute-done.2.other_ref = bf16[111,256]{1,0:T(8,128)(2,1)S(1)} collective-permute-done((bf16[111,256]{1,0:T(8,128)(2,1)S(1)}, bf16[111,256]{1,0:T(8,128)(2,1)S(1)}, u32[]{:S(2)}, u32[]{:S(2)}) %collective-permute-start.2) | collective-permute-done | bytes 56864 | tf_op jit(solution)/shard_map/ppermute | solution.py:519
  37.4 0.0 collective-permute-done.3.pair_ref
  37.4 1.2 %shard_map.113 = bf16[8,16,256]{2,1,0:T(8,128)(2,1)} custom-call(f32[3,256]{1,0:T(4,128)S(1)} %iota.10._.place_ref, f32[3,24,256]{2,1,0:T(8,128)S(1)} %get-tuple-element.39.own_even_ref, f32[3,32,256]{2,1,0:T(8,128)S(1)} %get-tuple-element.40.own_odd_ref, f32[2,24,256]{2,1,0:T(8,128)S(1)} %get-tuple-element.41.upper_ref, ...), custom_call_target="tpu_custom_call" | custom-call | tf_op jit(solution)/shard_map/pallas_call | solution.py:463
  (9 shorter events, 0.1 us)
Async XLA Ops:
  0.0 24.7 %copy-start.4 = (bf16[384,256]{1,0:T(8,128)(2,1)S(1)}, bf16[384,256]{1,0:T(8,128)(2,1)}, u32[]{:S(2)}) copy-start(bf16[384,256]{1,0:T(8,128)(2,1)} %embed_ref.1) | copy-start | bytes 589828
  0.0 24.7 %copy-start.5 = (f32[256]{0:T(256)S(1)}, f32[256]{0:T(256)}, u32[]{:S(2)}) copy-start(f32[256]{0:T(256)} %param.17) | copy-start | bytes 3076
  26.9 6.6 %collective-permute-start = (bf16[3,16,256]{2,1,0:T(8,128)(2,1)S(1)}, bf16[3,16,256]{2,1,0:T(8,128)(2,1)S(1)}, u32[]{:S(2)}, u32[]{:S(2)}) collective-permute-start(bf16[3,16,256]{2,1,0:T(8,128)(2,1)S(1)} %get-tuple-element.37), channel_id=1, source_target_pairs={{0,4},{4,8},{8,12},{12,16},{16,20},{20,24},{24,28},{28,0},{1,5},{5... | collective-permute-start | bytes 73736 | tf_op jit(solution)/shard_map/ppermute | solution.py:506
  28.2 4.9 %collective-permute-start.1 = (bf16[2,16,256]{2,1,0:T(8,128)(2,1)S(1)}, bf16[2,16,256]{2,1,0:T(8,128)(2,1)S(1)}, u32[]{:S(2)}, u32[]{:S(2)}) collective-permute-start(bf16[2,16,256]{2,1,0:T(8,128)(2,1)S(1)} %get-tuple-element.38), channel_id=1, source_target_pairs={{4,0},{8,4},{12,8},{16,12},{20,16},{24,20},{28,24},{0,28},{5,1},{9... | collective-permute-start | bytes 49160 | tf_op jit(solution)/shard_map/ppermute | solution.py:507
  31.7 3.2 %copy-start = (bf16[9,256,256]{2,1,0:T(8,128)(2,1)S(1)}, bf16[9,256,256]{2,1,0:T(8,128)(2,1)}, u32[]{:S(2)}) copy-start(bf16[9,256,256]{2,1,0:T(8,128)(2,1)} %param.18) | copy-start | bytes 3538948
  31.7 3.2 %copy-start.1 = (f32[9,256]{1,0:T(8,128)S(1)}, f32[9,256]{1,0:T(8,128)}, u32[]{:S(2)}) copy-start(f32[9,256]{1,0:T(8,128)} %depth_ref.3) | copy-start | bytes 27652
  31.7 3.2 %copy-start.2 = (f32[256]{0:T(256)S(1)}, f32[256]{0:T(256)}, u32[]{:S(2)}) copy-start(f32[256]{0:T(256)} %param.19) | copy-start | bytes 3076
  31.7 3.2 %copy-start.3 = (f32[256]{0:T(256)S(1)}, f32[256]{0:T(256)}, u32[]{:S(2)}) copy-start(f32[256]{0:T(256)} %param.21) | copy-start | bytes 3076
  33.5 3.9 %collective-permute-start.2 = (bf16[111,256]{1,0:T(8,128)(2,1)S(1)}, bf16[111,256]{1,0:T(8,128)(2,1)S(1)}, u32[]{:S(2)}, u32[]{:S(2)}) collective-permute-start(bf16[111,256]{1,0:T(8,128)(2,1)S(1)} %get-tuple-element.46), channel_id=1, source_target_pairs={{1,2},{3,0},{2,1},{0,3},{5,6},{7,4},{6,5},{4,7},{9,10},{11,8},{10,... | collective-permute-start | bytes 170504 | tf_op jit(solution)/shard_map/ppermute | solution.py:519
  33.8 3.7 %collective-permute-start.3 = (bf16[111,256]{1,0:T(8,128)(2,1)S(1)}, bf16[111,256]{1,0:T(8,128)(2,1)S(1)}, u32[]{:S(2)}, u32[]{:S(2)}) collective-permute-start(bf16[111,256]{1,0:T(8,128)(2,1)S(1)} %get-tuple-element.45), channel_id=1, source_target_pairs={{0,1},{2,3},{1,0},{3,2},{4,5},{6,7},{5,4},{7,6},{8,9},{10,11},{9,8... | collective-permute-start | bytes 170504 | tf_op jit(solution)/shard_map/ppermute | solution.py:516

commit v11 on v10

--- a/solution.py
+++ b/solution.py
@@ -20,7 +20,7 @@
 GROUP = 16
 TILE = 4
 CHUNK = 32
-EARLY = 22
+EARLY = 24
 SPAN = 24
 CELLS = TLAT * TLON
 MID = 12

time: 38.8 us -> 38.8 us (level)
  no operation moved by 1% of the time
where the time goes in v11:
time: 38.8 us; the launch traced here: 38.7 us
  blocking collectives  23.2 us (60%)
  Pallas kernels  8.37 us (22%)
  starting transfers between devices  6.01 us (15%)
  waiting for transfers between devices  0.73 us (2%)
    all_to_all x1, blocking collectives, on_device(): lax.all_to_all(packed, ('lon', 'lat'), split_axis=0, concat_axis=0, tiled...  23.2 us
    ppermute x1, starting transfers between devices, on_device(): east = lax.ppermute(first, 'lon', [(j, i) for i, j in ring])  3.43 us
    pallas_call x1, Pallas kernels, sides(): pl.pallas_call(sides_kernel, in_specs=[VMEM] * 3, out_specs=[VMEM] * len(...  2.15 us
    pallas_call x1, Pallas kernels, inner(): pl.pallas_call(inner_kernel, in_specs=[VMEM] * (1 + len(arrays)), out_spe...  2.04 us
    pallas_call x1, Pallas kernels, edges(): pl.pallas_call(edges_kernel, in_specs=[VMEM] * (1 + len(arrays)), out_spe...  1.49 us
    pallas_call x1, Pallas kernels, pack(): pl.pallas_call(pack_kernel, in_specs=[ANY] * len(arrays), out_specs=VMEM,...  1.46 us
    ppermute x1, starting transfers between devices, on_device(): west = lax.ppermute(last, 'lon', ring)  1.35 us
    pallas_call x1, Pallas kernels, outer(): pl.pallas_call(outer_kernel, in_specs=[VMEM] * len(arrays), out_specs=ANY...  1.22 us
  transfers between devices with their start and end apart: 4, of which 2 were waited for; matrix products, arithmetic and copies ran while one was open for 0% of the time, Pallas kernels for 9%

profile of v11, /device:TPU:0, one launch (start us, length us, event | category | flops | bytes accessed | tf_op | source)
XLA Modules:
  0.0 38.7 jit_solution(13656310366467122706)
XLA Ops:
  0.0 0.0 copy-start.4
  0.0 0.0 copy-start.5
  0.0 1.5 %shard_map.109 = bf16[32,17,4,128]{3,2,1,0:T(4,128)(2,1)S(1)} custom-call(s32[1,32]{1,0:T(1,128)} %count_hbm.1, bf16[31,32,256]{2,1,0:T(8,128)(2,1)} %bitcast.16, f32[32,2,256]{2,1,0:T(2,128)} %offset_hbm.1, s32[32,256]{1,0:T(8,128)} %cell_hbm.1, s32[32,256]{1,0:T(8,128)} %slot_hbm.1), custom_call_target="tpu_custom_call" | custom-call | tf_op jit(solution)/shard_map/pallas_call | solution.py:130
  1.5 23.2 %all_to_all.5.x_ref = bf16[32,17,4,128]{3,2,1,0:T(4,128)(2,1)S(1)} all-to-all(bf16[32,17,4,128]{3,2,1,0:T(4,128)(2,1)S(1)} %shard_map.109), channel_id=1, replica_groups=mesh['lon'=8,'lat'=4] {'lon','lat'}, dimensions={0} | all-to-all | bytes 1114112 | tf_op jit(solution)/shard_map/all_to_all | solution.py:500
  24.7 0.0 copy-done.4
  24.7 0.0 copy-done.5
  24.7 2.2 %shard_map.110 = (f32[128,256]{1,0:T(8,128)S(1)}, f32[384,128]{1,0:T(8,128)S(1)}, bf16[3,16,256]{2,1,0:T(8,128)(2,1)S(1)}, bf16[2,16,256]{2,1,0:T(8,128)(2,1)S(1)}) custom-call(bf16[32,17,4,128]{3,2,1,0:T(4,128)(2,1)S(1)} %all_to_all.5.x_ref, bf16[384,256]{1,0:T(8,128)(2,1)S(1)} %copy-done.4, f32[1,256]{1,0:T(1,128)S(1)} %bitcast.13), custom_call_target="tpu_custom_call" | custom-call | flops 1610612736 | bytes 4194304 | tf_op jit(solution)/shard_map/pallas_call | solution.py:252
  26.9 1.3 %collective-permute-start = (bf16[3,16,256]{2,1,0:T(8,128)(2,1)S(1)}, bf16[3,16,256]{2,1,0:T(8,128)(2,1)S(1)}, u32[]{:S(2)}, u32[]{:S(2)}) collective-permute-start(bf16[3,16,256]{2,1,0:T(8,128)(2,1)S(1)} %get-tuple-element.37), channel_id=1, source_target_pairs={{0,4},{4,8},{8,12},{12,16},{16,20},{20,24},{24,28},{28,0},{1,5},{5... | collective-permute-start | bytes 73736 | tf_op jit(solution)/shard_map/ppermute | solution.py:506
  28.2 3.4 %collective-permute-start.1 = (bf16[2,16,256]{2,1,0:T(8,128)(2,1)S(1)}, bf16[2,16,256]{2,1,0:T(8,128)(2,1)S(1)}, u32[]{:S(2)}, u32[]{:S(2)}) collective-permute-start(bf16[2,16,256]{2,1,0:T(8,128)(2,1)S(1)} %get-tuple-element.38), channel_id=1, source_target_pairs={{4,0},{8,4},{12,8},{16,12},{20,16},{24,20},{28,24},{0,28},{5,1},{9... | collective-permute-start | bytes 49160 | tf_op jit(solution)/shard_map/ppermute | solution.py:507
  31.7 0.0 copy-start
  31.7 0.0 copy-start.1
  31.7 0.0 copy-start.2
  31.7 0.0 copy-start.3
  31.7 1.5 %shard_map.111 = (f32[384,256]{1,0:T(8,128)S(1)}, f32[128,256]{1,0:T(8,128)S(1)}, bf16[5,32,256]{2,1,0:T(8,128)(2,1)S(1)}) custom-call(bf16[32,17,4,128]{3,2,1,0:T(4,128)(2,1)S(1)} %all_to_all.5.x_ref, bf16[384,256]{1,0:T(8,128)(2,1)S(1)} %copy-done.4, f32[1,256]{1,0:T(1,128)S(1)} %bitcast.14, f32[128,256]{1,0:T(8,128)S(1)} %get-tuple-element.33.sides_ref, ...), custom_call_target="tpu_custom_call" | custom-call | flops 1610612736 | bytes 4194304 | tf_op jit(solution)/shard_map/pallas_call | solution.py:269
  33.2 0.0 collective-permute-done.1.east_ref
  33.3 0.2 collective-permute-done.west_ref
  33.5 0.3 collective-permute-start.2
  33.9 0.9 %collective-permute-start.3 = (bf16[111,256]{1,0:T(8,128)(2,1)S(1)}, bf16[111,256]{1,0:T(8,128)(2,1)S(1)}, u32[]{:S(2)}, u32[]{:S(2)}) collective-permute-start(bf16[111,256]{1,0:T(8,128)(2,1)S(1)} %get-tuple-element.45), channel_id=1, source_target_pairs={{0,1},{2,3},{1,0},{3,2},{4,5},{6,7},{5,4},{7,6},{8,9},{10,11},{9,8... | collective-permute-start | bytes 170504 | tf_op jit(solution)/shard_map/ppermute | solution.py:516
  34.8 0.1 iota.10._.place_ref
  34.8 0.0 copy-done
  34.9 0.0 copy-done.1
  34.9 0.0 copy-done.2
  34.9 0.0 copy-done.3
  34.9 2.0 %shard_map.112 = (f32[3,24,256]{2,1,0:T(8,128)S(1)}, f32[3,32,256]{2,1,0:T(8,128)S(1)}, f32[2,24,256]{2,1,0:T(8,128)S(1)}, f32[2,24,256]{2,1,0:T(8,128)S(1)}, bf16[5,16,256]{2,1,0:T(8,128)(2,1)S(1)}) custom-call(bf16[32,17,4,128]{3,2,1,0:T(4,128)(2,1)S(1)} %all_to_all.5.x_ref, f32[384,256]{1,0:T(8,128)S(1)} %get-tuple-element.35.half_ref, ...), custom_call_target="tpu_custom_call" | custom-call | flops 1610612736 | bytes 4194304 | tf_op jit(solution)/shard_map/pallas_call | solution.py:381
  36.9 0.5 %collective-permute-done.2.other_ref = bf16[111,256]{1,0:T(8,128)(2,1)S(1)} collective-permute-done((bf16[111,256]{1,0:T(8,128)(2,1)S(1)}, bf16[111,256]{1,0:T(8,128)(2,1)S(1)}, u32[]{:S(2)}, u32[]{:S(2)}) %collective-permute-start.2) | collective-permute-done | bytes 56864 | tf_op jit(solution)/shard_map/ppermute | solution.py:519
  37.4 0.0 collective-permute-done.3.pair_ref
  37.4 1.2 %shard_map.113 = bf16[8,16,256]{2,1,0:T(8,128)(2,1)} custom-call(f32[3,256]{1,0:T(4,128)S(1)} %iota.10._.place_ref, f32[3,24,256]{2,1,0:T(8,128)S(1)} %get-tuple-element.39.own_even_ref, f32[3,32,256]{2,1,0:T(8,128)S(1)} %get-tuple-element.40.own_odd_ref, f32[2,24,256]{2,1,0:T(8,128)S(1)} %get-tuple-element.41.upper_ref, ...), custom_call_target="tpu_custom_call" | custom-call | tf_op jit(solution)/shard_map/pallas_call | solution.py:463
  (9 shorter events, 0.1 us)
Async XLA Ops:
  0.0 24.7 %copy-start.4 = (bf16[384,256]{1,0:T(8,128)(2,1)S(1)}, bf16[384,256]{1,0:T(8,128)(2,1)}, u32[]{:S(2)}) copy-start(bf16[384,256]{1,0:T(8,128)(2,1)} %embed_ref.1) | copy-start | bytes 589828
  0.0 24.7 %copy-start.5 = (f32[256]{0:T(256)S(1)}, f32[256]{0:T(256)}, u32[]{:S(2)}) copy-start(f32[256]{0:T(256)} %param.17) | copy-start | bytes 3076
  26.9 6.6 %collective-permute-start = (bf16[3,16,256]{2,1,0:T(8,128)(2,1)S(1)}, bf16[3,16,256]{2,1,0:T(8,128)(2,1)S(1)}, u32[]{:S(2)}, u32[]{:S(2)}) collective-permute-start(bf16[3,16,256]{2,1,0:T(8,128)(2,1)S(1)} %get-tuple-element.37), channel_id=1, source_target_pairs={{0,4},{4,8},{8,12},{12,16},{16,20},{20,24},{24,28},{28,0},{1,5},{5... | collective-permute-start | bytes 73736 | tf_op jit(solution)/shard_map/ppermute | solution.py:506
  28.2 5.0 %collective-permute-start.1 = (bf16[2,16,256]{2,1,0:T(8,128)(2,1)S(1)}, bf16[2,16,256]{2,1,0:T(8,128)(2,1)S(1)}, u32[]{:S(2)}, u32[]{:S(2)}) collective-permute-start(bf16[2,16,256]{2,1,0:T(8,128)(2,1)S(1)} %get-tuple-element.38), channel_id=1, source_target_pairs={{4,0},{8,4},{12,8},{16,12},{20,16},{24,20},{28,24},{0,28},{5,1},{9... | collective-permute-start | bytes 49160 | tf_op jit(solution)/shard_map/ppermute | solution.py:507
  31.7 3.2 %copy-start = (bf16[9,256,256]{2,1,0:T(8,128)(2,1)S(1)}, bf16[9,256,256]{2,1,0:T(8,128)(2,1)}, u32[]{:S(2)}) copy-start(bf16[9,256,256]{2,1,0:T(8,128)(2,1)} %param.18) | copy-start | bytes 3538948
  31.7 3.2 %copy-start.1 = (f32[9,256]{1,0:T(8,128)S(1)}, f32[9,256]{1,0:T(8,128)}, u32[]{:S(2)}) copy-start(f32[9,256]{1,0:T(8,128)} %depth_ref.3) | copy-start | bytes 27652
  31.7 3.2 %copy-start.2 = (f32[256]{0:T(256)S(1)}, f32[256]{0:T(256)}, u32[]{:S(2)}) copy-start(f32[256]{0:T(256)} %param.19) | copy-start | bytes 3076
  31.7 3.2 %copy-start.3 = (f32[256]{0:T(256)S(1)}, f32[256]{0:T(256)}, u32[]{:S(2)}) copy-start(f32[256]{0:T(256)} %param.21) | copy-start | bytes 3076
  33.5 3.9 %collective-permute-start.2 = (bf16[111,256]{1,0:T(8,128)(2,1)S(1)}, bf16[111,256]{1,0:T(8,128)(2,1)S(1)}, u32[]{:S(2)}, u32[]{:S(2)}) collective-permute-start(bf16[111,256]{1,0:T(8,128)(2,1)S(1)} %get-tuple-element.46), channel_id=1, source_target_pairs={{1,2},{3,0},{2,1},{0,3},{5,6},{7,4},{6,5},{4,7},{9,10},{11,8},{10,... | collective-permute-start | bytes 170504 | tf_op jit(solution)/shard_map/ppermute | solution.py:519
  33.9 3.6 %collective-permute-start.3 = (bf16[111,256]{1,0:T(8,128)(2,1)S(1)}, bf16[111,256]{1,0:T(8,128)(2,1)S(1)}, u32[]{:S(2)}, u32[]{:S(2)}) collective-permute-start(bf16[111,256]{1,0:T(8,128)(2,1)S(1)} %get-tuple-element.45), channel_id=1, source_target_pairs={{0,1},{2,3},{1,0},{3,2},{4,5},{6,7},{5,4},{7,6},{8,9},{10,11},{9,8... | collective-permute-start | bytes 170504 | tf_op jit(solution)/shard_map/ppermute | solution.py:516
